TPU v7x, 32 devices: a whole 2x2x4 slice. The times are simulated.
32 devices in a mesh: dp: 32 (over z, y, x, core).
Axes of the slice: x: 2, y: 2, z: 4, core: 2. Of those that a mesh axis runs over, the one named last changes fastest.
Arguments:
- arrival_descriptors: bfloat16 [2, 32, 128, 1024], P(None, 'dp'), may hold values from -6 to 6
- opening_sheet_amounts: bfloat16 [2, 32, 128, 1024], P(None, 'dp'), may hold values from -6 to 6
- series_spans: int32 [2, 32], P(None, 'dp'), may hold values from 32 to 128, as said below
- arrival_derivative: bfloat16 [2, 32, 128, 1024], P(None, 'dp'), may hold values from -6 to 6
- preceding_merge_ratios: bfloat16 [7, 1024], P(None, 'dp'), may hold values from 0 to 1
- normalizing_stretches: bfloat16 [3, 1024], P(None, 'dp'), may hold values from 0.5 to 1.5
- normalizing_translations: bfloat16 [3, 1024], P(None, 'dp'), may hold values from -3 to 3
- deletion_tying_ratios: bfloat16 [2, 1024], P(None, 'dp'), may hold values from 0.5 to 1.5
- immediate_extra_ratios: bfloat16 [1024], P('dp'), may hold values from -0.25 to 0.25
- dwindle_footing: bfloat16 [1024], P('dp'), may hold values from -8 to -1
- squashing_footings: bfloat16 [2, 1024], P(None, 'dp'), may hold values from -1 to 1
- reducing_transforms: bfloat16 [1024, 288], P('dp'), may hold values from -0.1875 to 0.1875
- enlarging_transforms: bfloat16 [288, 1024], P(None, 'dp'), may hold values from -0.75 to 0.75
- ingoing_affine_transforms: bfloat16 [3, 1024, 1024], P(None, None, 'dp'), may hold values from -0.1875 to 0.1875
- concluding_affine_transform: bfloat16 [1024, 1024], P(None, 'dp'), may hold values from -0.1875 to 0.1875
- perceptron_address_transform: bfloat16 [1024, 4096], P('dp'), may hold values from -0.1875 to 0.1875
- perceptron_amount_transform: bfloat16 [4096, 1024], P('dp'), may hold values from -0.09375 to 0.09375
Outputs:
- outputs: bfloat16 [2, 32, 128, 1024], P(None, 'dp')
- input_grad: bfloat16 [2, 32, 128, 1024], P(None, 'dp')
- first_value_grad: bfloat16 [2, 32, 128, 1024], P(None, 'dp')
- mix_coef_grad: float32 [7, 1024], P(None, 'dp')
- norm_gain_grad: float32 [3, 1024], P(None, 'dp')
- norm_bias_grad: float32 [3, 1024], P(None, 'dp')
- head_coef_grad: float32 [2, 1024], P(None, 'dp')
- bonus_coef_grad: float32 [1024], P('dp')
- decay_base_grad: float32 [1024], P('dp')
- gate_base_grad: float32 [2, 1024], P(None, 'dp')
- lora_in_grad: float32 [1024, 288], P('dp')
- lora_out_grad: float32 [288, 1024], P(None, 'dp')
- proj_in_grad: float32 [3, 1024, 1024], P(None, None, 'dp')
- proj_out_grad: float32 [1024, 1024], P(None, 'dp')
- ffn_key_grad: float32 [1024, 4096], P('dp')
- ffn_value_grad: float32 [4096, 1024], P('dp')
Inputs may be any that keep to these rules, and one draw needn't show every extreme that they name: `series_spans`: valid slots of each sequence, counted from its first slot; in each micro-batch some sequence has all 128 slots valid.
All inputs are finite; a program needn't handle non-finite values.
Results may differ from a plain program's by a relative error of at most 0.012.
Values may be sent and summed in bfloat16 or wider, within the bound.
No kernel may reach another device: no remote copies, remote signals or barrier semaphores. Data moves between devices by JAX's collectives and lax.ppermute only.
A program may use at most 256 MiB of HBM per device.

v0:
```python
import math

import jax
import jax.numpy as jnp
from jax import lax
from jax.sharding import PartitionSpec as P

HEAD_SIZE = 64
DECAY_RANK = 64
RATE_RANK = 64
VALUE_RANK = 32
GATE_RANK = 128
SPAN = 64


HIGHEST = lax.Precision.HIGHEST
lowrank_inputs = (1, 4, 3, 5)


def lowrank_slices():
    return (
        0,
        DECAY_RANK,
        DECAY_RANK + RATE_RANK,
        DECAY_RANK + RATE_RANK + VALUE_RANK,
        DECAY_RANK + RATE_RANK + VALUE_RANK + GATE_RANK,
    )


def layer_norm(values, weight, offset):
    average = jnp.mean(values, -1, keepdims=True)
    centered = values - average
    spread = jnp.mean(centered * centered, -1, keepdims=True)
    return centered * lax.rsqrt(spread + 1e-05) * weight + offset


def shift_prev(values):
    return jnp.concatenate([jnp.zeros_like(values[:, :1]), values[:, :-1]], axis=1)


def product_result(left, right):
    return lax.dot_general(
        left, right, (((left.ndim - 1,), (0,)), ((), ())), preferred_element_type=jnp.float32
    )


def product_backward(grad_rows, right):
    return lax.dot_general(
        grad_rows,
        right,
        (((grad_rows.ndim - 1,), (1,)), ((), ())),
        preferred_element_type=jnp.float32,
    )


def weight_gradient(left, grad_rows):
    return lax.dot_general(
        left, grad_rows, (((0, 1), (0, 1)), ((), ())), preferred_element_type=jnp.float32
    )


def divide_subspaces(manyfold_lattice):
    return manyfold_lattice.reshape(
        manyfold_lattice.shape[:-1] + (manyfold_lattice.shape[-1] // HEAD_SIZE, HEAD_SIZE)
    )


def recur_blocks(acceptance_columns, log_decay, key_rows, value_rows, remove, insert):
    seq_count, length, head_count, head_size = acceptance_columns.shape
    width = min(SPAN, length)
    blocks = length // width

    def arrange(manyfold_lattice):
        return manyfold_lattice.reshape(seq_count, blocks, width, head_count, head_size).transpose(
            1, 0, 3, 2, 4
        )

    places = jnp.arange(width)
    inclusive = places[:, None] >= places[None, :]
    strict = places[:, None] > places[None, :]
    summing = inclusive.astype(jnp.float32)
    identity_mat = jnp.eye(width, dtype=jnp.float32)

    def paired(left, right, keep):
        return jnp.where(keep, jnp.einsum("bhtn,bhsn->bhts", left, right, precision=HIGHEST), 0.0)

    def block_step(memory, batch_item):
        r_blk, d_blk, k_blk, v_blk, a_blk, b_blk = batch_item
        cumul = jnp.einsum("ts,bhsn->bhtn", summing, d_blk, precision=HIGHEST)
        growth = jnp.exp(cumul)
        before = jnp.exp(cumul - d_blk)
        shrink = jnp.exp(-cumul)
        ending = growth[:, :, -1:, :]
        a_scaled = a_blk * before
        r_scaled = r_blk * growth
        b_scaled = b_blk * shrink
        k_scaled = k_blk * shrink
        right_side = jnp.einsum(
            "bhtk,bhkv->bhtv", a_scaled, memory, precision=HIGHEST
        ) + jnp.einsum(
            "bhts,bhsv->bhtv", paired(a_scaled, k_scaled, strict), v_blk, precision=HIGHEST
        )
        removed = jax.scipy.linalg.solve_triangular(
            identity_mat - paired(a_scaled, b_scaled, strict),
            right_side,
            lower=True,
            unit_diagonal=True,
        )
        emitted = jnp.einsum("bhtk,bhkv->bhtv", r_scaled, memory, precision=HIGHEST)
        emitted = emitted + jnp.einsum(
            "bhts,bhsv->bhtv", paired(r_scaled, b_scaled, inclusive), removed, precision=HIGHEST
        )
        emitted = emitted + jnp.einsum(
            "bhts,bhsv->bhtv", paired(r_scaled, k_scaled, inclusive), v_blk, precision=HIGHEST
        )
        memory = jnp.swapaxes(ending, 2, 3) * memory
        memory = memory + jnp.einsum(
            "bhsk,bhsv->bhkv", b_scaled * ending, removed, precision=HIGHEST
        )
        memory = memory + jnp.einsum("bhsk,bhsv->bhkv", k_scaled * ending, v_blk, precision=HIGHEST)
        return (memory, emitted)

    initial = jnp.zeros((seq_count, head_count, head_size, head_size), jnp.float32)
    sliced = tuple(
        (
            arrange(manyfold_lattice)
            for manyfold_lattice in (
                acceptance_columns,
                log_decay,
                key_rows,
                value_rows,
                remove,
                insert,
            )
        )
    )
    unused_item, emitted = lax.scan(block_step, initial, sliced)
    return emitted.transpose(1, 0, 3, 2, 4).reshape(seq_count, length, head_count, head_size)


def repeating_focus_engine(
    acceptance_columns,
    address_columns,
    payoff_columns,
    dwindle_ratio,
    adaptation_tempo,
    payoff_carryover_merge,
    squashing_ratio,
    starting_payoff_columns,
    deletion_tying_ratios,
    immediate_extra_ratios,
    dwindle_footing,
    squashing_footings,
    subgroup_multiplicand,
    subgroup_summand,
):
    log_decay = -jnp.exp(-jax.nn.softplus(-(dwindle_footing + dwindle_ratio)) - 0.5)
    adaptation_sigmoid = jax.nn.sigmoid(squashing_footings[0] + adaptation_tempo)
    amount_sigmoid = jax.nn.sigmoid(squashing_footings[1] + payoff_carryover_merge)
    value_mix = payoff_columns + (starting_payoff_columns - payoff_columns) * amount_sigmoid
    key_mod = address_columns * (1.0 + (adaptation_sigmoid - 1.0) * deletion_tying_ratios[1])
    key_unit = divide_subspaces(address_columns * deletion_tying_ratios[0])
    key_unit = key_unit * lax.rsqrt(jnp.sum(key_unit * key_unit, -1, keepdims=True) + 1e-06)
    reception_per_subspace = divide_subspaces(acceptance_columns)
    lookup_per_subspace = divide_subspaces(key_mod)
    content_per_subspace = divide_subspaces(value_mix)
    mixed = recur_blocks(
        reception_per_subspace,
        divide_subspaces(log_decay),
        lookup_per_subspace,
        content_per_subspace,
        -key_unit,
        key_unit * divide_subspaces(adaptation_sigmoid),
    )
    average = jnp.mean(mixed, -1, keepdims=True)
    centered = mixed - average
    spread = jnp.mean(centered * centered, -1, keepdims=True)
    standardized_features = (centered * lax.rsqrt(spread + 4.0)).reshape(
        acceptance_columns.shape
    ) * subgroup_multiplicand + subgroup_summand
    present_reward_share = (
        jnp.sum(
            reception_per_subspace * lookup_per_subspace * divide_subspaces(immediate_extra_ratios),
            -1,
            keepdims=True,
        )
        * content_per_subspace
    )
    return (
        standardized_features + present_reward_share.reshape(acceptance_columns.shape)
    ) * squashing_ratio


def front(x_values, mix_six, weight, offset):
    standardized_features = layer_norm(x_values, weight, offset)
    change = shift_prev(standardized_features) - standardized_features
    return tuple(
        (standardized_features + change * mix_six[index_position] for index_position in range(6))
    )


def channel_front(values, mix_row, weight, offset):
    standardized_features = layer_norm(values, weight, offset)
    return (
        standardized_features
        + (shift_prev(standardized_features) - standardized_features) * mix_row
    )


def lowrank_activation(
    decay_preactivation, rate_preactivation, value_preactivation, gate_preactivation
):
    return (
        jnp.tanh(decay_preactivation),
        rate_preactivation,
        value_preactivation,
        jax.nn.sigmoid(gate_preactivation),
    )


def squared(pre_act):
    return jnp.square(jax.nn.relu(pre_act))


def run_forward(learnable_package, x_float, first_value_wide, filled_cell_selector):
    (
        preceding_merge_ratios,
        normalizing_stretches,
        normalizing_translations,
        deletion_tying_ratios,
        immediate_extra_ratios,
        dwindle_footing,
        squashing_footings,
        reducing_transforms,
        enlarging_transforms,
        ingoing_affine_transforms,
        concluding_affine_transform,
        perceptron_address_transform,
        perceptron_amount_transform,
    ) = learnable_package
    small_number = tuple(
        (
            manyfold_lattice.astype(jnp.float32)
            for manyfold_lattice in (
                preceding_merge_ratios,
                normalizing_stretches,
                normalizing_translations,
                deletion_tying_ratios,
                immediate_extra_ratios,
                dwindle_footing,
                squashing_footings,
            )
        )
    )
    (
        lagged_coef_entry,
        scaling_entry,
        additive_entry,
        attention_coupling_entry,
        present_reward_entry,
        fading_entry,
        sigmoid_entry,
    ) = small_number
    shifted_hidden = tuple(
        (
            manyfold_lattice.astype(jnp.bfloat16)
            for manyfold_lattice in front(
                x_float, lagged_coef_entry[:6], scaling_entry[0], additive_entry[0]
            )
        )
    )
    acceptance_columns = product_result(shifted_hidden[0], ingoing_affine_transforms[0])
    address_columns = product_result(shifted_hidden[2], ingoing_affine_transforms[1])
    payoff_columns = product_result(shifted_hidden[3], ingoing_affine_transforms[2])
    slice_points = lowrank_slices()
    lowrank_before = tuple(
        (
            product_result(
                shifted_hidden[source_rows],
                reducing_transforms[
                    :, slice_points[index_position] : slice_points[index_position + 1]
                ],
            )
            for index_position, source_rows in enumerate(lowrank_inputs)
        )
    )
    lowrank_hidden = tuple(
        (
            manyfold_lattice.astype(jnp.bfloat16)
            for manyfold_lattice in lowrank_activation(*lowrank_before)
        )
    )
    lowrank_after = tuple(
        (
            product_result(
                lowrank_hidden[index_position],
                enlarging_transforms[
                    slice_points[index_position] : slice_points[index_position + 1]
                ],
            )
            for index_position in range(4)
        )
    )
    kernel_inputs = (
        (acceptance_columns, address_columns, payoff_columns) + lowrank_after + (first_value_wide,)
    )
    kernel_parameters = (
        attention_coupling_entry,
        present_reward_entry,
        fading_entry,
        sigmoid_entry,
        scaling_entry[1],
        additive_entry[1],
    )
    squashing_resized_merge = repeating_focus_engine(*kernel_inputs, *kernel_parameters).astype(
        jnp.bfloat16
    )
    mixed_in = x_float + product_result(squashing_resized_merge, concluding_affine_transform)
    chan_low = channel_front(
        mixed_in, lagged_coef_entry[6], scaling_entry[2], additive_entry[2]
    ).astype(jnp.bfloat16)
    chan_pre = product_result(chan_low, perceptron_address_transform)
    hidden = squared(chan_pre).astype(jnp.bfloat16)
    result = filled_cell_selector * (mixed_in + product_result(hidden, perceptron_amount_transform))
    saved = (
        small_number,
        shifted_hidden,
        lowrank_before,
        lowrank_hidden,
        kernel_inputs,
        kernel_parameters,
        squashing_resized_merge,
        mixed_in,
        chan_low,
        chan_pre,
        hidden,
    )
    return (result, saved)


def run_backward(learnable_package, x_float, filled_cell_selector, grad_out, saved):
    (
        reducing_transforms,
        enlarging_transforms,
        ingoing_affine_transforms,
        concluding_affine_transform,
        perceptron_address_transform,
        perceptron_amount_transform,
    ) = learnable_package[7:]
    (
        small_number,
        shifted_hidden,
        lowrank_before,
        lowrank_hidden,
        kernel_inputs,
        kernel_parameters,
        squashing_resized_merge,
        mixed_in,
        chan_low,
        chan_pre,
        hidden,
    ) = saved
    lagged_coef_entry, scaling_entry, additive_entry = (
        small_number[0],
        small_number[1],
        small_number[2],
    )
    grad_y = filled_cell_selector * grad_out
    grad_ffn = grad_y.astype(jnp.bfloat16)
    g_ffn_value = weight_gradient(hidden, grad_ffn)
    unused_item, pull_square = jax.vjp(squared, chan_pre)
    grad_pre = pull_square(product_backward(grad_ffn, perceptron_amount_transform))[0].astype(
        jnp.bfloat16
    )
    g_ffn_key = weight_gradient(chan_low, grad_pre)
    unused_item, pull_chan = jax.vjp(
        channel_front, mixed_in, lagged_coef_entry[6], scaling_entry[2], additive_entry[2]
    )
    grad_mixed, grad_mix_c, grad_gain_c, grad_bias_c = pull_chan(
        product_backward(grad_pre, perceptron_address_transform)
    )
    grad_mixed = grad_y + grad_mixed
    grad_att = grad_mixed.astype(jnp.bfloat16)
    g_proj_out = weight_gradient(squashing_resized_merge, grad_att)
    unused_item, pull_core = jax.vjp(repeating_focus_engine, *kernel_inputs, *kernel_parameters)
    kernel_gradients = pull_core(product_backward(grad_att, concluding_affine_transform))
    grad_recept = kernel_gradients[0].astype(jnp.bfloat16)
    grad_key = kernel_gradients[1].astype(jnp.bfloat16)
    value_gradient = kernel_gradients[2].astype(jnp.bfloat16)
    post_gradient = tuple(
        (manyfold_lattice.astype(jnp.bfloat16) for manyfold_lattice in kernel_gradients[3:7])
    )
    grad_first = kernel_gradients[7]
    (
        head_gradient,
        reward_cotangent,
        decay_gradient,
        gate_gradient,
        group_gain_gradient,
        group_bias_gradient,
    ) = kernel_gradients[8:]
    slice_points = lowrank_slices()
    gradient_rank_output = jnp.concatenate(
        [
            weight_gradient(lowrank_hidden[index_position], post_gradient[index_position])
            for index_position in range(4)
        ],
        axis=0,
    )
    unused_item, lowrank_pullback = jax.vjp(lowrank_activation, *lowrank_before)
    rank_gradient = lowrank_pullback(
        tuple(
            (
                product_backward(
                    post_gradient[index_position],
                    enlarging_transforms[
                        slice_points[index_position] : slice_points[index_position + 1]
                    ],
                )
                for index_position in range(4)
            )
        )
    )
    rank_gradient = tuple(
        (manyfold_lattice.astype(jnp.bfloat16) for manyfold_lattice in rank_gradient)
    )
    gradient_rank_input = jnp.concatenate(
        [
            weight_gradient(shifted_hidden[source_rows], rank_gradient[index_position])
            for index_position, source_rows in enumerate(lowrank_inputs)
        ],
        axis=1,
    )
    g_proj_in = jnp.stack(
        [
            weight_gradient(shifted_hidden[0], grad_recept),
            weight_gradient(shifted_hidden[2], grad_key),
            weight_gradient(shifted_hidden[3], value_gradient),
        ]
    )
    lowrank_backward = tuple(
        (
            product_backward(
                rank_gradient[index_position],
                reducing_transforms[
                    :, slice_points[index_position] : slice_points[index_position + 1]
                ],
            )
            for index_position in range(4)
        )
    )
    grad_mixes = (
        product_backward(grad_recept, ingoing_affine_transforms[0]),
        lowrank_backward[0],
        product_backward(grad_key, ingoing_affine_transforms[1]),
        product_backward(value_gradient, ingoing_affine_transforms[2]) + lowrank_backward[2],
        lowrank_backward[1],
        lowrank_backward[3],
    )
    unused_item, pull_front = jax.vjp(
        front, x_float, lagged_coef_entry[:6], scaling_entry[0], additive_entry[0]
    )
    grad_front, grad_mix_t, grad_gain_t, grad_bias_t = pull_front(grad_mixes)
    grad_input = grad_mixed + grad_front
    gradients = (
        jnp.concatenate([grad_mix_t, grad_mix_c[None]], axis=0),
        jnp.stack([grad_gain_t, group_gain_gradient, grad_gain_c]),
        jnp.stack([grad_bias_t, group_bias_gradient, grad_bias_c]),
        head_gradient,
        reward_cotangent,
        decay_gradient,
        gate_gradient,
        gradient_rank_input,
        gradient_rank_output,
        g_proj_in,
        g_proj_out,
        g_ffn_key,
        g_ffn_value,
    )
    return (grad_input, grad_first, gradients)


def on_device(
    arrival_descriptors,
    opening_sheet_amounts,
    series_spans,
    arrival_derivative,
    preceding_merge_ratios,
    normalizing_stretches,
    normalizing_translations,
    deletion_tying_ratios,
    immediate_extra_ratios,
    dwindle_footing,
    squashing_footings,
    reducing_transforms,
    enlarging_transforms,
    ingoing_affine_transforms,
    concluding_affine_transform,
    perceptron_address_transform,
    perceptron_amount_transform,
):

    def gather_all():
        mixer = (
            lax.all_gather(preceding_merge_ratios, "dp", axis=1, tiled=True),
            lax.all_gather(normalizing_stretches, "dp", axis=1, tiled=True),
            lax.all_gather(normalizing_translations, "dp", axis=1, tiled=True),
            lax.all_gather(deletion_tying_ratios, "dp", axis=1, tiled=True),
            lax.all_gather(immediate_extra_ratios, "dp", axis=0, tiled=True),
            lax.all_gather(dwindle_footing, "dp", axis=0, tiled=True),
            lax.all_gather(squashing_footings, "dp", axis=1, tiled=True),
            lax.all_gather(reducing_transforms, "dp", axis=0, tiled=True),
            lax.all_gather(enlarging_transforms, "dp", axis=1, tiled=True),
            lax.all_gather(ingoing_affine_transforms, "dp", axis=2, tiled=True),
            lax.all_gather(concluding_affine_transform, "dp", axis=1, tiled=True),
        )
        channel = (
            lax.all_gather(perceptron_address_transform, "dp", axis=0, tiled=True),
            lax.all_gather(perceptron_amount_transform, "dp", axis=0, tiled=True),
        )
        return tuple(mixer) + tuple(channel)

    micro_count = arrival_descriptors.shape[0]
    positions = jnp.arange(arrival_descriptors.shape[2], dtype=jnp.int32)
    totals = ()
    result_list = []
    input_list = []
    first_list = []
    for index_position in range(micro_count):
        x_float = arrival_descriptors[index_position].astype(jnp.float32)
        first_value_wide = opening_sheet_amounts[index_position].astype(jnp.float32)
        filled_cell_selector = (positions[None, :] < series_spans[index_position][:, None]).astype(
            jnp.float32
        )[:, :, None]
        learnable_package = gather_all()
        result, saved = run_forward(
            learnable_package, x_float, first_value_wide, filled_cell_selector
        )
        learnable_package = gather_all()
        unused_item, saved = run_forward(
            learnable_package, x_float, first_value_wide, filled_cell_selector
        )
        grad_input, grad_first, gradients = run_backward(
            learnable_package,
            x_float,
            filled_cell_selector,
            arrival_derivative[index_position].astype(jnp.float32),
            saved,
        )
        if index_position == 0:
            totals = gradients
        else:
            totals = tuple((running + fresh for running, fresh in zip(totals, gradients)))
        result_list.append(result.astype(jnp.bfloat16))
        input_list.append(grad_input.astype(jnp.bfloat16))
        first_list.append(grad_first.astype(jnp.bfloat16))
    mixer = (
        lax.psum_scatter(totals[0], "dp", scatter_dimension=1, tiled=True),
        lax.psum_scatter(totals[1], "dp", scatter_dimension=1, tiled=True),
        lax.psum_scatter(totals[2], "dp", scatter_dimension=1, tiled=True),
        lax.psum_scatter(totals[3], "dp", scatter_dimension=1, tiled=True),
        lax.psum_scatter(totals[4], "dp", scatter_dimension=0, tiled=True),
        lax.psum_scatter(totals[5], "dp", scatter_dimension=0, tiled=True),
        lax.psum_scatter(totals[6], "dp", scatter_dimension=1, tiled=True),
        lax.psum_scatter(totals[7], "dp", scatter_dimension=0, tiled=True),
        lax.psum_scatter(totals[8], "dp", scatter_dimension=1, tiled=True),
        lax.psum_scatter(totals[9], "dp", scatter_dimension=2, tiled=True),
        lax.psum_scatter(totals[10], "dp", scatter_dimension=1, tiled=True),
    )
    channel = (
        lax.psum_scatter(totals[11], "dp", scatter_dimension=0, tiled=True),
        lax.psum_scatter(totals[12], "dp", scatter_dimension=0, tiled=True),
    )
    totals = tuple(mixer) + tuple(channel)
    grad_scale = 1.0 / math.sqrt(
        micro_count
        * arrival_descriptors.shape[1]
        * lax.axis_size("dp")
        * arrival_descriptors.shape[2]
    )
    return (jnp.stack(result_list), jnp.stack(input_list), jnp.stack(first_list)) + tuple(
        (manyfold_lattice * grad_scale for manyfold_lattice in totals)
    )


def solution(mesh):
    in_specs = (
        P(None, "dp", None, None),
        P(None, "dp", None, None),
        P(None, "dp"),
        P(None, "dp", None, None),
        P(None, "dp"),
        P(None, "dp"),
        P(None, "dp"),
        P(None, "dp"),
        P("dp"),
        P("dp"),
        P(None, "dp"),
        P("dp", None),
        P(None, "dp"),
        P(None, None, "dp"),
        P(None, "dp"),
        P("dp", None),
        P("dp", None),
    )
    out_specs = (
        P(None, "dp", None, None),
        P(None, "dp", None, None),
        P(None, "dp", None, None),
        P(None, "dp"),
        P(None, "dp"),
        P(None, "dp"),
        P(None, "dp"),
        P("dp"),
        P("dp"),
        P(None, "dp"),
        P("dp", None),
        P(None, "dp"),
        P(None, None, "dp"),
        P(None, "dp"),
        P("dp", None),
        P("dp", None),
    )
    return jax.shard_map(
        on_device, mesh=mesh, in_specs=in_specs, out_specs=out_specs, check_vma=False
    )
```

profile of v0, /device:TPU:0, one launch (start us, length us, event | category | flops | bytes accessed | tf_op | source)
XLA Modules:
  0.0 3720.0 jit_solution(5685284066870977467)
XLA Ops:
  442.4 223.3 %while.202 = (s32[]{:T(128)}, f32[1,16,64,64]{3,2,1,0:T(8,128)}, f32[2,1,16,64,64]{3,4,2,1,0:T(8,128)}, f32[2,1,16,64,64]{4,3,2,1,0:T(8,128)}, f32[2,1,16,64,64]...) while((s32[]{:T(128)}, f32[1,16,64,64]{3,2,1,0:T(8,128)}, ...), condition=%wide.region_23.26_spmd.clone.clone, body=%wide.region_22.25_spmd.clone.clone.sunk | while | flops 656109632 | bytes 61261140 | solution.py:137
  459.3 80.0 %custom-call.34 = f32[16,1,64,64]{2,3,1,0:T(8,128)} custom-call(f32[16,1,64,64]{3,2,1,0:T(8,128)} %add_bitcast_fusion.6), custom_call_target="InvertDiagBlocksLowerTriangular" | custom-call | tf_op jit(solution)/shard_map/jvp()/while/body/eval_jaxpr/jit(_solve_triangular)/vmap()/triangular_solve/custom-call.1 | solution.py:103
  571.1 80.0 %custom-call.34 = f32[16,1,64,64]{2,3,1,0:T(8,128)} custom-call(f32[16,1,64,64]{3,2,1,0:T(8,128)} %add_bitcast_fusion.6), custom_call_target="InvertDiagBlocksLowerTriangular" | custom-call | tf_op jit(solution)/shard_map/jvp()/while/body/eval_jaxpr/jit(_solve_triangular)/vmap()/triangular_solve/custom-call.1 | solution.py:103
  688.2 223.4 %while.204 = (s32[]{:T(128)}, f32[1,16,64,64]{3,2,1,0:T(8,128)}, f32[2,1,16,64,64]{3,4,2,1,0:T(8,128)}, f32[2,1,16,64,64]{4,3,2,1,0:T(8,128)}, f32[2,1,16,64,64]...) while((s32[]{:T(128)}, f32[1,16,64,64]{3,2,1,0:T(8,128)}, ...), condition=%wide.region_40.44_spmd.clone.clone, body=%wide.region_39.43_spmd.clone.clone.sunk | while | flops 656109632 | bytes 61261140 | solution.py:137
  705.2 80.0 %custom-call.36 = f32[16,1,64,64]{2,3,1,0:T(8,128)} custom-call(f32[16,1,64,64]{3,2,1,0:T(8,128)} %add_bitcast_fusion.7), custom_call_target="InvertDiagBlocksLowerTriangular" | custom-call | tf_op jit(solution)/shard_map/jvp()/while/body/eval_jaxpr/jit(_solve_triangular)/vmap()/triangular_solve/custom-call.1 | solution.py:103
  817.0 80.0 %custom-call.36 = f32[16,1,64,64]{2,3,1,0:T(8,128)} custom-call(f32[16,1,64,64]{3,2,1,0:T(8,128)} %add_bitcast_fusion.7), custom_call_target="InvertDiagBlocksLowerTriangular" | custom-call | tf_op jit(solution)/shard_map/jvp()/while/body/eval_jaxpr/jit(_solve_triangular)/vmap()/triangular_solve/custom-call.1 | solution.py:103
  912.8 206.9 %while.201 = (s32[]{:T(128)}, f32[1,16,64,64]{3,2,1,0:T(8,128)}, f32[2,1,16,64,64]{4,3,2,1,0:T(8,128)}, f32[2,1,16,64,64]{4,3,2,1,0:T(8,128)}, f32[2,1,16,64,64]...) while((s32[]{:T(128)}, f32[1,16,64,64]{3,2,1,0:T(8,128)}, ...), condition=%wide.region_14.16_spmd.clone.clone, body=%wide.region_13.15_spmd.clone.clone.sunk | while | flops 655921216 | bytes 25549644 | solution.py:137
  925.7 80.0 %custom-call.33 = f32[16,1,64,64]{2,3,1,0:T(8,128)} custom-call(f32[16,1,64,64]{3,2,1,0:T(8,128)} %fusion.1284), custom_call_target="InvertDiagBlocksLowerTriangular" | custom-call | tf_op jit(solution)/shard_map/while/body/eval_jaxpr/jit(_solve_triangular)/vmap()/triangular_solve/custom-call.1 | solution.py:103
  1029.4 80.0 %custom-call.33 = f32[16,1,64,64]{2,3,1,0:T(8,128)} custom-call(f32[16,1,64,64]{3,2,1,0:T(8,128)} %fusion.1284), custom_call_target="InvertDiagBlocksLowerTriangular" | custom-call | tf_op jit(solution)/shard_map/while/body/eval_jaxpr/jit(_solve_triangular)/vmap()/triangular_solve/custom-call.1 | solution.py:103
  1130.2 204.0 %while.200 = (s32[]{:T(128)}, f32[1,16,64,64]{3,2,1,0:T(8,128)}, f32[2,1,16,64,64]{4,3,2,1,0:T(8,128)}, f32[2,1,16,64,64]{4,3,2,1,0:T(8,128)}, f32[2,1,16,64,64]...) while((s32[]{:T(128)}, f32[1,16,64,64]{3,2,1,0:T(8,128)}, ...), condition=%wide.region_4.6_spmd.clone.clone, body=%wide.region_3.5_spmd.clone.clone.sunk | while | flops 655921216 | bytes 22403832 | solution.py:137
  1432.9 238.1 %while.203 = (s32[]{:T(128)}, f32[1,16,64,64]{2,3,1,0:T(8,128)S(1)}, f32[2,1,16,64,64]{4,3,2,1,0:T(8,128)}, f32[2,1,16,64,64]{4,3,2,1,0:T(8,128)}, f32[2,1,16,64...) while((s32[]{:T(128)}, f32[1,16,64,64]{2,3,1,0:T(8,128)S(1)}, ...), condition=%wide.region_32.36_spmd.clone.clone, body=%wide.region_28.0_spmd.clone.clone.sunk | while | flops 1312377856 | bytes 125472696 | solution.py:137
  1446.4 80.0 %custom-call.35 = f32[16,1,64,64]{2,3,1,0:T(8,128)} custom-call(f32[16,1,64,64]{3,2,1,0:T(8,128)} %fusion.1355), custom_call_target="InvertDiagBlocksLowerTriangular" | custom-call | tf_op jit(solution)/shard_map/transpose(jvp())/while/body/eval_jaxpr/jit(_solve_triangular)/vmap()/triangular_solve/custom-call.0 | solution.py:103
  1565.2 80.0 %custom-call.35 = f32[16,1,64,64]{2,3,1,0:T(8,128)} custom-call(f32[16,1,64,64]{3,2,1,0:T(8,128)} %fusion.1355), custom_call_target="InvertDiagBlocksLowerTriangular" | custom-call | tf_op jit(solution)/shard_map/transpose(jvp())/while/body/eval_jaxpr/jit(_solve_triangular)/vmap()/triangular_solve/custom-call.0 | solution.py:103
  1689.7 238.0 %while.205 = (s32[]{:T(128)}, f32[1,16,64,64]{2,3,1,0:T(8,128)S(1)}, f32[2,1,16,64,64]{4,3,2,1,0:T(8,128)}, f32[2,1,16,64,64]{4,3,2,1,0:T(8,128)}, f32[2,1,16,64...) while((s32[]{:T(128)}, f32[1,16,64,64]{2,3,1,0:T(8,128)S(1)}, ...), condition=%wide.region_49.53_spmd.clone.clone, body=%wide.region_45.52_spmd.clone.clone.sunk | while | flops 1312377856 | bytes 125472696 | solution.py:137
  2188.7 131.0 %reduce-scatter.39.cloned.1.call-done = f32[32,2]{1,0:T(8,128)} async-done(((f32[1024,2]{1,0:T(8,128)}), f32[32,2]{1,0:T(8,128)}) %reduce-scatter.39.cloned.1.call-update) | async-done | bytes 272
  2321.6 129.9 %reduce-scatter.33.cloned.1.call-done = f32[32,3]{1,0:T(8,128)} async-done(((f32[1024,3]{1,0:T(8,128)}), f32[32,3]{1,0:T(8,128)}) %reduce-scatter.33.cloned.1.call-update) | async-done | bytes 400
  2452.3 131.1 %reduce-scatter.35.cloned.1.call-done = f32[32,3]{1,0:T(8,128)} async-done(((f32[1024,3]{1,0:T(8,128)}), f32[32,3]{1,0:T(8,128)}) %reduce-scatter.35.cloned.1.call-update) | async-done | bytes 400
  2585.4 129.8 %reduce-scatter.31.cloned.1.call-done = f32[32,7]{1,0:T(8,128)} async-done(((f32[1024,7]{1,0:T(8,128)}), f32[32,7]{1,0:T(8,128)}) %reduce-scatter.31.cloned.1.call-update) | async-done | bytes 912
  2716.6 97.5 %reduce-scatter.41.cloned.1.call-done = f32[32,288]{1,0:T(8,128)} async-done(((f32[1024,288]{1,0:T(8,128)}), f32[32,288]{1,0:T(8,128)}) %reduce-scatter.41.cloned.1.call-update) | async-done | bytes 36880
  2815.8 100.5 %reduce-scatter.43.cloned.1.call-done = f32[32,288]{1,0:T(8,128)} async-done(((f32[1024,288]{1,0:T(8,128)}), f32[32,288]{1,0:T(8,128)}) %reduce-scatter.43.cloned.1.call-update) | async-done | bytes 36880
  2918.0 282.6 %all-reduce.39.cloned.1.call-done = f32[3,1024,1024]{1,0,2:T(4,128)} async-done(((f32[3,1024,1024]{1,0,2:T(4,128)}), f32[3,1024,1024]{1,0,2:T(4,128)}) %all-reduce.39.cloned.1.call-update) | async-done | bytes 12582928
  3202.7 140.9 %reduce-scatter.25.cloned.1.call-done = f32[1024,32]{0,1:T(8,128)} async-done(((f32[1024,1024]{0,1:T(8,128)}), f32[1024,32]{0,1:T(8,128)}) %reduce-scatter.25.cloned.1.call-update) | async-done | bytes 131088 | tf_op jit(solution)/shard_map/reduce_scatter | solution.py:568
  3345.2 179.4 %reduce-scatter.27.cloned.1.call-done = f32[32,4096]{1,0:T(8,128)} async-done(((f32[1024,4096]{1,0:T(8,128)}), f32[32,4096]{1,0:T(8,128)}) %reduce-scatter.27.cloned.1.call-update) | async-done | bytes 524304 | tf_op jit(solution)/shard_map/reduce_scatter | solution.py:571
  3526.4 185.0 %reduce-scatter.29.cloned.1.call-done = f32[128,1024]{1,0:T(8,128)} async-done(((f32[4096,1024]{1,0:T(8,128)}), f32[128,1024]{1,0:T(8,128)}) %reduce-scatter.29.cloned.1.call-update) | async-done | bytes 524304 | tf_op jit(solution)/shard_map/reduce_scatter | solution.py:572
  (1986 shorter events, 1547.5 us)
Async XLA Ops:
  7.2 169.6 %copy-start.455 = (bf16[3,32]{1,0:T(4,128)(2,1)S(1)}, bf16[3,32]{1,0:T(4,128)(2,1)}, u32[]{:S(2)}) copy-start(bf16[3,32]{1,0:T(4,128)(2,1)} %param.39) | copy-start | bytes 580
  7.2 207.2 %copy-start.67 = (bf16[2,1,128,1024]{3,2,1,0:T(8,128)(2,1)S(1)}, bf16[2,1,128,1024]{3,2,1,0:T(8,128)(2,1)}, u32[]{:S(2)}) copy-start(bf16[2,1,128,1024]{3,2,1,0:T(8,128)(2,1)} %param.34) | copy-start | bytes 1572868
  7.2 208.3 %copy-start.410 = (bf16[32,288]{1,0:T(8,128)(2,1)S(1)}, bf16[32,288]{1,0:T(8,128)(2,1)}, u32[]{:S(2)}) copy-start(bf16[32,288]{1,0:T(8,128)(2,1)} %param.45) | copy-start | bytes 55300
  7.2 372.8 %all-gather.10.cloned.1.call-start = ((), (), s32[]{:S(2)}) async-start(), calls=%async_computation.10 | async-start | bytes 6488064 | tf_op jit(solution)/shard_map/all_gather | solution.py:514
  8.0 1365.5 %all-gather.12.cloned.1.call-start = ((), (), s32[]{:S(2)}) async-start(), calls=%async_computation.11 | async-start | bytes 2162688 | tf_op jit(solution)/shard_map/all_gather | solution.py:515
  8.7 248.2 %copy-start.458 = (bf16[2,32]{1,0:T(2,128)(2,1)S(1)}, bf16[2,32]{1,0:T(2,128)(2,1)}, u32[]{:S(2)}) copy-start(bf16[2,32]{1,0:T(2,128)(2,1)} %param.44) | copy-start | bytes 388
  8.7 1370.6 %all-gather.14.cloned.1.call-start = ((), (), s32[]{:S(2)}) async-start(), calls=%async_computation.12 | async-start | bytes 8650752 | tf_op jit(solution)/shard_map/all_gather | solution.py:518
  9.5 1378.6 %all-gather.16.cloned.1.call-start = ((), (), s32[]{:S(2)}) async-start(), calls=%async_computation.13 | async-start | bytes 8650752 | tf_op jit(solution)/shard_map/all_gather | solution.py:519
  10.0 2177.8 %reduce-scatter.37.cloned.1.call-start = ((), (), s32[]{:S(2)}) async-start(), calls=%async_computation.20 | async-start | bytes 540672
  100.0 265.7 %copy-start.103 = (bf16[288,1024]{0,1:T(8,128)(2,1)}, bf16[288,1024]{0,1:T(8,128)(2,1)S(1)}, u32[]{:S(2)}) copy-start(bf16[288,1024]{0,1:T(8,128)(2,1)S(1)} %all_gather.31) | copy-start | bytes 1769476
  138.0 161.7 %copy-start.360 = (f32[1,1024]{1,0:T(1,128)}, f32[1,1024]{1,0:T(1,128)S(1)}, u32[]{:S(2)}) copy-start(f32[1,1024]{1,0:T(1,128)S(1)} %get-tuple-element.4337) | copy-start | bytes 12292
  138.0 161.7 %copy-start.365 = (f32[1,1024]{1,0:T(1,128)}, f32[1,1024]{1,0:T(1,128)S(1)}, u32[]{:S(2)}) copy-start(f32[1,1024]{1,0:T(1,128)S(1)} %get-tuple-element.4335) | copy-start | bytes 12292
  138.0 161.7 %copy-start.367 = (f32[1,1024]{1,0:T(1,128)}, f32[1,1024]{1,0:T(1,128)S(1)}, u32[]{:S(2)}) copy-start(f32[1,1024]{1,0:T(1,128)S(1)} %get-tuple-element.4338) | copy-start | bytes 12292
  138.0 161.7 %copy-start.369 = (f32[1,1024]{1,0:T(1,128)}, f32[1,1024]{1,0:T(1,128)S(1)}, u32[]{:S(2)}) copy-start(f32[1,1024]{1,0:T(1,128)S(1)} %get-tuple-element.4339) | copy-start | bytes 12292
  2057.5 262.1 %reduce-scatter.39.cloned.1.call-start = ((), (), s32[]{:S(2)}) async-start(), calls=%async_computation.21 | async-start | bytes 540672
  2058.8 392.7 %reduce-scatter.33.cloned.1.call-start = ((), (), s32[]{:S(2)}) async-start(), calls=%async_computation.18 | async-start | bytes 540672
  2061.1 522.3 %reduce-scatter.35.cloned.1.call-start = ((), (), s32[]{:S(2)}) async-start(), calls=%async_computation.19 | async-start | bytes 540672
  2062.3 652.9 %reduce-scatter.31.cloned.1.call-start = ((), (), s32[]{:S(2)}) async-start(), calls=%async_computation.17 | async-start | bytes 540672
  2063.6 750.5 %reduce-scatter.41.cloned.1.call-start = ((), (), s32[]{:S(2)}) async-start(), calls=%async_computation.22 | async-start | bytes 1622016
  2066.9 849.4 %reduce-scatter.43.cloned.1.call-start = ((), (), s32[]{:S(2)}) async-start(), calls=%async_computation.23 | async-start | bytes 1622016
  2073.3 1127.2 %all-reduce.39.cloned.1.call-start = ((), (), s32[]{:S(2)}) async-start(), calls=%async_computation.24 | async-start | bytes 33554432
  2104.5 1239.1 %reduce-scatter.25.cloned.1.call-start = ((), (), s32[]{:S(2)}) async-start(), calls=%async_computation.14 | async-start | bytes 4325376 | tf_op jit(solution)/shard_map/reduce_scatter | solution.py:568
  2109.0 1415.5 %reduce-scatter.27.cloned.1.call-start = ((), (), s32[]{:S(2)}) async-start(), calls=%async_computation.15 | async-start | bytes 17301504 | tf_op jit(solution)/shard_map/reduce_scatter | solution.py:571
  2120.9 1590.6 %reduce-scatter.29.cloned.1.call-start = ((), (), s32[]{:S(2)}) async-start(), calls=%async_computation.16 | async-start | bytes 17301504 | tf_op jit(solution)/shard_map/reduce_scatter | solution.py:572
  (576 other events, 3218.1 us)
Sparse Core Ops, SparseCore 0:
  11.0 76.7 all-gather.9
  90.6 55.2 all-gather.11
  148.8 78.8 all-gather.13
  230.4 75.7 all-gather.15
  2057.7 130.1 reduce-scatter.36
  2190.1 129.5 reduce-scatter.38
  2321.9 129.5 reduce-scatter.32
  2453.8 129.5 reduce-scatter.34
  2585.7 129.5 reduce-scatter.30
  2721.1 92.9 reduce-scatter.40
  2820.2 96.0 reduce-scatter.42
  2923.2 277.2 all-reduce.38
  3202.9 140.6 reduce-scatter.24
  3345.9 178.6 reduce-scatter.26
  3526.8 184.6 reduce-scatter.28
where the time goes:
time: 3730 us; the launch traced here: 3720 us
  waiting for transfers between devices  1510 us (40%)
  other arithmetic  1070 us (29%)
  matrix products  407 us (11%)
  blocking collectives  353 us (9%)
  local copies, waits for them, and re-layouts  351 us (9%)
    unnamed x23, waiting for transfers between devices  1010 us
    another operation x48, other arithmetic, block_step(): jax.scipy.linalg.solve_triangular(identity_mat - paired(a_scaled, b_scale...  967 us
    reduce_scatter x1, waiting for transfers between devices, on_device(): lax.psum_scatter(totals[12], 'dp', scatter_dimension=0, tiled=True)  185 us
    reduce_scatter x1, waiting for transfers between devices, on_device(): lax.psum_scatter(totals[11], 'dp', scatter_dimension=0, tiled=True)  179 us
    reduce_scatter x1, waiting for transfers between devices, on_device(): lax.psum_scatter(totals[10], 'dp', scatter_dimension=1, tiled=True)  141 us
    unnamed x2, blocking collectives  79.4 us
  transfers between devices with their start and end apart: 15, of which 11 were waited for; matrix products, arithmetic and copies ran while one was open for 31% of the time, Pallas kernels for 0%

commit v1 on v0

v1 whole, which is shorter than its diff:
```python
import math

import jax
import jax.numpy as jnp
from jax import lax
from jax.experimental import pallas as pl
from jax.experimental.pallas import tpu as pltpu
from jax.sharding import PartitionSpec as P

bf16, f32 = jnp.bfloat16, jnp.float32
RANKS = (64, 64, 32, 128)
CUTS = (0, 64, 128, 160, 288)
LOW_FROM = (1, 4, 3, 5)
T = 128

def dn(x, y, cx, cy):
    return lax.dot_general(x, y, (((cx,), (cy,)), ((), ())), preferred_element_type=f32)

def split2(x):
    hi = x.astype(bf16)
    return hi, (x - hi.astype(f32)).astype(bf16)

def dot(x, y, cx=1, cy=0, passes=3):
    if passes == 1:
        return dn(x.astype(bf16), y.astype(bf16), cx, cy)
    xh, xl = split2(x); yh, yl = split2(y)
    return dn(xh, yh, cx, cy) + dn(xh, yl, cx, cy) + dn(xl, yh, cx, cy)

def ones_dot(left, x):
    hi = x.astype(bf16); r = x - hi.astype(f32)
    mid = r.astype(bf16); lo = (r - mid.astype(f32)).astype(bf16)
    w = x.shape[1]
    o = dn(left, jnp.concatenate([hi, mid, lo], 1), 1, 0)
    return o[:, :w] + o[:, w:2*w] + o[:, 2*w:]

def head_sum(x, J):
    hi, lo = split2(x)
    return dn(jnp.concatenate([hi, lo], 1), jnp.concatenate([J, J], 0), 1, 0)

def sig(z):
    return 1.0 / (1.0 + jnp.exp(-z))

def iota(shape, d):
    return lax.broadcasted_iota(jnp.int32, shape, d)

def consts():
    r, c = iota((T, T), 0), iota((T, T), 1)
    J = jnp.where((r // 64) == (c // 64), 1.0, 0.0).astype(bf16)
    low = jnp.where(r >= c, 1.0, 0.0).astype(bf16)
    up = jnp.where(r <= c, 1.0, 0.0).astype(bf16)
    h0 = c < 64
    return r, c, J, low, up, h0

def halves(x, h0):
    z = jnp.zeros_like(x)
    m = h0 if x.shape[0] == T else jnp.concatenate([h0, h0], 0)
    return jnp.where(m, x, z), jnp.where(m, z, x)

def prep(r_, kx, vx, ow, oa, ov, first, par, K):
    r, c, J, low, up, h0 = K
    dk0, dk1, bonus, db, sq0, sq1 = (par[i:i+1] for i in range(6))
    sg = sig(db + ow)
    ld = sg * (-0.6065306597126334)
    cum = ones_dot(low, ld)
    cm = cum - cum[63:64]
    G = jnp.exp(cm); S = jnp.exp(-cm); B = jnp.exp(cm - ld)
    ag = sig(sq0 + oa); vg = sig(sq1 + ov)
    v2 = vx + (first - vx) * vg
    kfac = 1.0 + (ag - 1.0) * dk1
    km = kx * kfac
    cc = kx * dk0
    n = lax.rsqrt(head_sum(cc * cc, J) + 1e-6)
    kk = cc * n
    return sg, ld, G, S, B, ag, vg, v2, kfac, km, n, kk

def inverse(N0, N1, K, passes):
    r, c = K[0], K[1]
    z = jnp.zeros((T, T), f32)
    eye = jnp.where(r == c, 1.0, 0.0)
    m = ((r // 2) == (c // 2))
    T0 = eye + jnp.where(m, N0, 0.0); T1 = eye + jnp.where(m, N1, 0.0)
    s = 2
    def bd(a, b):
        return jnp.concatenate([jnp.concatenate([a, z], 1), jnp.concatenate([z, b], 1)], 0)
    TT = jnp.concatenate([T0, T1], 1)
    while s < T:
        m = ((r // (2*s)) == (c // (2*s))) & ((r // s) != (c // s))
        o = dot(TT, bd(jnp.where(m, N0, 0.0), jnp.where(m, N1, 0.0)), passes=passes)
        TT = TT + dot(o, bd(TT[:, :T], TT[:, T:]), passes=passes)
        s *= 2
    res = jnp.concatenate([eye, eye], 1) - TT + dot(jnp.concatenate([N0, N1], 1), bd(TT[:, :T], TT[:, T:]))
    return TT + dot(TT, bd(res[:, :T], res[:, T:]), passes=1)

def fwd_core(r_, kx, vx, ow, oa, ov, og, first, par, pA=3, pI=1, pO=3):
    K = consts(); r, c, J, low, up, h0 = K
    sg, ld, G, S, B, ag, vg, v2, kfac, km, n, kk = prep(r_, kx, vx, ow, oa, ov, first, par, K)
    at = -kk * B; rt = r_ * G; bt = kk * ag * S; kt = km * S
    Q = jnp.concatenate([at, rt], 0); Kf = jnp.concatenate([bt, kt], 0)
    Q0, Q1 = halves(Q, h0)
    A0 = dot(Q0, Kf, 1, 1, pA); A1 = dot(Q1, Kf, 1, 1, pA)
    st = r > c; inc = r >= c
    def msk(A):
        return (jnp.where(st, A[:T, :T], 0.0), jnp.where(st, A[:T, T:], 0.0),
                jnp.where(inc, A[T:, :T], 0.0), jnp.where(inc, A[T:, T:], 0.0))
    ab0, ak0, rb0, rk0 = msk(A0); ab1, ak1, rb1, rk1 = msk(A1)
    TT = inverse(ab0, ab1, K, pI)
    v0, v1 = halves(v2, h0)
    Pm = dot(jnp.concatenate([ak0, ak1], 1), jnp.concatenate([v0, v1], 0), passes=pO)
    U = dot(TT, jnp.concatenate(halves(Pm, h0), 0), passes=pO)
    u0, u1 = halves(U, h0)
    Y = dot(jnp.concatenate([rb0, rk0, rb1, rk1], 1), jnp.concatenate([u0, v0, u1, v1], 0), passes=pO)
    mean = head_sum(Y, J) * (1/64)
    cy = Y - mean
    rstd = lax.rsqrt(head_sum(cy * cy, J) * (1/64) + 4.0)
    bonus, gain, bias = par[2:3], par[6:7], par[7:8]
    bs = head_sum(r_ * km * bonus, J)
    out = (cy * rstd * gain + bias + bs * v2) * og
    return out, TT, U, Y

def bwd_core(r_, kx, vx, ow, oa, ov, og, first, par, TT, U, Y, gg, pA=3, pW=3, pD=3):
    K = consts(); r, c, J, low, up, h0 = K
    dk0, dk1, bonus, db, sq0, sq1, gain, bias = (par[i:i+1] for i in range(8))
    sg, ld, G, S, B, ag, vg, v2, kfac, km, n, kk = prep(r_, kx, vx, ow, oa, ov, first, par, K)
    at = -kk * B; rt = r_ * G; bt = kk * ag * S; kt = km * S
    mean = head_sum(Y, J) * (1/64)
    cy = Y - mean
    rstd = lax.rsqrt(head_sum(cy * cy, J) * (1/64) + 4.0)
    gn = cy * rstd
    bs = head_sum(r_ * km * bonus, J)
    g_og = gg * (gn * gain + bias + bs * v2)
    gi = gg * og
    g_gn = gi * gain
    gY = rstd * (g_gn - head_sum(g_gn, J) * (1/64) - gn * (head_sum(g_gn * gn, J) * (1/64)))
    g_bs = head_sum(gi * v2, J)
    Q = jnp.concatenate([at, rt], 0); Kf = jnp.concatenate([bt, kt], 0)
    Q0, Q1 = halves(Q, h0)
    At0 = dot(Kf, Q0, 1, 1, pA); At1 = dot(Kf, Q1, 1, 1, pA)
    st = r < c; inc = r <= c
    akT = jnp.concatenate([jnp.where(st, At0[T:, :T], 0.0), jnp.where(st, At1[T:, :T], 0.0)], 1)
    inc2 = jnp.concatenate([inc, inc], 0)
    rT = jnp.concatenate([jnp.where(inc2, At0[:, T:], 0.0), jnp.where(inc2, At1[:, T:], 0.0)], 1)
    gy0, gy1 = halves(gY, h0)
    dUV = dot(rT, jnp.concatenate([gy0, gy1], 0), passes=pW)
    dU, dV = dUV[:T], dUV[T:]
    R = dot(TT, dU, 0, 0, pW)
    W = jnp.where(h0, R[:T], R[T:])
    w0, w1 = halves(W, h0)
    dV = dV + dot(akT, jnp.concatenate([w0, w1], 0), passes=pW)
    X = jnp.concatenate([U, v2], 0)
    Yg0 = jnp.concatenate([w0, gy0], 0); Yg1 = jnp.concatenate([w1, gy1], 0)
    r2, c2 = iota((2*T, 2*T), 0), iota((2*T, 2*T), 1)
    keep = ((r2 & 127) > (c2 & 127)) | ((r2 >= T) & ((r2 & 127) == (c2 & 127)))
    keepT = ((r2 & 127) < (c2 & 127)) | ((c2 >= T) & ((r2 & 127) == (c2 & 127)))
    dA0 = jnp.where(keep, dot(Yg0, X, 1, 1, pD), 0.0)
    dA1 = jnp.where(keep, dot(Yg1, X, 1, 1, pD), 0.0)
    dT0 = jnp.where(keepT, dot(X, Yg0, 1, 1, pD), 0.0)
    dT1 = jnp.where(keepT, dot(X, Yg1, 1, 1, pD), 0.0)
    K0, K1 = halves(Kf, h0)
    dQ = dot(jnp.concatenate([dA0, dA1], 1), jnp.concatenate([K0, K1], 0), passes=pD)
    dK = dot(jnp.concatenate([dT0, dT1], 1), jnp.concatenate([Q0, Q1], 0), passes=pD)
    da_, dr_ = dQ[:T], dQ[T:]; db_, dk_ = dK[:T], dK[T:]
    e = dr_ * rt - db_ * bt - dk_ * kt
    f = da_ * at
    g_ld = ones_dot(up, e + f) - f
    g_kk = db_ * S * ag - da_ * B
    g_b = db_ * S
    g_km = g_bs * r_ * bonus + dk_ * S
    g_r = g_bs * km * bonus + dr_ * G
    g_ag = g_b * kk + g_km * kx * dk1
    g_c = n * (g_kk - kk * head_sum(g_kk * kk, J))
    g_kx = g_km * kfac + g_c * dk0
    g_v2 = gi * bs + dV
    g_first = g_v2 * vg
    g_vx = g_v2 - g_first
    g_ov = g_first * (1.0 - vg) * (first - vx)
    g_oa = g_ag * ag * (1.0 - ag)
    g_ow = g_ld * ld * (1.0 - sg)
    def cs(x): return jnp.sum(x, 0, keepdims=True)
    pg = jnp.concatenate([cs(g_c * kx), cs(g_km * kx * (ag - 1.0)), cs(g_bs * r_ * km),
                          cs(g_ow), cs(g_oa), cs(g_ov), cs(gi * gn), cs(gi)], 0)
    return g_r, g_kx, g_vx, g_ow, g_oa, g_ov, g_og, g_first, pg


def fwd_kernel(r, k, v, ow, oa, ov, og, first, par, out, tt, u, y):
    o, t_, u_, y_ = fwd_core(
        r[...], k[...], v[...], ow[...], oa[...], ov[...], og[...],
        first[...].astype(f32), par[...])
    out[...] = o.astype(bf16)
    tt[...] = t_
    u[...] = u_
    y[...] = y_


def bwd_kernel(r, k, v, ow, oa, ov, og, first, par, tt, u, y, gg,
               gr, gk, gv, gow, goa, gov, gog, gf, gp):
    res = bwd_core(
        r[...], k[...], v[...], ow[...], oa[...], ov[...], og[...],
        first[...].astype(f32), par[...], tt[...], u[...], y[...], gg[...])
    for ref, val in zip((gr, gk, gv, gow, goa, gov, gog, gf), res[:8]):
        ref[...] = val.astype(bf16)
    gp[...] = res[8]


def specs(rows, width):
    tile = pl.BlockSpec((T, 128), lambda s, p: (s, p))
    par = pl.BlockSpec((8, 128), lambda s, p: (0, p))
    pairs = width // 128
    inv = pl.BlockSpec((T, 2 * T), lambda s, p: (s * pairs + p, 0))
    gpar = pl.BlockSpec((8, 128), lambda s, p: (s, p))
    return tile, par, inv, gpar, (rows // T, pairs)


def mixer_fwd(args, par):
    rows, width = args[0].shape
    tile, pspec, inv, gpar, grid = specs(rows, width)
    wide = jax.ShapeDtypeStruct((rows, width), f32)
    return pl.pallas_call(
        fwd_kernel,
        grid=grid,
        in_specs=[tile] * 8 + [pspec],
        out_specs=[tile, inv, tile, tile],
        out_shape=[jax.ShapeDtypeStruct((rows, width), bf16),
                   jax.ShapeDtypeStruct((rows * width // 128, 2 * T), f32), wide, wide],
        compiler_params=pltpu.CompilerParams(vmem_limit_bytes=32 * 1024 * 1024),
        name="mixer_fwd",
    )(*args, par)


def mixer_bwd(args, par, saved, gg, part, before):
    rows, width = args[0].shape
    seqs, pairs = rows // T, width // 128
    half = seqs // 2
    off = part * half
    tile = pl.BlockSpec((T, 128), lambda s, p: (s + off, p))
    pspec = pl.BlockSpec((8, 128), lambda s, p: (0, p))
    inv = pl.BlockSpec((T, 2 * T), lambda s, p: ((s + off) * pairs + p, 0))
    gpar = pl.BlockSpec((8, 128), lambda s, p: (s + off, p))
    thin = jax.ShapeDtypeStruct((rows, width), bf16)

    def body(*refs):
        bwd_kernel(*refs[:13], *refs[13 + len(before):])

    return pl.pallas_call(
        body,
        grid=(half, pairs),
        in_specs=[tile] * 8 + [pspec, inv, tile, tile, tile]
        + [pl.BlockSpec(memory_space=pl.ANY)] * len(before),
        out_specs=[tile] * 8 + [gpar],
        out_shape=[thin] * 8 + [jax.ShapeDtypeStruct((seqs * 8, width), f32)],
        input_output_aliases={13 + i: i for i in range(len(before))},
        compiler_params=pltpu.CompilerParams(vmem_limit_bytes=32 * 1024 * 1024),
        cost_estimate=pl.CostEstimate(flops=20 * 10**9, bytes_accessed=10**7, transcendentals=10**6),
        name="mixer_bwd",
    )(*args, par, *saved, gg, *before)


def layer_norm(x, gain, bias):
    c = x - jnp.mean(x, -1, keepdims=True)
    return c * lax.rsqrt(jnp.mean(c * c, -1, keepdims=True) + 1e-5) * gain + bias


def prev(z):
    z = z.reshape(-1, T, z.shape[-1])
    z = jnp.concatenate([jnp.zeros_like(z[:, :1]), z[:, :-1]], 1)
    return z.reshape(-1, z.shape[-1])


def front(x, mix, gain, bias):
    h = layer_norm(x, gain, bias)
    d = prev(h) - h
    return tuple(h + d * mix[i] for i in range(mix.shape[0]))


def mm(a, b):
    return dn(a, b, 1, 0)


def mmt(a, b):
    return dn(a, b, 1, 1)


def tmm(a, b):
    return dn(a, b, 0, 0)


def lowrank_act(zw, za, zv, zg):
    return jnp.tanh(zw), za, zv, jax.nn.sigmoid(zg)


def swap(x, bit):
    n = lax.axis_size("dp")
    return lax.ppermute(x, "dp", [(i, i ^ bit) for i in range(n)])


def add(a, b):
    return (a.astype(f32) + b.astype(f32)).astype(bf16)


def pick(x, index, axis):
    return lax.dynamic_index_in_dim(x, index, axis, keepdims=False)


def other_way(g, step):
    me = lax.axis_index("dp")
    out = []
    for part, (axis, bit) in zip(g, step):
        mine = (me // bit) % 2
        out.append(add(pick(part, mine, axis), swap(pick(part, 1 - mine, axis), bit)))
    return out


STEPS = (((2, 4), (3, 2)), ((2, 2), (2, 4)), ((1, 8), (1, 8)), ((0, 16), (0, 16)))


def chip_sum_begin(g):
    n = lax.axis_size("dp")
    if n != 32:
        groups = [list(range(c, n, 2)) for c in range(2)]
        return lax.psum_scatter(g, "dp", scatter_dimension=0, axis_index_groups=groups)
    cut = g.shape[1] // 2
    return [p.reshape((2, 2, 2, 2) + p.shape[1:]) for p in (g[:, :cut], g[:, cut:])]


def chip_sum_step(g, count=1):
    if lax.axis_size("dp") != 32:
        return g
    for _ in range(count):
        g = other_way(g, STEPS[6 - g[0].ndim])
    return g


def chip_sum_end(g):
    if lax.axis_size("dp") != 32:
        return g.astype(f32)
    return jnp.concatenate(g, 0).astype(f32)


def tie(*values):
    return lax.optimization_barrier(values)


def on_core(keep, send):
    return (keep + swap(send, 1).astype(f32)).astype(bf16)


def by_chip(g):
    chips = lax.axis_size("dp") // 2
    return g.reshape(chips, g.shape[0] // chips, g.shape[1])


def trade_rows(h):
    core = lax.axis_index("dp") % 2
    h = h.reshape(2, h.shape[0] // 2, h.shape[1])
    own, got = pick(h, core, 0), swap(pick(h, 1 - core, 0).astype(bf16), 1).astype(f32)
    return jnp.where(core == 0, own, got), jnp.where(core == 0, got, own)


def on_device(x_in, first_in, spans, gout_in, mix, gains, biases, tying, extra, dwindle,
              squash, reducing, enlarging, ingoing, concluding, ffn_key, ffn_value):
    micro, seqs, length, width = x_in.shape
    rows = micro * seqs * length
    shard = mix.shape[1]
    small = jnp.concatenate([mix, gains, biases, tying, extra[None], dwindle[None], squash], 0)
    n_small = small.shape[0]
    pad = jnp.zeros((64 - n_small, shard), bf16)
    pack = jnp.concatenate(
        [jnp.swapaxes(ingoing, 1, 2)[i] for i in range(3)]
        + [concluding.T, reducing, enlarging.T, jnp.concatenate([small, pad], 0).T], 1)
    pack = lax.all_gather(pack, "dp", axis=0, tiled=True)
    wk = lax.all_gather(ffn_key, "dp", axis=0, tiled=True)
    wv = lax.all_gather(ffn_value, "dp", axis=0, tiled=True)
    wi = [pack[:, i * width:(i + 1) * width] for i in range(3)]
    wo = pack[:, 3 * width:4 * width]
    base = 4 * width
    w_in = pack[:, base:base + CUTS[4]]
    w_out = pack[:, base + CUTS[4]:base + 2 * CUTS[4]]
    small = pack[:, base + 2 * CUTS[4]:].T.astype(f32)
    mix, gains, biases, tying = small[0:7], small[7:10], small[10:13], small[13:15]
    par = jnp.concatenate([small[13:19], gains[1:2], biases[1:2]], 0)

    x = x_in.reshape(rows, width).astype(f32)
    first = first_in.reshape(rows, width)
    place = jnp.arange(length, dtype=jnp.int32)
    valid = (place[None, None, :] < spans[:, :, None]).astype(f32).reshape(rows, 1)
    g_out = valid * gout_in.reshape(rows, width).astype(f32)
    gf = g_out.astype(bf16)

    xs, pull_front = jax.vjp(front, x, mix[:6], gains[0], biases[0])
    xs = [z.astype(bf16) for z in xs]
    proj = [mmt(xs[j], wi[i]) for i, j in enumerate((0, 2, 3))]
    zs = [mm(xs[j], w_in[:, CUTS[i]:CUTS[i + 1]]) for i, j in enumerate(LOW_FROM)]
    ls, pull_low = jax.vjp(lowrank_act, *zs)
    ls = [z.astype(bf16) for z in ls]
    os_ = [mmt(ls[i], w_out[:, CUTS[i]:CUTS[i + 1]]) for i in range(4)]
    args = (*proj, *os_, first)
    gated, *saved = mixer_fwd(args, par)
    mixed = x + mmt(gated, wo)
    (xc,), pull_chan = jax.vjp(front, mixed, mix[6:7], gains[2], biases[2])
    xc = xc.astype(bf16)
    pre = jax.nn.relu(mm(xc, wk))
    hidden = (pre * pre).astype(bf16)
    out = valid * (mixed + mm(hidden, wv))

    core = lax.axis_index("dp") % 2
    chips = lax.axis_size("dp") // 2
    scale = 1.0 / math.sqrt(rows * lax.axis_size("dp"))

    def cut(a, c):
        return pick(a.reshape(rows, chips, 2, -1), c, 2).reshape(rows, -1)

    def side(a, c):
        return lax.dynamic_slice_in_dim(a, c * (width // 2), width // 2, 1)

    d_value = on_core(tmm(cut(hidden, core), gf), tmm(cut(hidden, 1 - core), gf).astype(bf16))
    d_value = chip_sum_begin(by_chip(d_value))
    g_pre = (mmt(gf, wv) * (2.0 * pre)).astype(bf16)
    d_value, g_pre = tie(d_value, g_pre)
    d_key = on_core(tmm(xc, cut(g_pre, core)), tmm(xc, cut(g_pre, 1 - core)).astype(bf16))
    g_mixed, g_mix_c, g_gain_c, g_bias_c = pull_chan((mmt(g_pre, wk),))
    g_mixed = g_out + g_mixed
    g_att = g_mixed.astype(bf16)
    d_conc = on_core(tmm(g_att, side(gated, core)), tmm(g_att, side(gated, 1 - core)).astype(bf16))
    d_value = chip_sum_step(d_value)
    d_key = chip_sum_begin(by_chip(jnp.concatenate([d_key, d_conc], 1)))
    gg = mm(g_att, wo)
    gg, d_key, d_value = tie(gg, d_key, d_value)
    grads = mixer_bwd(args, par, saved, gg, 0, ())
    d_value = chip_sum_step(d_value)
    d_key = chip_sum_step(d_key)
    grads, d_key, d_value = tie(grads, d_key, d_value)
    grads = mixer_bwd(args, par, saved, gg, 1, grads)
    d_value = chip_sum_step(d_value)
    d_key = chip_sum_step(d_key)
    grads, d_key, d_value = tie(grads, d_key, d_value)
    d_value = chip_sum_end(chip_sum_step(d_value))
    d_key = chip_sum_end(chip_sum_step(d_key, 2))
    gp = jnp.sum(grads[8].reshape(-1, 8, width), 0)
    g_proj, g_os, g_first = grads[:3], grads[3:7], grads[7]
    g_ls = tuple(mm(g_os[i], w_out[:, CUTS[i]:CUTS[i + 1]]) for i in range(4))
    g_zs = [z.astype(bf16) for z in pull_low(g_ls)]
    back = [mmt(g_zs[i], w_in[:, CUTS[i]:CUTS[i + 1]]) for i in range(4)]
    g_xs = (mm(g_proj[0], wi[0]), back[0], mm(g_proj[1], wi[1]),
            mm(g_proj[2], wi[2]) + back[2], back[1], back[3])
    g_x, g_mix_t, g_gain_t, g_bias_t = pull_front(g_xs)
    g_x = g_mixed + g_x
    g_small = jnp.concatenate(
        [g_mix_t, g_mix_c, g_gain_t[None], gp[6:7], g_gain_c[None], g_bias_t[None], gp[7:8],
         g_bias_c[None], gp[0:6], jnp.zeros((13, width), f32)], 0).T
    fill = jnp.zeros((width, 80), f32)
    low_a = jnp.concatenate([tmm(xs[j], g_zs[i]) for i, j in enumerate(LOW_FROM)]
                            + [g_small[:, :16], fill], 1)
    low_b = jnp.concatenate([tmm(g_os[i], ls[i]) for i in range(4)] + [g_small[:, 16:], fill], 1)

    def mixer_half(c):
        return jnp.concatenate(
            [tmm(g_proj[i], side(xs[j], c)) for i, j in enumerate((0, 2, 3))]
            + [jnp.where(c == 0, low_a, low_b)], 1)

    d_mix = on_core(mixer_half(core), mixer_half(1 - core).astype(bf16))
    d_mix = chip_sum_end(chip_sum_step(chip_sum_begin(by_chip(d_mix)), 4))
    half_a, half_b = trade_rows(d_mix * scale)
    key_a, key_b = trade_rows(d_key * scale)
    hw = width // 2
    wide = [jnp.concatenate([half_a[:, i * hw:(i + 1) * hw], half_b[:, i * hw:(i + 1) * hw]], 1)
            for i in range(3)]
    d_in = jnp.stack([w.T for w in wide])
    low_a, low_b = half_a[:, 3 * hw:], half_b[:, 3 * hw:]
    d_conc = jnp.concatenate([key_a[:, -hw:], key_b[:, -hw:]], 1).T
    key_a, key_b = key_a[:, :-hw], key_b[:, :-hw]
    d_small = jnp.concatenate([low_a[:, CUTS[4]:CUTS[4] + 16], low_b[:, CUTS[4]:CUTS[4] + 16]], 1).T
    d_key = jnp.stack([key_a.reshape(shard, chips, -1), key_b.reshape(shard, chips, -1)], 2)
    d_key = d_key.reshape(shard, -1)
    return (
        out.astype(bf16).reshape(x_in.shape), g_x.astype(bf16).reshape(x_in.shape),
        g_first.reshape(x_in.shape), d_small[0:7], d_small[7:10], d_small[10:13],
        d_small[13:15], d_small[15], d_small[16], d_small[17:19],
        low_a[:, :CUTS[4]], low_b[:, :CUTS[4]].T, d_in, d_conc, d_key, d_value * scale)


def solution(mesh):
    tok, row, col = P(None, "dp", None, None), P("dp", None), P(None, "dp")
    vec, cube = P("dp"), P(None, None, "dp")
    in_specs = (tok, tok, col, tok, col, col, col, col, vec, vec, col, row, col, cube, col, row, row)
    out_specs = (tok, tok, tok, col, col, col, col, vec, vec, col, row, col, cube, col, row, row)
    return jax.shard_map(
        on_device, mesh=mesh, in_specs=in_specs, out_specs=out_specs, check_vma=False)
```

time: 3730 us -> 584 us (0.16)
  waiting for transfers between devices: 1510 us -> 221 us
  other arithmetic: 1070 us -> 32.9 us
  blocking collectives: 353 us -> 0 us
  matrix products: 407 us -> 84.9 us
  local copies, waits for them, and re-layouts: 351 us -> 100 us
  Pallas kernels: 0 us -> 97.1 us
    unnamed x23 -> x3, waiting for transfers between devices: 1010 us -> 1.39 us
    another operation x60 -> x6, other arithmetic: 979 us -> 3.06 us  [the longest x48 967 us: block_step(): jax.scipy.linalg.solve_triangular(identity_mat - paired(a_scaled, b_scale...]
    reduce_scatter x3 -> x0, waiting for transfers between devices: 505 us -> none  [the longest x1 185 us: on_device(): lax.psum_scatter(totals[12], 'dp', scatter_dimension=0, tiled=True)]
    dot_general x276 -> x48, matrix products: 376 us -> 84.9 us  [dn(): lax.dot_general(x, y, (((cx,), (cy,)), ((), ())), preferred_element_type=...]
    all_gather x7 -> x0, blocking collectives: 273 us -> none  [the longest x1 44.4 us: gather_all(): lax.all_gather(enlarging_transforms, 'dp', axis=1, tiled=True)]
    all_gather x4 -> x3, waiting for transfers between devices: 0.01 us -> 129 us  [the longest x1 83 us: on_device(): pack = lax.all_gather(pack, 'dp', axis=0, tiled=True)]
    pallas_call x0 -> x3, Pallas kernels: none -> 97.1 us  [the longest x1 53.8 us: mixer_fwd(): pl.pallas_call(fwd_kernel, grid=grid, in_specs=[tile] * 8 + [pspec], out_...]
    ppermute x0 -> x30, waiting for transfers between devices: none -> 89.7 us  [swap(): return lax.ppermute(x, 'dp', [(i, i ^ bit) for i in range(n)])]
  transfers between devices with their start and end apart: 15 -> 33, of which waited for: 11 -> 14; matrix products, arithmetic and copies ran while one was open for 31% -> 25% of each run, Pallas kernels for 0% -> 17%
where the time goes in v1:
time: 584 us; the launch traced here: 577 us
  waiting for transfers between devices  221 us (38%)
  local copies, waits for them, and re-layouts  100 us (17%)
  Pallas kernels  97.1 us (17%)
  matrix products  84.9 us (15%)
  other arithmetic  32.9 us (6%)
  starting transfers between devices  25.3 us (4%)
  between operations  15.8 us (3%)
    ppermute x30, waiting for transfers between devices, swap(): return lax.ppermute(x, 'dp', [(i, i ^ bit) for i in range(n)])  89.7 us
    dot_general x48, matrix products, dn(): lax.dot_general(x, y, (((cx,), (cy,)), ((), ())), preferred_element_type=...  84.9 us
    all_gather x1, waiting for transfers between devices, on_device(): pack = lax.all_gather(pack, 'dp', axis=0, tiled=True)  83 us
    pallas_call x1, Pallas kernels, mixer_fwd(): pl.pallas_call(fwd_kernel, grid=grid, in_specs=[tile] * 8 + [pspec], out_...  53.8 us
    unnamed x179, local copies, waits for them, and re-layouts  45.8 us
    pallas_call x2, Pallas kernels, mixer_bwd(): pl.pallas_call(body, grid=(half, pairs), in_specs=[tile] * 8 + [pspec, in...  43.3 us
    all_gather x1, waiting for transfers between devices, on_device(): wv = lax.all_gather(ffn_value, 'dp', axis=0, tiled=True)  38.5 us
    ppermute x30, starting transfers between devices, swap(): return lax.ppermute(x, 'dp', [(i, i ^ bit) for i in range(n)])  25.2 us
  transfers between devices with their start and end apart: 33, of which 14 were waited for; matrix products, arithmetic and copies ran while one was open for 25% of the time, Pallas kernels for 17%

profile of v1, /device:TPU:0, one launch (start us, length us, event | category | flops | bytes accessed | tf_op | source)
XLA Modules:
  0.0 576.8 jit_solution(3797383759707090015)
XLA Ops:
  18.5 83.0 %all-gather.4.cloned.1.call-done = bf16[1024,4736]{1,0:T(8,128)(2,1)} async-done(((bf16[32,4736]{1,0:T(8,128)(2,1)}), bf16[1024,4736]{1,0:T(8,128)(2,1)}) %all-gather.4.cloned.1.call-update) | async-done | bytes 9699344 | tf_op jit(solution)/shard_map/all_gather | solution.py:369
  114.1 53.8 %mixer_fwd.1 = (bf16[256,1024]{1,0:T(8,128)(2,1)S(1)}, f32[2048,256]{1,0:T(8,128)S(1)}, f32[256,1024]{1,0:T(8,128)S(1)}, f32[256,1024]{1,0:T(8,128)S(1)}) custom-call(f32[256,1024]{1,0:T(8,128)S(1)} %fusion.22.r.refs_0_, f32[256,1024]{1,0:T(8,128)S(1)} %fusion.18.k.refs_1_, f32[256,1024]{1,0:T(8,128)S(1)} %fusion.14.v.refs_2_, ...), custom_call_target="tpu_custom_call" | custom-call | tf_op jit(solution)/shard_map/mixer_fwd/pallas_call | solution.py:217
  172.9 8.0 %all-gather.6.cloned.1.call-done = bf16[1024,4096]{1,0:T(8,128)(2,1)} async-done(((bf16[32,4096]{1,0:T(8,128)(2,1)}), bf16[1024,4096]{1,0:T(8,128)(2,1)}) %all-gather.6.cloned.1.call-update) | async-done | bytes 8388624 | tf_op jit(solution)/shard_map/all_gather | solution.py:370
  180.9 8.6 %multiply_convert_fusion = (bf16[256,4096]{1,0:T(8,128)(2,1)}, f32[256,4096]{1,0:T(8,128)}) fusion(bf16[256,1024]{1,0:T(8,128)(2,1)} %add_convert_fusion.4, bf16[1024,4096]{1,0:T(8,128)(2,1)} %all-gather.6.cloned.1.call-done), kind=kOutput, calls=%fused_computation.8 | convolution fusion | flops 2150629376 | bytes 15204352 | tf_op jit(solution)/shard_map/dot_general | solution.py:17
  194.0 8.5 %constant_dynamic-slice_fusion.7 = (bf16[256,16,1,128]{3,2,1,0:T(2,128)(2,1)}, bf16[256,16,1,128]{3,2,1,0:T(2,128)(2,1)}) fusion(bf16[256,16,2,128]{3,2,1,0:T(2,128)(2,1)} %reshape.389, s32[]{:T(128)S(6)} %select_n.246, s32[]{:T(128)S(6)} %select_n.245), kind=kLoop, calls=%fused_computation.277 | loop fusion | bytes 4194312 | tf_op jit(solution)/shard_map/jit(dynamic_index_in_dim)/dynamic_slice | solution.py:300
  202.6 5.8 %copy.128 = bf16[256,16,1,128]{0,3,1,2:T(8,128)(2,1)} copy(bf16[256,16,1,128]{3,2,1,0:T(2,128)(2,1)} %get-tuple-element.206) | data formatting | bytes 2097152
  215.4 6.0 %copy.127 = bf16[256,16,1,128]{0,3,1,2:T(8,128)(2,1)} copy(bf16[256,16,1,128]{3,2,1,0:T(2,128)(2,1)} %get-tuple-element.207) | data formatting | bytes 2097152
  221.4 38.5 %all-gather.8.cloned.1.call-done = bf16[4096,1024]{1,0:T(8,128)(2,1)} async-done(((bf16[128,1024]{1,0:T(8,128)(2,1)}), bf16[4096,1024]{1,0:T(8,128)(2,1)}) %all-gather.8.cloned.1.call-update) | async-done | bytes 8388624 | tf_op jit(solution)/shard_map/all_gather | solution.py:371
  259.9 8.7 %fusion.1 = bf16[256,4096]{1,0:T(8,128)(2,1)} fusion(bf16[256,1024]{1,0:T(8,128)(2,1)} %fusion.63, bf16[4096,1024]{1,0:T(8,128)(2,1)} %all-gather.8.cloned.1.call-done, f32[256,4096]{1,0:T(8,128)} %get-tuple-element.255), kind=kOutput, calls=%fused_computation.7 | convolution fusion | flops 2150629376 | bytes 15204352 | tf_op jit(solution)/shard_map/dot_general | solution.py:17
  279.1 8.5 %constant_dynamic-slice_fusion.5 = (bf16[256,16,1,128]{3,2,1,0:T(2,128)(2,1)}, bf16[256,16,1,128]{3,2,1,0:T(2,128)(2,1)}) fusion(bf16[256,16,2,128]{3,2,1,0:T(2,128)(2,1)} %reshape.397, s32[]{:T(128)S(6)} %select_n.246, s32[]{:T(128)S(6)} %select_n.245), kind=kLoop, calls=%fused_computation.275 | loop fusion | bytes 4194312 | tf_op jit(solution)/shard_map/jit(dynamic_index_in_dim)/dynamic_slice | solution.py:300
  287.6 6.2 %copy.130 = bf16[256,16,1,128]{0,3,1,2:T(8,128)(2,1)} copy(bf16[256,16,1,128]{3,2,1,0:T(2,128)(2,1)} %get-tuple-element.204) | data formatting | bytes 2097152
  293.8 4.9 convolution_convert_fusion
  299.0 5.9 %broadcast_multiply_fusion = (f32[256,1024]{1,0:T(8,128)S(1)}, f32[256,1024]{1,0:T(8,128)S(1)}) fusion(f32[1024]{0:T(1024)S(1)} %bitcast.463, bf16[256,4096]{1,0:T(8,128)(2,1)S(1)} %copy-done.69, bf16[1024,4096]{1,0:T(8,128)(2,1)} %all-gather.6.cloned.1.call-done), kind=kOutput, calls=%fused_computation.162 | convolution fusion | flops 2147745792 | bytes 12587008 | tf_op jit(solution)/shard_map/dot_general | solution.py:17
  317.6 5.9 %copy.129 = bf16[256,16,1,128]{0,3,1,2:T(8,128)(2,1)} copy(bf16[256,16,1,128]{3,2,1,0:T(2,128)(2,1)} %get-tuple-element.205) | data formatting | bytes 2097152
  326.2 9.2 %collective-permute-done.3 = bf16[2,2,2,64,1024]{4,3,2,1,0:T(8,128)(2,1)} collective-permute-done((bf16[2,2,2,64,1024]{4,3,2,1,0:T(8,128)(2,1)}, bf16[2,2,2,64,1024]{4,3,2,1,0:T(8,128)(2,1)}, u32[]{:S(2)}, u32[]{:S(2)}) %collective-permute-start.3) | collective-permute-done | bytes 1048608 | tf_op jit(solution)/shard_map/ppermute | solution.py:292
  353.8 21.6 %mixer_bwd.2 = (bf16[256,1024]{1,0:T(8,128)(2,1)S(1)}, bf16[256,1024]{1,0:T(8,128)(2,1)S(1)}, bf16[256,1024]{1,0:T(8,128)(2,1)S(1)}, bf16[256,1024]{1,0:T(8,128)...) custom-call(f32[256,1024]{1,0:T(8,128)S(1)} %copy-done.7, ...), custom_call_target="tpu_custom_call" | custom-call | flops 20000000000 | bytes 10000000 | tf_op jit(solution)/shard_map/mixer_bwd/pallas_call | solution.py:243
  375.9 14.9 %collective-permute-done.6 = bf16[2,2,2,32,2560]{4,3,0,1,2:T(8,128)(2,1)S(1)} collective-permute-done((bf16[2,2,2,32,2560]{4,3,0,1,2:T(8,128)(2,1)S(1)}, bf16[2,2,2,32,2560]{4,3,0,1,2:T(8,128)(2,1)S(1)}, u32[]{:S(2)}, u32[]{:S(2)}) %collective-permute-start.6) | collective-permute-done | bytes 1310752 | tf_op jit(solution)/shard_map/ppermute | solution.py:292
  395.8 21.6 %mixer_bwd.3 = (bf16[256,1024]{1,0:T(8,128)(2,1)S(1)}, bf16[256,1024]{1,0:T(8,128)(2,1)S(1)}, bf16[256,1024]{1,0:T(8,128)(2,1)S(1)}, bf16[256,1024]{1,0:T(8,128)...) custom-call(f32[256,1024]{1,0:T(8,128)S(1)} %copy-done.7, ...), custom_call_target="tpu_custom_call", output_to_operand_aliasing={{0}: (13, {}), {1}: (14, {}), {2}: (15, {}), {3}: (16, {}),... | custom-call | flops 20000000000 | bytes 10000000 | tf_op jit(solution)/shard_map/mixer_bwd/pallas_call | solution.py:243
  475.6 10.9 %collective-permute-done.26 = bf16[32,2560]{1,0:T(8,128)(2,1)S(1)} collective-permute-done((bf16[32,2560]{1,0:T(8,128)(2,1)S(1)}, bf16[32,2560]{1,0:T(8,128)(2,1)S(1)}, u32[]{:S(2)}, u32[]{:S(2)}) %collective-permute-start.26) | collective-permute-done | bytes 163872 | tf_op jit(solution)/shard_map/ppermute | solution.py:292
  492.8 6.2 %copy.112 = bf16[1024,1920]{1,0:T(8,128)(2,1)} copy(bf16[1024,1920]{0,1:T(8,128)(2,1)} %fusion) | data formatting | bytes 7864320 | tf_op jit(solution)/shard_map/convert_element_type | solution.py:343
  504.2 21.6 %collective-permute-done.18 = bf16[2,2,2,32,1920]{4,3,2,1,0:T(8,128)(2,1)S(1)} collective-permute-done((bf16[2,2,2,32,1920]{4,3,2,1,0:T(8,128)(2,1)S(1)}, bf16[2,2,2,32,1920]{4,3,2,1,0:T(8,128)(2,1)S(1)}, u32[]{:S(2)}, u32[]{:S(2)}) %collective-permute-start.18) | collective-permute-done | bytes 983072 | tf_op jit(solution)/shard_map/ppermute | solution.py:292
  528.5 10.4 %collective-permute-done.19 = bf16[2,2,32,1920]{3,2,1,0:T(8,128)(2,1)S(1)} collective-permute-done((bf16[2,2,32,1920]{3,2,1,0:T(8,128)(2,1)S(1)}, bf16[2,2,32,1920]{3,2,1,0:T(8,128)(2,1)S(1)}, u32[]{:S(2)}, u32[]{:S(2)}) %collective-permute-start.19) | collective-permute-done | bytes 491552 | tf_op jit(solution)/shard_map/ppermute | solution.py:292
  541.4 8.0 %collective-permute-done.20 = bf16[2,32,1920]{2,1,0:T(8,128)(2,1)S(1)} collective-permute-done((bf16[2,32,1920]{2,1,0:T(8,128)(2,1)S(1)}, bf16[2,32,1920]{2,1,0:T(8,128)(2,1)S(1)}, u32[]{:S(2)}, u32[]{:S(2)}) %collective-permute-start.20) | collective-permute-done | bytes 245792 | tf_op jit(solution)/shard_map/ppermute | solution.py:292
  553.3 6.3 %collective-permute-done.21 = bf16[32,1920]{1,0:T(8,128)(2,1)S(1)} collective-permute-done((bf16[32,1920]{1,0:T(8,128)(2,1)S(1)}, bf16[32,1920]{1,0:T(8,128)(2,1)S(1)}, u32[]{:S(2)}, u32[]{:S(2)}) %collective-permute-start.21) | collective-permute-done | bytes 122912 | tf_op jit(solution)/shard_map/ppermute | solution.py:292
  (415 shorter events, 177.9 us)
Async XLA Ops:
  7.2 94.3 %all-gather.4.cloned.1.call-start = ((), (), s32[]{:S(2)}) async-start(), calls=%async_computation | async-start | bytes 10002432 | tf_op jit(solution)/shard_map/all_gather | solution.py:369
  15.4 165.5 %all-gather.6.cloned.1.call-start = ((), (), s32[]{:S(2)}) async-start(), calls=%async_computation.1 | async-start | bytes 8650752 | tf_op jit(solution)/shard_map/all_gather | solution.py:370
  16.1 243.8 %all-gather.8.cloned.1.call-start = ((), (), s32[]{:S(2)}) async-start(), calls=%async_computation.2 | async-start | bytes 8650752 | tf_op jit(solution)/shard_map/all_gather | solution.py:371
  213.0 55.5 %collective-permute-start = (bf16[2048,1024]{1,0:T(8,128)(2,1)}, bf16[2048,1024]{1,0:T(8,128)(2,1)}, u32[]{:S(2)}, u32[]{:S(2)}) collective-permute-start(bf16[2048,1024]{1,0:T(8,128)(2,1)} %convolution_convert_fusion.1), channel_id=1, source_target_pairs={{0,1},{1,0},{2,3},{3,2},{4,5},{5,4},{6,7},{7,6},{8,9},{9,8},{10,11... | collective-permute-start | bytes 12582920 | tf_op jit(solution)/shard_map/ppermute | solution.py:292
  298.7 44.9 %collective-permute-start.1 = (bf16[1024,2048]{1,0:T(8,128)(2,1)}, bf16[1024,2048]{1,0:T(8,128)(2,1)}, u32[]{:S(2)}, u32[]{:S(2)}) collective-permute-start(bf16[1024,2048]{1,0:T(8,128)(2,1)} %convolution_convert_fusion), channel_id=1, source_target_pairs={{0,1},{1,0},{2,3},{3,2},{4,5},{5,4},{6,7},{7,6},{8,9},{9,8},{10,11... | collective-permute-start | bytes 12582920 | tf_op jit(solution)/shard_map/ppermute | solution.py:292
  307.5 33.4 %collective-permute-start.4 = (bf16[2,2,2,64,1024]{4,3,0,1,2:T(8,128)(2,1)}, bf16[2,2,2,64,1024]{4,3,0,1,2:T(8,128)(2,1)}, u32[]{:S(2)}, u32[]{:S(2)}) collective-permute-start(bf16[2,2,2,64,1024]{4,3,0,1,2:T(8,128)(2,1)} %copy_bitcast_fusion.2), channel_id=1, source_target_pairs={{0,2},{1,3},{2,0},{3,1},{4,6},{5,7},{6,4},{7,5},{8,10},{9,11},{10,... | collective-permute-start | bytes 3145736 | tf_op jit(solution)/shard_map/ppermute | solution.py:292
  310.1 25.4 %collective-permute-start.3 = (bf16[2,2,2,64,1024]{4,3,2,1,0:T(8,128)(2,1)}, bf16[2,2,2,64,1024]{4,3,2,1,0:T(8,128)(2,1)}, u32[]{:S(2)}, u32[]{:S(2)}) collective-permute-start(bf16[2,2,2,64,1024]{4,3,2,1,0:T(8,128)(2,1)} %dynamic-slice_bitcast_fusion), channel_id=1, source_target_pairs={{0,4},{1,5},{2,6},{3,7},{4,0},{5,1},{6,2},{7,3},{8,12},{9,13},{10,... | collective-permute-start | bytes 3145736 | tf_op jit(solution)/shard_map/ppermute | solution.py:292
  314.4 23.7 %collective-permute-start.2 = (bf16[1024,512]{1,0:T(8,128)(2,1)}, bf16[1024,512]{1,0:T(8,128)(2,1)}, u32[]{:S(2)}, u32[]{:S(2)}) collective-permute-start(bf16[1024,512]{1,0:T(8,128)(2,1)} %convolution_convert_fusion.5), channel_id=1, source_target_pairs={{0,1},{1,0},{2,3},{3,2},{4,5},{5,4},{6,7},{7,6},{8,9},{9,8},{10,11... | collective-permute-start | bytes 3145736 | tf_op jit(solution)/shard_map/ppermute | solution.py:292
  349.4 26.1 %collective-permute-start.8 = (bf16[2,2,64,1024]{3,2,0,1:T(8,128)(2,1)S(1)}, bf16[2,2,64,1024]{3,2,0,1:T(8,128)(2,1)S(1)}, u32[]{:S(2)}, u32[]{:S(2)}) collective-permute-start(bf16[2,2,64,1024]{3,2,0,1:T(8,128)(2,1)S(1)} %dynamic-slice_bitcast_fusion.4), channel_id=1, source_target_pairs={{0,4},{1,5},{2,6},{3,7},{4,0},{5,1},{6,2},{7,3},{8,12},{9,13},{10,... | collective-permute-start | bytes 1572872 | tf_op jit(solution)/shard_map/ppermute | solution.py:292
  350.1 25.6 %collective-permute-start.7 = (bf16[2,2,64,1024]{3,2,1,0:T(8,128)(2,1)S(1)}, bf16[2,2,64,1024]{3,2,1,0:T(8,128)(2,1)S(1)}, u32[]{:S(2)}, u32[]{:S(2)}) collective-permute-start(bf16[2,2,64,1024]{3,2,1,0:T(8,128)(2,1)S(1)} %dynamic-slice_bitcast_fusion.5), channel_id=1, source_target_pairs={{0,2},{1,3},{2,0},{3,1},{4,6},{5,7},{6,4},{7,5},{8,10},{9,11},{10,... | collective-permute-start | bytes 1572872 | tf_op jit(solution)/shard_map/ppermute | solution.py:292
  351.7 39.1 %collective-permute-start.6 = (bf16[2,2,2,32,2560]{4,3,0,1,2:T(8,128)(2,1)S(1)}, bf16[2,2,2,32,2560]{4,3,0,1,2:T(8,128)(2,1)S(1)}, u32[]{:S(2)}, u32[]{:S(2)}) collective-permute-start(bf16[2,2,2,32,2560]{4,3,0,1,2:T(8,128)(2,1)S(1)} %copy_bitcast_fusion), channel_id=1, source_target_pairs={{0,2},{1,3},{2,0},{3,1},{4,6},{5,7},{6,4},{7,5},{8,10},{9,11},{10,... | collective-permute-start | bytes 3932168 | tf_op jit(solution)/shard_map/ppermute | solution.py:292
  352.3 38.8 %collective-permute-start.5 = (bf16[2,2,2,32,2560]{4,3,0,1,2:T(8,128)(2,1)S(1)}, bf16[2,2,2,32,2560]{4,3,0,1,2:T(8,128)(2,1)S(1)}, u32[]{:S(2)}, u32[]{:S(2)}) collective-permute-start(bf16[2,2,2,32,2560]{4,3,0,1,2:T(8,128)(2,1)S(1)} %copy_bitcast_fusion.1), channel_id=1, source_target_pairs={{0,4},{1,5},{2,6},{3,7},{4,0},{5,1},{6,2},{7,3},{8,12},{9,13},{10,... | collective-permute-start | bytes 3932168 | tf_op jit(solution)/shard_map/ppermute | solution.py:292
  391.6 25.9 %collective-permute-start.12 = (bf16[2,64,1024]{2,1,0:T(8,128)(2,1)S(1)}, bf16[2,64,1024]{2,1,0:T(8,128)(2,1)S(1)}, u32[]{:S(2)}, u32[]{:S(2)}) collective-permute-start(bf16[2,64,1024]{2,1,0:T(8,128)(2,1)S(1)} %dynamic-slice_bitcast_fusion.10), channel_id=1, source_target_pairs={{0,8},{1,9},{2,10},{3,11},{4,12},{5,13},{6,14},{7,15},{8,0},{9,1},... | collective-permute-start | bytes 786440 | tf_op jit(solution)/shard_map/ppermute | solution.py:292
  393.1 24.4 %collective-permute-start.11 = (bf16[2,64,1024]{2,1,0:T(8,128)(2,1)S(1)}, bf16[2,64,1024]{2,1,0:T(8,128)(2,1)S(1)}, u32[]{:S(2)}, u32[]{:S(2)}) collective-permute-start(bf16[2,64,1024]{2,1,0:T(8,128)(2,1)S(1)} %dynamic-slice_bitcast_fusion.11), channel_id=1, source_target_pairs={{0,8},{1,9},{2,10},{3,11},{4,12},{5,13},{6,14},{7,15},{8,0},{9,1},... | collective-permute-start | bytes 786440 | tf_op jit(solution)/shard_map/ppermute | solution.py:292
  393.8 23.9 %collective-permute-start.10 = (bf16[2,2,32,2560]{3,2,0,1:T(8,128)(2,1)S(1)}, bf16[2,2,32,2560]{3,2,0,1:T(8,128)(2,1)S(1)}, u32[]{:S(2)}, u32[]{:S(2)}) collective-permute-start(bf16[2,2,32,2560]{3,2,0,1:T(8,128)(2,1)S(1)} %dynamic-slice_bitcast_fusion.2), channel_id=1, source_target_pairs={{0,4},{1,5},{2,6},{3,7},{4,0},{5,1},{6,2},{7,3},{8,12},{9,13},{10,... | collective-permute-start | bytes 1966088 | tf_op jit(solution)/shard_map/ppermute | solution.py:292
  395.2 22.6 %collective-permute-start.9 = (bf16[2,2,32,2560]{3,2,0,1:T(8,128)(2,1)S(1)}, bf16[2,2,32,2560]{3,2,0,1:T(8,128)(2,1)S(1)}, u32[]{:S(2)}, u32[]{:S(2)}) collective-permute-start(bf16[2,2,32,2560]{3,2,0,1:T(8,128)(2,1)S(1)} %dynamic-slice_bitcast_fusion.3), channel_id=1, source_target_pairs={{0,2},{1,3},{2,0},{3,1},{4,6},{5,7},{6,4},{7,5},{8,10},{9,11},{10,... | collective-permute-start | bytes 1966088 | tf_op jit(solution)/shard_map/ppermute | solution.py:292
  428.0 39.3 %collective-permute-start.29 = (bf16[64,1024]{1,0:T(8,128)(2,1)}, bf16[64,1024]{1,0:T(8,128)(2,1)}, u32[]{:S(2)}, u32[]{:S(2)}) collective-permute-start(bf16[64,1024]{1,0:T(8,128)(2,1)} %dynamic-slice_bitcast_fusion.16), channel_id=1, source_target_pairs={{0,16},{1,17},{2,18},{3,19},{4,20},{5,21},{6,22},{7,23},{8,24},{9,... | collective-permute-start | bytes 393224 | tf_op jit(solution)/shard_map/ppermute | solution.py:292
  429.9 38.4 %collective-permute-start.28 = (bf16[64,1024]{1,0:T(8,128)(2,1)}, bf16[64,1024]{1,0:T(8,128)(2,1)}, u32[]{:S(2)}, u32[]{:S(2)}) collective-permute-start(bf16[64,1024]{1,0:T(8,128)(2,1)} %dynamic-slice_bitcast_fusion.17), channel_id=1, source_target_pairs={{0,16},{1,17},{2,18},{3,19},{4,20},{5,21},{6,22},{7,23},{8,24},{9,... | collective-permute-start | bytes 393224 | tf_op jit(solution)/shard_map/ppermute | solution.py:292
  432.4 37.7 %collective-permute-start.25 = (bf16[2,32,2560]{2,1,0:T(8,128)(2,1)}, bf16[2,32,2560]{2,1,0:T(8,128)(2,1)}, u32[]{:S(2)}, u32[]{:S(2)}) collective-permute-start(bf16[2,32,2560]{2,1,0:T(8,128)(2,1)} %dynamic-slice_bitcast_fusion.8), channel_id=1, source_target_pairs={{0,8},{1,9},{2,10},{3,11},{4,12},{5,13},{6,14},{7,15},{8,0},{9,1},... | collective-permute-start | bytes 983048 | tf_op jit(solution)/shard_map/ppermute | solution.py:292
  433.9 39.5 %collective-permute-start.23 = (bf16[2,32,2560]{2,1,0:T(8,128)(2,1)}, bf16[2,32,2560]{2,1,0:T(8,128)(2,1)}, u32[]{:S(2)}, u32[]{:S(2)}) collective-permute-start(bf16[2,32,2560]{2,1,0:T(8,128)(2,1)} %dynamic-slice_bitcast_fusion.9), channel_id=1, source_target_pairs={{0,8},{1,9},{2,10},{3,11},{4,12},{5,13},{6,14},{7,15},{8,0},{9,1},... | collective-permute-start | bytes 983048 | tf_op jit(solution)/shard_map/ppermute | solution.py:292
  467.2 22.4 %collective-permute-start.13 = (bf16[1024,1920]{0,1:T(8,128)(2,1)S(1)}, bf16[1024,1920]{0,1:T(8,128)(2,1)S(1)}, u32[]{:S(2)}, u32[]{:S(2)}) collective-permute-start(bf16[1024,1920]{0,1:T(8,128)(2,1)S(1)} %pad_maximum_fusion.1), channel_id=1, source_target_pairs={{0,1},{1,0},{2,3},{3,2},{4,5},{5,4},{6,7},{7,6},{8,9},{9,8},{10,11... | collective-permute-start | bytes 11796488 | tf_op jit(solution)/shard_map/ppermute | solution.py:292
  471.4 15.0 %collective-permute-start.26 = (bf16[32,2560]{1,0:T(8,128)(2,1)S(1)}, bf16[32,2560]{1,0:T(8,128)(2,1)S(1)}, u32[]{:S(2)}, u32[]{:S(2)}) collective-permute-start(bf16[32,2560]{1,0:T(8,128)(2,1)S(1)} %dynamic-slice_bitcast_fusion.14), channel_id=1, source_target_pairs={{0,16},{1,17},{2,18},{3,19},{4,20},{5,21},{6,22},{7,23},{8,24},{9,... | collective-permute-start | bytes 491528 | tf_op jit(solution)/shard_map/ppermute | solution.py:292
  501.5 24.2 %collective-permute-start.18 = (bf16[2,2,2,32,1920]{4,3,2,1,0:T(8,128)(2,1)S(1)}, bf16[2,2,2,32,1920]{4,3,2,1,0:T(8,128)(2,1)S(1)}, u32[]{:S(2)}, u32[]{:S(2)}) collective-permute-start(bf16[2,2,2,32,1920]{4,3,2,1,0:T(8,128)(2,1)S(1)} %dynamic-slice_bitcast_fusion.1), channel_id=1, source_target_pairs={{0,2},{1,3},{2,0},{3,1},{4,6},{5,7},{6,4},{7,5},{8,10},{9,11},{10,... | collective-permute-start | bytes 2949128 | tf_op jit(solution)/shard_map/ppermute | solution.py:292
  503.3 24.3 %collective-permute-start.14 = (bf16[2,2,2,32,1920]{4,3,0,1,2:T(8,128)(2,1)S(1)}, bf16[2,2,2,32,1920]{4,3,0,1,2:T(8,128)(2,1)S(1)}, u32[]{:S(2)}, u32[]{:S(2)}) collective-permute-start(bf16[2,2,2,32,1920]{4,3,0,1,2:T(8,128)(2,1)S(1)} %bitcast.422), channel_id=1, source_target_pairs={{0,4},{1,5},{2,6},{3,7},{4,0},{5,1},{6,2},{7,3},{8,12},{9,13},{10,... | collective-permute-start | bytes 2949128 | tf_op jit(solution)/shard_map/ppermute | solution.py:292
  (89 other events, 661.1 us)
Sparse Core Ops, SparseCore 0:
  15.5 85.9 all-gather.3
  104.3 76.4 all-gather.5
  183.7 76.1 all-gather.7

commit v2 on v1

--- a/solution.py
+++ b/solution.py
@@ -181,77 +181,187 @@
     return g_r, g_kx, g_vx, g_ow, g_oa, g_ov, g_og, g_first, pg
 
 
-def fwd_kernel(r, k, v, ow, oa, ov, og, first, par, out, tt, u, y):
-    o, t_, u_, y_ = fwd_core(
-        r[...], k[...], v[...], ow[...], oa[...], ov[...], og[...],
-        first[...].astype(f32), par[...])
-    out[...] = o.astype(bf16)
-    tt[...] = t_
-    u[...] = u_
-    y[...] = y_
-
-
-def bwd_kernel(r, k, v, ow, oa, ov, og, first, par, tt, u, y, gg,
-               gr, gk, gv, gow, goa, gov, gog, gf, gp):
-    res = bwd_core(
-        r[...], k[...], v[...], ow[...], oa[...], ov[...], og[...],
-        first[...].astype(f32), par[...], tt[...], u[...], y[...], gg[...])
-    for ref, val in zip((gr, gk, gv, gow, goa, gov, gog, gf), res[:8]):
-        ref[...] = val.astype(bf16)
-    gp[...] = res[8]
-
-
-def specs(rows, width):
-    tile = pl.BlockSpec((T, 128), lambda s, p: (s, p))
-    par = pl.BlockSpec((8, 128), lambda s, p: (0, p))
-    pairs = width // 128
-    inv = pl.BlockSpec((T, 2 * T), lambda s, p: (s * pairs + p, 0))
-    gpar = pl.BlockSpec((8, 128), lambda s, p: (s, p))
-    return tile, par, inv, gpar, (rows // T, pairs)
-
-
-def mixer_fwd(args, par):
+def fwd_kernel(*refs):
+    ins, par, outs = refs[:8], refs[8], refs[9:]
+    for q in range(2):
+        rows = pl.ds(q * T, T)
+        vals = [ref[rows, :] for ref in ins]
+        res = fwd_core(*vals[:7], vals[7].astype(f32), par[...])
+        outs[0][rows, :] = res[0].astype(bf16)
+        for ref, val in zip(outs[1:], res[1:]):
+            ref[rows, :] = val
+
+
+def bwd_kernel(*refs):
+    ins, par, saved, outs = refs[:8], refs[8], refs[9:13], refs[13:]
+    for q in range(2):
+        rows = pl.ds(q * T, T)
+        vals = [ref[rows, :] for ref in ins]
+        res = bwd_core(*vals[:7], vals[7].astype(f32), par[...], *[ref[rows, :] for ref in saved])
+        for ref, val in zip(outs[:8], res[:8]):
+            ref[rows, :] = val.astype(bf16)
+        outs[8][pl.ds(q * 8, 8), :] = res[8]
+        for ref, val in zip(outs[9:], res[:3]):
+            ref[rows, :] = val.astype(bf16)
+
+
+MIXER = dict(
+    compiler_params=pltpu.CompilerParams(vmem_limit_bytes=32 * 1024 * 1024),
+    cost_estimate=pl.CostEstimate(flops=10 * 10**9, bytes_accessed=10**7, transcendentals=10**6))
+
+
+def mixer_fwd(args, par, part, before):
     rows, width = args[0].shape
-    tile, pspec, inv, gpar, grid = specs(rows, width)
+    seqs, pairs = rows // T, width // 128
+    p0 = part * (pairs // 4)
+    tile = pl.BlockSpec((2 * T, 128), lambda s, p: (s, p + p0))
+    pspec = pl.BlockSpec((8, 128), lambda s, p: (0, p + p0))
+    inv = pl.BlockSpec((2 * T, 2 * T), lambda s, p: (s * pairs + p + p0, 0))
     wide = jax.ShapeDtypeStruct((rows, width), f32)
+
+    def body(*refs):
+        fwd_kernel(*refs[:9], *refs[9 + len(before):])
+
     return pl.pallas_call(
-        fwd_kernel,
-        grid=grid,
-        in_specs=[tile] * 8 + [pspec],
+        body,
+        grid=(seqs // 2, pairs // 4),
+        in_specs=[tile] * 8 + [pspec] + [pl.BlockSpec(memory_space=pl.ANY)] * len(before),
         out_specs=[tile, inv, tile, tile],
         out_shape=[jax.ShapeDtypeStruct((rows, width), bf16),
-                   jax.ShapeDtypeStruct((rows * width // 128, 2 * T), f32), wide, wide],
-        compiler_params=pltpu.CompilerParams(vmem_limit_bytes=32 * 1024 * 1024),
+                   jax.ShapeDtypeStruct((rows * pairs, 2 * T), f32), wide, wide],
+        input_output_aliases={9 + i: i for i in range(len(before))},
         name="mixer_fwd",
-    )(*args, par)
-
-
-def mixer_bwd(args, par, saved, gg, part, before):
+        **MIXER,
+    )(*args, par, *before)
+
+
+def mixer_bwd(args, par, saved, gg, side, part, before):
     rows, width = args[0].shape
     seqs, pairs = rows // T, width // 128
-    half = seqs // 2
-    off = part * half
-    tile = pl.BlockSpec((T, 128), lambda s, p: (s + off, p))
-    pspec = pl.BlockSpec((8, 128), lambda s, p: (0, p))
-    inv = pl.BlockSpec((T, 2 * T), lambda s, p: ((s + off) * pairs + p, 0))
-    gpar = pl.BlockSpec((8, 128), lambda s, p: (s + off, p))
+    keep, p0 = part // 2, part % 2 * (pairs // 4)
+
+    def pair(p, side):
+        return 2 * (p + p0) + (side[0] if keep else 1 - side[0])
+
+    tile = pl.BlockSpec((2 * T, 128), lambda s, p, side: (s, pair(p, side)))
+    pspec = pl.BlockSpec((8, 128), lambda s, p, side: (0, pair(p, side)))
+    inv = pl.BlockSpec((2 * T, 2 * T), lambda s, p, side: (s * pairs + pair(p, side), 0))
+    gpar = pl.BlockSpec((16, 128), lambda s, p, side: (s, pair(p, side)))
+    rel = pl.BlockSpec((2 * T, 128), lambda s, p, side: (s, p + p0 + keep * (pairs // 2)))
     thin = jax.ShapeDtypeStruct((rows, width), bf16)
 
     def body(*refs):
-        bwd_kernel(*refs[:13], *refs[13 + len(before):])
+        bwd_kernel(*refs[1:14], *refs[14 + len(before):])
 
     return pl.pallas_call(
         body,
-        grid=(half, pairs),
-        in_specs=[tile] * 8 + [pspec, inv, tile, tile, tile]
-        + [pl.BlockSpec(memory_space=pl.ANY)] * len(before),
-        out_specs=[tile] * 8 + [gpar],
-        out_shape=[thin] * 8 + [jax.ShapeDtypeStruct((seqs * 8, width), f32)],
-        input_output_aliases={13 + i: i for i in range(len(before))},
+        grid_spec=pltpu.PrefetchScalarGridSpec(
+            num_scalar_prefetch=1,
+            grid=(seqs // 2, pairs // 4),
+            in_specs=[tile] * 8 + [pspec, inv, tile, tile, tile]
+            + [pl.BlockSpec(memory_space=pl.ANY)] * len(before),
+            out_specs=[tile] * 8 + [gpar] + [rel] * 3),
+        out_shape=[thin] * 8 + [jax.ShapeDtypeStruct((seqs * 8, width), f32)] + [thin] * 3,
+        input_output_aliases={14 + i: i for i in range(len(before))},
+        name="mixer_bwd",
+        **MIXER,
+    )(side, *args, par, *saved, gg, *before)
+
+
+def ffn_kernel(xc, xct, gf, wk, wv, hid, gpre, gx, *grads):
+    pre = jnp.maximum(mm(xc[...], wk[...]), 0.0)
+    h = (pre * pre).astype(bf16)
+    hid[...] = h
+    g = (mmt(gf[...], wv[...]) * (2.0 * pre)).astype(bf16)
+    gpre[...] = g
+    if grads:
+        d_val, d_key = grads
+        d_val[...] = tmm(h, gf[...]).astype(bf16)
+        d_key[...] = mm(xct[...], g).astype(bf16)
+    g = mmt(g, wk[...])
+
+    @pl.when(pl.program_id(0) == 0)
+    def _():
+        gx[...] = g
+
+    @pl.when(pl.program_id(0) > 0)
+    def _():
+        gx[...] += g
+
+
+FFN_BLOCK = 512
+
+
+def ffn_params(name):
+    return dict(
         compiler_params=pltpu.CompilerParams(vmem_limit_bytes=32 * 1024 * 1024),
-        cost_estimate=pl.CostEstimate(flops=20 * 10**9, bytes_accessed=10**7, transcendentals=10**6),
-        name="mixer_bwd",
-    )(*args, par, *saved, gg, *before)
+        cost_estimate=pl.CostEstimate(flops=5 * 10**9, bytes_accessed=10**7, transcendentals=0),
+        name=name)
+
+
+def ffn_half(xc, xct, gf, wk, wv, with_grads):
+    rows, width = xc.shape
+    units = wv.shape[0]
+    tall = pl.BlockSpec((rows, width), lambda j: (0, 0))
+    unit = pl.BlockSpec((rows, FFN_BLOCK), lambda j: (0, j))
+    down = pl.BlockSpec((FFN_BLOCK, width), lambda j: (j, 0))
+    across = pl.BlockSpec((width, FFN_BLOCK), lambda j: (0, j))
+    hidden = jax.ShapeDtypeStruct((rows, units), bf16)
+    more = with_grads * 1
+    return pl.pallas_call(
+        ffn_kernel,
+        grid=(units // FFN_BLOCK,),
+        in_specs=[tall, pl.BlockSpec((width, rows), lambda j: (0, 0)), tall, across, down],
+        out_specs=[unit, unit, tall] + [down, across] * more,
+        out_shape=[hidden, hidden, jax.ShapeDtypeStruct((rows, width), f32)]
+        + [jax.ShapeDtypeStruct((units, width), bf16), jax.ShapeDtypeStruct((width, units), bf16)] * more,
+        **ffn_params("ffn_half"),
+    )(xc, xct, gf, wk, wv)
+
+
+def grad_kernel(xct, gf, hid, gpre, val_got, key_got, d_val, d_key):
+    d_val[...] = (tmm(hid[...], gf[...]) + val_got[...].astype(f32)).astype(bf16)
+    d_key[...] = (mm(xct[...], gpre[...]) + key_got[...].astype(f32)).astype(bf16)
+
+
+def ffn_grads(xct, gf, hid, gpre, val_got, key_got):
+    width, rows = xct.shape
+    units = hid.shape[1]
+    unit = pl.BlockSpec((rows, FFN_BLOCK), lambda j: (0, j))
+    down = pl.BlockSpec((FFN_BLOCK, width), lambda j: (j, 0))
+    across = pl.BlockSpec((width, FFN_BLOCK), lambda j: (0, j))
+    return pl.pallas_call(
+        grad_kernel,
+        grid=(units // FFN_BLOCK,),
+        in_specs=[pl.BlockSpec((width, rows), lambda j: (0, 0)),
+                  pl.BlockSpec((rows, width), lambda j: (0, 0)), unit, unit, down, across],
+        out_specs=[down, across],
+        out_shape=[jax.ShapeDtypeStruct((units, width), bf16),
+                   jax.ShapeDtypeStruct((width, units + width // 2), bf16)],
+        **ffn_params("ffn_grads"),
+    )(xct, gf, hid, gpre, val_got, key_got)
+
+
+def conc_kernel(att, gated, got, before, d_key):
+    d_key[...] = (tmm(att[...], gated[...]) + got[...].astype(f32)).astype(bf16)
+
+
+def conc_grad(att, gated, got, d_key):
+    rows, width = att.shape
+    cols = gated.shape[1]
+    last = d_key.shape[1] // cols - 1
+    return pl.pallas_call(
+        conc_kernel,
+        grid=(1,),
+        in_specs=[pl.BlockSpec((rows, width), lambda j: (0, 0)),
+                  pl.BlockSpec((rows, cols), lambda j: (0, 0)),
+                  pl.BlockSpec((width, cols), lambda j: (0, 0)),
+                  pl.BlockSpec(memory_space=pl.ANY)],
+        out_specs=pl.BlockSpec((width, cols), lambda j: (0, last)),
+        out_shape=jax.ShapeDtypeStruct(d_key.shape, bf16),
+        input_output_aliases={3: 0},
+        **ffn_params("conc_grad"),
+    )(att, gated, got, d_key)
 
 
 def layer_norm(x, gain, bias):
@@ -300,39 +410,63 @@
     return lax.dynamic_index_in_dim(x, index, axis, keepdims=False)
 
 
-def other_way(g, step):
-    me = lax.axis_index("dp")
-    out = []
-    for part, (axis, bit) in zip(g, step):
-        mine = (me // bit) % 2
-        out.append(add(pick(part, mine, axis), swap(pick(part, 1 - mine, axis), bit)))
-    return out
-
-
-STEPS = (((2, 4), (3, 2)), ((2, 2), (2, 4)), ((1, 8), (1, 8)), ((0, 16), (0, 16)))
-
-
-def chip_sum_begin(g):
+BOTH = (((2, 4), (3, 2)), ((2, 2), (2, 4)), ((1, 8), (1, 8)), ((0, 16), (0, 16)))
+ONE = (((2, 4),), ((2, 2),), ((1, 8),), ((0, 16),))
+TAIL = (((2, 2), (1, 8)), ((1, 8), (0, 16)), ((0, 16), (0, 2)))
+
+
+def side_of(bit):
+    return (lax.axis_index("dp") // bit) % 2
+
+
+def sum_send(parts, step):
+    return [swap(pick(part, 1 - side_of(bit), axis), bit) for part, (axis, bit) in zip(parts, step)]
+
+
+def sum_take(parts, got, step):
+    return [add(pick(part, side_of(bit), axis), g) for part, g, (axis, bit) in zip(parts, got, step)]
+
+
+def two(g):
+    g = g.reshape(2, 2, 2, 2, g.shape[0] // 16, g.shape[1])
+    cut = g.shape[4] // 2
+    return [g[..., :cut, :], g[..., cut:, :]]
+
+
+def whole_sum(g):
+    n = lax.axis_size("dp")
+    groups = [list(range(c, n, 2)) for c in range(2)]
+    g = g.reshape(n // 2, g.shape[0] // (n // 2), g.shape[1])
+    return lax.psum_scatter(g, "dp", scatter_dimension=0, axis_index_groups=groups).astype(f32)
+
+
+def join(a, b, axis, bit):
+    mine = (lax.axis_index("dp") // bit) % 2
+    return jnp.where(mine == 0, jnp.stack([a, b], axis), jnp.stack([b, a], axis))
+
+
+def gather_send(parts, step):
+    if lax.axis_size("dp") != 32:
+        return parts
+    return [swap(p, bit) for p, (axis, bit) in zip(parts, BOTH[3 - step])]
+
+
+def gather_take(parts, got, step):
+    if lax.axis_size("dp") != 32:
+        return parts
+    return [join(p, g, axis, bit) for p, g, (axis, bit) in zip(parts, got, BOTH[3 - step])]
+
+
+def gather_step(parts, step):
+    return gather_take(parts, gather_send(parts, step), step)
+
+
+def chip_gather_end(parts):
     n = lax.axis_size("dp")
     if n != 32:
         groups = [list(range(c, n, 2)) for c in range(2)]
-        return lax.psum_scatter(g, "dp", scatter_dimension=0, axis_index_groups=groups)
-    cut = g.shape[1] // 2
-    return [p.reshape((2, 2, 2, 2) + p.shape[1:]) for p in (g[:, :cut], g[:, cut:])]
-
-
-def chip_sum_step(g, count=1):
-    if lax.axis_size("dp") != 32:
-        return g
-    for _ in range(count):
-        g = other_way(g, STEPS[6 - g[0].ndim])
-    return g
-
-
-def chip_sum_end(g):
-    if lax.axis_size("dp") != 32:
-        return g.astype(f32)
-    return jnp.concatenate(g, 0).astype(f32)
+        return [lax.all_gather(p, "dp", axis=0, axis_index_groups=groups, tiled=True) for p in parts]
+    return [p.reshape(-1, p.shape[-1]) for p in parts]
 
 
 def tie(*values):
@@ -341,11 +475,6 @@
 
 def on_core(keep, send):
     return (keep + swap(send, 1).astype(f32)).astype(bf16)
-
-
-def by_chip(g):
-    chips = lax.axis_size("dp") // 2
-    return g.reshape(chips, g.shape[0] // chips, g.shape[1])
 
 
 def trade_rows(h):
@@ -360,22 +489,68 @@
     micro, seqs, length, width = x_in.shape
     rows = micro * seqs * length
     shard = mix.shape[1]
+    core = lax.axis_index("dp") % 2
+    chips = lax.axis_size("dp") // 2
+    half = width // 2
     small = jnp.concatenate([mix, gains, biases, tying, extra[None], dwindle[None], squash], 0)
     n_small = small.shape[0]
-    pad = jnp.zeros((64 - n_small, shard), bf16)
-    pack = jnp.concatenate(
-        [jnp.swapaxes(ingoing, 1, 2)[i] for i in range(3)]
-        + [concluding.T, reducing, enlarging.T, jnp.concatenate([small, pad], 0).T], 1)
-    pack = lax.all_gather(pack, "dp", axis=0, tiled=True)
-    wk = lax.all_gather(ffn_key, "dp", axis=0, tiled=True)
-    wv = lax.all_gather(ffn_value, "dp", axis=0, tiled=True)
-    wi = [pack[:, i * width:(i + 1) * width] for i in range(3)]
-    wo = pack[:, 3 * width:4 * width]
-    base = 4 * width
-    w_in = pack[:, base:base + CUTS[4]]
-    w_out = pack[:, base + CUTS[4]:base + 2 * CUTS[4]]
-    small = pack[:, base + 2 * CUTS[4]:].T.astype(f32)
+    fill = jnp.zeros((80, shard), bf16)
+    low_a = jnp.concatenate([reducing, jnp.concatenate([small[:16], fill], 0).T], 1)
+    low_b = jnp.concatenate(
+        [enlarging, small[16:], jnp.zeros((16 - n_small + 16, shard), bf16), fill], 0).T
+    turned = jnp.swapaxes(ingoing, 1, 2)
+    q_halves = jnp.stack([jnp.concatenate([turned[0][:, c * half:(c + 1) * half],
+                                           turned[1][:, c * half:(c + 1) * half]], 1)
+                          for c in range(2)])
+    r_halves = jnp.stack([jnp.concatenate([turned[2][:, c * half:(c + 1) * half], low], 1)
+                          for c, low in enumerate((low_a, low_b))])
+    keys = ffn_key.reshape(shard, chips, 2, -1)
+    k_halves = jnp.stack([jnp.concatenate([keys[:, :, c].reshape(shard, -1),
+                                           concluding.T[:, c * half:(c + 1) * half]], 1)
+                          for c in range(2)])
+
+    def trade(halves):
+        own, sent = pick(halves, core, 0), pick(halves, 1 - core, 0)
+        return join(own, swap(sent, 1), 0, 1).reshape(2 * shard, -1)
+
+    mixer = [trade(q_halves), trade(r_halves)]
+    mixer = gather_step(gather_step(mixer, 0), 1)
+    ffn = [trade(k_halves), ffn_value]
+    mixer, ffn = tie(mixer, ffn)
+
+    def one_send(p, step, which):
+        axis, bit = BOTH[3 - step][which]
+        return swap(p, bit) if lax.axis_size("dp") == 32 else p
+
+    def one_take(p, got, step, which):
+        axis, bit = BOTH[3 - step][which]
+        return join(p, got, axis, bit) if lax.axis_size("dp") == 32 else p
+
+    got, k_got = tie(gather_send(mixer, 2), one_send(ffn[0], 0, 0))
+    mixer = gather_take(mixer, got, 2)
+    f_key, f_val = one_take(ffn[0], k_got, 0, 0), ffn[1]
+    got, k_got, v_got = tie(gather_send(mixer, 3), one_send(f_key, 1, 0), one_send(f_val, 0, 1))
+    f_key, f_val = one_take(f_key, k_got, 1, 0), one_take(f_val, v_got, 0, 1)
+    got, f_key, f_val = tie(got, f_key, f_val)
+    v_got, k_got = one_send(f_val, 1, 1), one_send(f_key, 2, 0)
+    mixer = chip_gather_end(gather_take(mixer, got, 3))
+    far = [swap(p, 1) for p in mixer]
+
+    def in_core_order(a, b, axis):
+        return jnp.where(core == 0, jnp.concatenate([a, b], axis), jnp.concatenate([b, a], axis))
+
+    wi = [(mixer[0][:, :half], far[0][:, :half]), (mixer[0][:, half:], far[0][:, half:]),
+          (mixer[1][:, :half], far[1][:, :half])]
+    low_a = jnp.where(core == 0, mixer[1][:, half:], far[1][:, half:])
+    low_b = jnp.where(core == 0, far[1][:, half:], mixer[1][:, half:])
+    w_in, w_out = low_a[:, :CUTS[4]], low_b[:, :CUTS[4]]
+    small = jnp.concatenate([low_a[:, CUTS[4]:CUTS[4] + 16], low_b[:, CUTS[4]:CUTS[4] + 16]], 1)
+    small = small.T.astype(f32)
     mix, gains, biases, tying = small[0:7], small[7:10], small[10:13], small[13:15]
+
+    def by_core(a):
+        return in_core_order(a[..., :half], a[..., half:], -1)
+
     par = jnp.concatenate([small[13:19], gains[1:2], biases[1:2]], 0)
 
     x = x_in.reshape(rows, width).astype(f32)
@@ -385,96 +560,169 @@
     g_out = valid * gout_in.reshape(rows, width).astype(f32)
     gf = g_out.astype(bf16)
 
-    xs, pull_front = jax.vjp(front, x, mix[:6], gains[0], biases[0])
+    xs, pull_front = jax.vjp(front, by_core(x), by_core(mix[:6]), by_core(gains[0]), by_core(biases[0]))
     xs = [z.astype(bf16) for z in xs]
-    proj = [mmt(xs[j], wi[i]) for i, j in enumerate((0, 2, 3))]
+    xs, v_got, gf = tie(xs, v_got, gf)
+    f_val = one_take(f_val, v_got, 1, 1)
+    v_got = one_send(f_val, 2, 1)
+    proj = [mmt(xs[j][:, :half], wi[i][0]) + mmt(xs[j][:, half:], wi[i][1])
+            for i, j in enumerate((0, 2, 3))]
+    w_in = in_core_order(w_in[:half], w_in[half:], 0)
     zs = [mm(xs[j], w_in[:, CUTS[i]:CUTS[i + 1]]) for i, j in enumerate(LOW_FROM)]
     ls, pull_low = jax.vjp(lowrank_act, *zs)
     ls = [z.astype(bf16) for z in ls]
     os_ = [mmt(ls[i], w_out[:, CUTS[i]:CUTS[i + 1]]) for i in range(4)]
     args = (*proj, *os_, first)
-    gated, *saved = mixer_fwd(args, par)
-    mixed = x + mmt(gated, wo)
+    done = mixer_fwd(args, par, 0, ())
+    done, k_got, v_got = tie(done, k_got, v_got)
+    ffn = [one_take(f_key, k_got, 2, 0), one_take(f_val, v_got, 2, 1)]
+    ffn_got = gather_send(ffn, 3)
+    for part in (1, 2, 3):
+        done = mixer_fwd(args, par, part, done)
+    done, ffn_got = tie(done, ffn_got)
+    ffn = chip_gather_end(gather_take(ffn, ffn_got, 3))
+    gated, *saved = done
+    wk, wv = ffn
+    wo = wk[:, -half:]
+    wo_far, wk, wv = tie(swap(wo, 1), wk, wv)
+    wk_far, wv_far = swap(wk, 1), swap(wv, 1)
+
+    def side(a, c):
+        return lax.dynamic_slice_in_dim(a, c * half, half, 1)
+
+    gated_near, gated_far = side(gated, core), side(gated, 1 - core)
+    mixed = x + mmt(gated_near, wo) + mmt(gated_far, wo_far)
     (xc,), pull_chan = jax.vjp(front, mixed, mix[6:7], gains[2], biases[2])
     xc = xc.astype(bf16)
-    pre = jax.nn.relu(mm(xc, wk))
-    hidden = (pre * pre).astype(bf16)
-    out = valid * (mixed + mm(hidden, wv))
-
-    core = lax.axis_index("dp") % 2
-    chips = lax.axis_size("dp") // 2
+    xct = xc.T
+    hidden, g_pre, g_xc = ffn_half(xc, xct, gf, wk, wv, False)
+    g_pre, wk_far, wv_far = tie(g_pre, wk_far, wv_far)
+    hidden_far, _, g_xc_far, val_far, key_far = ffn_half(xc, xct, gf, wk_far, wv_far, True)
+
     scale = 1.0 / math.sqrt(rows * lax.axis_size("dp"))
 
-    def cut(a, c):
-        return pick(a.reshape(rows, chips, 2, -1), c, 2).reshape(rows, -1)
-
-    def side(a, c):
-        return lax.dynamic_slice_in_dim(a, c * (width // 2), width // 2, 1)
-
-    d_value = on_core(tmm(cut(hidden, core), gf), tmm(cut(hidden, 1 - core), gf).astype(bf16))
-    d_value = chip_sum_begin(by_chip(d_value))
-    g_pre = (mmt(gf, wv) * (2.0 * pre)).astype(bf16)
-    d_value, g_pre = tie(d_value, g_pre)
-    d_key = on_core(tmm(xc, cut(g_pre, core)), tmm(xc, cut(g_pre, 1 - core)).astype(bf16))
-    g_mixed, g_mix_c, g_gain_c, g_bias_c = pull_chan((mmt(g_pre, wk),))
+    small_slice = lax.axis_size("dp") == 32
+    side_y = lax.axis_index("dp") // 4 % 2 if small_slice else jnp.int32(0)
+    side_y = side_y.reshape(1)
+    steps = BOTH if small_slice else ((), (), (), ())
+
+    def start(g):
+        return two(g) if small_slice else whole_sum(g)
+
+    def send(parts, step):
+        return sum_send(parts, steps[step]) if small_slice else []
+
+    def take(parts, got, step):
+        return sum_take(parts, got, steps[step]) if small_slice else parts
+
+    def finish(parts):
+        return jnp.concatenate(parts, 0).astype(f32) if small_slice else parts
+
+    val_got, key_got = swap(val_far, 1), swap(key_far, 1)
+    g_mixed, g_mix_c, g_gain_c, g_bias_c = pull_chan((g_xc + g_xc_far,))
     g_mixed = g_out + g_mixed
     g_att = g_mixed.astype(bf16)
-    d_conc = on_core(tmm(g_att, side(gated, core)), tmm(g_att, side(gated, 1 - core)).astype(bf16))
-    d_value = chip_sum_step(d_value)
-    d_key = chip_sum_begin(by_chip(jnp.concatenate([d_key, d_conc], 1)))
-    gg = mm(g_att, wo)
-    gg, d_key, d_value = tie(gg, d_key, d_value)
-    grads = mixer_bwd(args, par, saved, gg, 0, ())
-    d_value = chip_sum_step(d_value)
-    d_key = chip_sum_step(d_key)
-    grads, d_key, d_value = tie(grads, d_key, d_value)
-    grads = mixer_bwd(args, par, saved, gg, 1, grads)
-    d_value = chip_sum_step(d_value)
-    d_key = chip_sum_step(d_key)
-    grads, d_key, d_value = tie(grads, d_key, d_value)
-    d_value = chip_sum_end(chip_sum_step(d_value))
-    d_key = chip_sum_end(chip_sum_step(d_key, 2))
+    conc_got = swap(tmm(g_att, gated_far).astype(bf16), 1)
+    gg = in_core_order(mm(g_att, wo), mm(g_att, wo_far), 1)
+    gg, val_got, key_got, conc_got = tie(gg, val_got, key_got, conc_got)
+    d_value, d_key = ffn_grads(xct, gf, hidden, g_pre, val_got, key_got)
+    d_key = conc_grad(g_att, gated_near, conc_got, d_key)
+    d_value, d_key = start(d_value), start(d_key)
+    v_got, k_got = send(d_value, 0), send(d_key, 0)
+    gg, d_value, d_key = tie(gg, d_value, d_key)
+    grads = mixer_bwd(args, par, saved, gg, side_y, 0, ())
+    grads, v_got = tie(grads, v_got)
+    d_value = take(d_value, v_got, 0)
+    v_got = send(d_value, 1)
+    grads = mixer_bwd(args, par, saved, gg, side_y, 1, grads)
+
+    def proj_part(near, keep):
+        cols = slice(0, half) if near else slice(half, width)
+        outs = slice(half, width) if keep else slice(0, half)
+        return jnp.concatenate(
+            [tmm(grads[9 + i][:, outs], xs[j][:, cols]) for i, j in enumerate((0, 2, 3))], 1)
+
+    away = on_core(proj_part(True, False), proj_part(False, False).astype(bf16))
+    grads = mixer_bwd(args, par, saved, gg, side_y, 2, grads)
+    grads, v_got, k_got, away = tie(grads, v_got, k_got, away)
+    d_value, d_key = take(d_value, v_got, 1), take(d_key, k_got, 0)
+    v_got, k_got = send(d_value, 2), send(d_key, 1)
+    if small_slice:
+        away = swap(away, 4)
+    grads = mixer_bwd(args, par, saved, gg, side_y, 3, grads)
+    grads, v_got, k_got = tie(grads, v_got, k_got)
+    d_value, d_key = take(d_value, v_got, 2), take(d_key, k_got, 1)
+    v_got, k_got = send(d_value, 3), send(d_key, 2)
+    home = proj_part(True, True) + swap(proj_part(False, True).astype(bf16), 1).astype(f32)
     gp = jnp.sum(grads[8].reshape(-1, 8, width), 0)
     g_proj, g_os, g_first = grads[:3], grads[3:7], grads[7]
     g_ls = tuple(mm(g_os[i], w_out[:, CUTS[i]:CUTS[i + 1]]) for i in range(4))
     g_zs = [z.astype(bf16) for z in pull_low(g_ls)]
     back = [mmt(g_zs[i], w_in[:, CUTS[i]:CUTS[i + 1]]) for i in range(4)]
-    g_xs = (mm(g_proj[0], wi[0]), back[0], mm(g_proj[1], wi[1]),
-            mm(g_proj[2], wi[2]) + back[2], back[1], back[3])
+
+    def down(i):
+        return jnp.concatenate([mm(g_proj[i], wi[i][0]), mm(g_proj[i], wi[i][1])], 1)
+
+    g_xs = (down(0), back[0], down(1), down(2) + back[2], back[1], back[3])
+    low_a = jnp.concatenate([tmm(xs[j], g_zs[i]) for i, j in enumerate(LOW_FROM)], 1)
+    low_a = in_core_order(low_a[:half], low_a[half:], 0)
+    low_b = jnp.concatenate([tmm(g_os[i], ls[i]) for i in range(4)], 1)
+    d_low = on_core(jnp.where(core == 0, low_a, low_b),
+                    jnp.where(core == 0, low_b, low_a).astype(bf16))
+    if small_slice:
+        d_low = [d_low.reshape(2, 2, 2, 2, 64, -1)]
+        l_got = sum_send(d_low, ONE[0])
+    if small_slice:
+        g_xs, away, home, v_got, k_got, l_got = tie(g_xs, away, home, v_got, k_got, l_got)
+        d_proj = (home + away.astype(f32)).astype(bf16)
+        d_proj = d_proj.reshape(2, 2, 2, 64, d_proj.shape[1])
+        d_proj = [d_proj[..., :32, :], d_proj[..., 32:, :]]
+        d_key, d_low = take(d_key, k_got, 2), sum_take(d_low, l_got, ONE[0])
+        p_got, l_got, k_got = sum_send(d_proj, TAIL[0]), sum_send(d_low, ONE[1]), send(d_key, 3)
     g_x, g_mix_t, g_gain_t, g_bias_t = pull_front(g_xs)
-    g_x = g_mixed + g_x
-    g_small = jnp.concatenate(
+    g_x = g_mixed + by_core(g_x)
+    g_mix_t, g_gain_t, g_bias_t = by_core(g_mix_t), by_core(g_gain_t), by_core(g_bias_t)
+    d_small = jnp.concatenate(
         [g_mix_t, g_mix_c, g_gain_t[None], gp[6:7], g_gain_c[None], g_bias_t[None], gp[7:8],
-         g_bias_c[None], gp[0:6], jnp.zeros((13, width), f32)], 0).T
-    fill = jnp.zeros((width, 80), f32)
-    low_a = jnp.concatenate([tmm(xs[j], g_zs[i]) for i, j in enumerate(LOW_FROM)]
-                            + [g_small[:, :16], fill], 1)
-    low_b = jnp.concatenate([tmm(g_os[i], ls[i]) for i in range(4)] + [g_small[:, 16:], fill], 1)
-
-    def mixer_half(c):
-        return jnp.concatenate(
-            [tmm(g_proj[i], side(xs[j], c)) for i, j in enumerate((0, 2, 3))]
-            + [jnp.where(c == 0, low_a, low_b)], 1)
-
-    d_mix = on_core(mixer_half(core), mixer_half(1 - core).astype(bf16))
-    d_mix = chip_sum_end(chip_sum_step(chip_sum_begin(by_chip(d_mix)), 4))
-    half_a, half_b = trade_rows(d_mix * scale)
+         g_bias_c[None], gp[0:6], jnp.zeros((5, width), f32)], 0)
+    if small_slice:
+        d_small, p_got, l_got, hidden, hidden_far = tie(d_small, p_got, l_got, hidden, hidden_far)
+        d_proj, d_low = sum_take(d_proj, p_got, TAIL[0]), sum_take(d_low, l_got, ONE[1])
+        p_got, l_got = sum_send(d_proj, TAIL[1]), sum_send(d_low, ONE[2])
+        for bit in (1, 2, 4, 8, 16):
+            d_small = d_small + swap(d_small, bit)
+        out = mixed + mm(hidden, wv)
+        out, p_got, l_got = tie(out, p_got, l_got)
+        d_proj, d_low = sum_take(d_proj, p_got, TAIL[1]), sum_take(d_low, l_got, ONE[2])
+        p_got, l_got = sum_send(d_proj, TAIL[2]), sum_send(d_low, ONE[3])
+        out = valid * (out + mm(hidden_far, wv_far))
+        d_proj = finish(sum_take(d_proj, p_got, TAIL[2]))
+        d_low = finish(sum_take(d_low, l_got, ONE[3]))
+    else:
+        home = home.astype(bf16).reshape(width // 256, 1, 128, -1)
+        d_proj = whole_sum(jnp.concatenate([home, away.reshape(home.shape)], 1).reshape(width, -1))
+        d_low = whole_sum(d_low)
+        d_small = lax.psum(d_small, "dp")
+        out = valid * (mixed + mm(hidden, wv) + mm(hidden_far, wv_far))
+    d_key = finish(take(d_key, k_got, 3))
+    d_value = finish(take(d_value, v_got, 3))
+    d_small = scale * lax.dynamic_slice_in_dim(d_small, lax.axis_index("dp") * shard, shard, 1)
+    half_a, half_b = trade_rows(d_proj * scale)
+    low_a, low_b = trade_rows(d_low * scale)
     key_a, key_b = trade_rows(d_key * scale)
-    hw = width // 2
+    hw = half
     wide = [jnp.concatenate([half_a[:, i * hw:(i + 1) * hw], half_b[:, i * hw:(i + 1) * hw]], 1)
             for i in range(3)]
     d_in = jnp.stack([w.T for w in wide])
-    low_a, low_b = half_a[:, 3 * hw:], half_b[:, 3 * hw:]
     d_conc = jnp.concatenate([key_a[:, -hw:], key_b[:, -hw:]], 1).T
     key_a, key_b = key_a[:, :-hw], key_b[:, :-hw]
-    d_small = jnp.concatenate([low_a[:, CUTS[4]:CUTS[4] + 16], low_b[:, CUTS[4]:CUTS[4] + 16]], 1).T
     d_key = jnp.stack([key_a.reshape(shard, chips, -1), key_b.reshape(shard, chips, -1)], 2)
     d_key = d_key.reshape(shard, -1)
     return (
         out.astype(bf16).reshape(x_in.shape), g_x.astype(bf16).reshape(x_in.shape),
         g_first.reshape(x_in.shape), d_small[0:7], d_small[7:10], d_small[10:13],
         d_small[13:15], d_small[15], d_small[16], d_small[17:19],
-        low_a[:, :CUTS[4]], low_b[:, :CUTS[4]].T, d_in, d_conc, d_key, d_value * scale)
+        low_a, low_b.T, d_in, d_conc, d_key, d_value * scale)
 
 
 def solution(mesh):

time: 584 us -> 469 us (0.80)
  waiting for transfers between devices: 221 us -> 112 us
  matrix products: 84.9 us -> 36.3 us
  local copies, waits for them, and re-layouts: 100 us -> 55.1 us
  starting transfers between devices: 25.3 us -> 65.5 us
  other arithmetic: 32.9 us -> 67.9 us
  Pallas kernels: 97.1 us -> 122 us
  between operations: 15.8 us -> 4.17 us
    all_gather x3 -> x0, waiting for transfers between devices: 129 us -> none  [the longest x1 83 us: on_device(): pack = lax.all_gather(pack, 'dp', axis=0, tiled=True)]
    dot_general x48 -> x55, matrix products: 84.9 us -> 36.3 us  [dn(): lax.dot_general(x, y, (((cx,), (cy,)), ((), ())), preferred_element_type=...]
    ppermute x30 -> x65, starting transfers between devices: 25.2 us -> 65.5 us  [swap(): return lax.ppermute(x, 'dp', [(i, i ^ bit) for i in range(n)])]
    unnamed x179 -> x293, local copies, waits for them, and re-layouts: 45.8 us -> 15.4 us
    pallas_call x3 -> x12, Pallas kernels: 97.1 us -> 122 us  [the longest x4 51.9 us: mixer_fwd(): pl.pallas_call(body, grid=(seqs // 2, pairs // 4), in_specs=[tile] * 8 +...]
    ppermute x30 -> x65, waiting for transfers between devices: 89.7 us -> 112 us  [swap(): return lax.ppermute(x, 'dp', [(i, i ^ bit) for i in range(n)])]
    select_n x1 -> x31, other arithmetic: 0.26 us -> 16.8 us  [the longest x26 14 us: join(): jnp.where(mine == 0, jnp.stack([a, b], axis), jnp.stack([b, a], axis))]
    dynamic_slice x4 -> x1, local copies, waits for them, and re-layouts: 17.3 us -> 0.8 us  [pick(): return lax.dynamic_index_in_dim(x, index, axis, keepdims=False)]
  transfers between devices with their start and end apart: 33 -> 65, of which waited for: 14 -> 27; matrix products, arithmetic and copies ran while one was open for 25% -> 26% of each run, Pallas kernels for 17% -> 22%
where the time goes in v2:
time: 469 us; the launch traced here: 462 us
  Pallas kernels  122 us (26%)
  waiting for transfers between devices  112 us (24%)
  other arithmetic  67.9 us (14%)
  starting transfers between devices  65.5 us (14%)
  local copies, waits for them, and re-layouts  55.1 us (12%)
  matrix products  36.3 us (8%)
    ppermute x65, waiting for transfers between devices, swap(): return lax.ppermute(x, 'dp', [(i, i ^ bit) for i in range(n)])  112 us
    ppermute x65, starting transfers between devices, swap(): return lax.ppermute(x, 'dp', [(i, i ^ bit) for i in range(n)])  65.5 us
    pallas_call x4, Pallas kernels, mixer_fwd(): pl.pallas_call(body, grid=(seqs // 2, pairs // 4), in_specs=[tile] * 8 +...  51.9 us
    pallas_call x4, Pallas kernels, mixer_bwd(): pl.pallas_call(body, grid_spec=pltpu.PrefetchScalarGridSpec(num_scalar_pr...  44.7 us
    dot_general x55, matrix products, dn(): lax.dot_general(x, y, (((cx,), (cy,)), ((), ())), preferred_element_type=...  36.3 us
    pallas_call x2, Pallas kernels, ffn_half(): pl.pallas_call(ffn_kernel, grid=(units // FFN_BLOCK,), in_specs=[tall, pl...  17.6 us
    convert_element_type x24, other arithmetic, add(): return (a.astype(f32) + b.astype(f32)).astype(bf16)  15.5 us
    unnamed x293, local copies, waits for them, and re-layouts  15.4 us
  transfers between devices with their start and end apart: 65, of which 27 were waited for; matrix products, arithmetic and copies ran while one was open for 26% of the time, Pallas kernels for 22%

profile of v2, /device:TPU:0, one launch (start us, length us, event | category | flops | bytes accessed | tf_op | source)
XLA Modules:
  0.0 462.5 jit_solution(1584208268579752096)
XLA Ops:
  7.5 3.8 collective-permute-start.4
  11.9 8.7 %collective-permute-done.4 = bf16[64,896]{1,0:T(8,128)(2,1)S(1)} collective-permute-done((bf16[64,896]{1,0:T(8,128)(2,1)S(1)}, bf16[64,896]{1,0:T(8,128)(2,1)S(1)}, u32[]{:S(2)}, u32[]{:S(2)}) %collective-permute-start.4) | collective-permute-done | bytes 114720 | tf_op jit(solution)/shard_map/ppermute | solution.py:402
  23.9 5.3 %collective-permute-done.5 = bf16[2,64,896]{2,1,0:T(8,128)(2,1)S(1)} collective-permute-done((bf16[2,64,896]{2,1,0:T(8,128)(2,1)S(1)}, bf16[2,64,896]{2,1,0:T(8,128)(2,1)S(1)}, u32[]{:S(2)}, u32[]{:S(2)}) %collective-permute-start.5) | collective-permute-done | bytes 229408 | tf_op jit(solution)/shard_map/ppermute | solution.py:402
  29.3 4.3 collective-permute-done.2
  39.3 13.5 %collective-permute-done.9 = bf16[64,2560]{1,0:T(8,128)(2,1)S(1)} collective-permute-done((bf16[64,2560]{1,0:T(8,128)(2,1)S(1)}, bf16[64,2560]{1,0:T(8,128)(2,1)S(1)}, u32[]{:S(2)}, u32[]{:S(2)}) %collective-permute-start.9) | collective-permute-done | bytes 327712 | tf_op jit(solution)/shard_map/ppermute | solution.py:402
  61.3 14.4 %collective-permute-done.13 = bf16[128,1024]{1,0:T(8,128)(2,1)S(1)} collective-permute-done((bf16[128,1024]{1,0:T(8,128)(2,1)S(1)}, bf16[128,1024]{1,0:T(8,128)(2,1)S(1)}, u32[]{:S(2)}, u32[]{:S(2)}) %collective-permute-start.13) | collective-permute-done | bytes 262176 | tf_op jit(solution)/shard_map/ppermute | solution.py:402
  99.0 4.4 collective-permute-done.15
  112.3 13.0 %mixer_fwd.4 = (bf16[256,1024]{1,0:T(8,128)(2,1)S(1)}, f32[2048,256]{1,0:T(8,128)S(1)}, f32[256,1024]{1,0:T(8,128)S(1)}, f32[256,1024]{1,0:T(8,128)S(1)}) custom-call(f32[256,1024]{1,0:T(8,128)S(1)} %convolution_add_fusion.5.refs_0_.refs_1_, f32[256,1024]{1,0:T(8,128)S(1)} %convolution_add_fusion.4.refs_1_.refs_2_, ...), custom_call_target="tpu_custom_call" | custom-call | flops 10000000000 | bytes 10000000 | tf_op jit(solution)/shard_map/mixer_fwd/pallas_call | solution.py:225
  132.3 13.0 %mixer_fwd.5 = (bf16[256,1024]{1,0:T(8,128)(2,1)S(1)}, f32[2048,256]{1,0:T(8,128)S(1)}, f32[256,1024]{1,0:T(8,128)S(1)}, f32[256,1024]{1,0:T(8,128)S(1)}) custom-call(f32[256,1024]{1,0:T(8,128)S(1)} %convolution_add_fusion.5.refs_0_.refs_1_, ...), custom_call_target="tpu_custom_call", output_to_operand_aliasing={{0}: (9, {}), {1}: (10, {}), {2}: (11, {}), {3}: (12, {})} | custom-call | flops 10000000000 | bytes 10000000 | tf_op jit(solution)/shard_map/mixer_fwd/pallas_call | solution.py:225
  145.5 13.0 %mixer_fwd.6 = (bf16[256,1024]{1,0:T(8,128)(2,1)S(1)}, f32[2048,256]{1,0:T(8,128)S(1)}, f32[256,1024]{1,0:T(8,128)S(1)}, f32[256,1024]{1,0:T(8,128)S(1)}) custom-call(f32[256,1024]{1,0:T(8,128)S(1)} %convolution_add_fusion.5.refs_0_.refs_1_, ...), custom_call_target="tpu_custom_call", output_to_operand_aliasing={{0}: (9, {}), {1}: (10, {}), {2}: (11, {}), {3}: (12, {})} | custom-call | flops 10000000000 | bytes 10000000 | tf_op jit(solution)/shard_map/mixer_fwd/pallas_call | solution.py:225
  158.6 13.0 %mixer_fwd.7 = (bf16[256,1024]{1,0:T(8,128)(2,1)S(1)}, f32[2048,256]{1,0:T(8,128)S(1)}, f32[256,1024]{1,0:T(8,128)S(1)}, f32[256,1024]{1,0:T(8,128)S(1)}) custom-call(f32[256,1024]{1,0:T(8,128)S(1)} %convolution_add_fusion.5.refs_0_.refs_1_, ...), custom_call_target="tpu_custom_call", output_to_operand_aliasing={{0}: (9, {}), {1}: (10, {}), {2}: (11, {}), {3}: (12, {})} | custom-call | flops 10000000000 | bytes 10000000 | tf_op jit(solution)/shard_map/mixer_fwd/pallas_call | solution.py:225
  175.3 13.1 %collective-permute-done.19 = bf16[2,2,2,64,2560]{4,3,2,1,0:T(8,128)(2,1)S(1)} collective-permute-done((bf16[2,2,2,64,2560]{4,3,2,1,0:T(8,128)(2,1)S(1)}, bf16[2,2,2,64,2560]{4,3,2,1,0:T(8,128)(2,1)S(1)}, u32[]{:S(2)}, u32[]{:S(2)}) %collective-permute-start.19) | collective-permute-done | bytes 2621472 | tf_op jit(solution)/shard_map/ppermute | solution.py:402
  205.5 6.7 %ffn_half.2 = (bf16[256,2048]{1,0:T(8,128)(2,1)S(1)}, bf16[256,2048]{1,0:T(8,128)(2,1)S(1)}, f32[256,1024]{1,0:T(8,128)S(1)}) custom-call(bf16[256,1024]{1,0:T(8,128)(2,1)S(1)} %add_convert_fusion.2.xc, bf16[1024,256]{1,0:T(8,128)(2,1)S(1)} %copy-done.12, bf16[256,1024]{1,0:T(8,128)(2,1)S(1)} %copy-done.10, bf16[1024,2560]{1,0:T(8,128)(2,1)} %bitcast.91.wk, ...), custom_call_target="tpu_custom_call" | custom-call | flops 5000000000 | bytes 10000000 | tf_op jit(solution)/shard_map/ffn_half/pallas_call | solution.py:311
  213.2 10.9 %ffn_half.3 = (bf16[256,2048]{1,0:T(8,128)(2,1)S(1)}, bf16[256,2048]{1,0:T(8,128)(2,1)}, f32[256,1024]{1,0:T(8,128)S(1)}, bf16[2048,1024]{1,0:T(8,128)(2,1)}, bf16[1024,2048]{1,0:T(8,128)(2,1)}) custom-call(bf16[256,1024]{1,0:T(8,128)(2,1)S(1)} %add_convert_fusion.2.xc, bf16[1024,256]{1,0:T(8,128)(2,1)S(1)} %copy-done.12, bf16[256,1024]{1,0:T(8,128)(2,1)S(1)} %copy-done.10, ...), custom_call_target="tpu_custom_call" | custom-call | flops 5000000000 | bytes 10000000 | tf_op jit(solution)/shard_map/ffn_half/pallas_call | solution.py:311
  235.0 4.3 collective-permute-done.26.got
  239.3 5.8 %ffn_grads.1 = (bf16[2048,1024]{1,0:T(8,128)(2,1)S(1)}, bf16[1024,2560]{1,0:T(8,128)(2,1)S(1)}) custom-call(bf16[1024,256]{1,0:T(8,128)(2,1)S(1)} %copy-done.13, bf16[256,1024]{1,0:T(8,128)(2,1)S(1)} %copy-done.11, bf16[256,2048]{1,0:T(8,128)(2,1)S(1)} %copy-done.17, bf16[256,2048]{1,0:T(8,128)(2,1)S(1)} %copy-done.22, ...), custom_call_target="tpu_custom_call" | custom-call | flops 5000000000 | bytes 10000000 | tf_op jit(solution)/shard_map/ffn_grads/pallas_call | solution.py:333
  256.2 11.4 %mixer_bwd.4 = (bf16[256,1024]{1,0:T(8,128)(2,1)S(1)}, bf16[256,1024]{1,0:T(8,128)(2,1)S(1)}, bf16[256,1024]{1,0:T(8,128)(2,1)S(1)}, bf16[256,1024]{1,0:T(8,128)...) custom-call(s32[1]{0:T(128)} %bitcast.96.refs_0_, ...), custom_call_target="tpu_custom_call" | custom-call | flops 10000000000 | bytes 10000000 | tf_op jit(solution)/shard_map/mixer_bwd/pallas_call | solution.py:256
  267.5 6.7 %collective-permute-done.27 = bf16[2,2,2,64,1024]{4,3,0,1,2:T(8,128)(2,1)S(1)} collective-permute-done((bf16[2,2,2,64,1024]{4,3,0,1,2:T(8,128)(2,1)S(1)}, bf16[2,2,2,64,1024]{4,3,0,1,2:T(8,128)(2,1)S(1)}, u32[]{:S(2)}, u32[]{:S(2)}) %collective-permute-start.27) | collective-permute-done | bytes 1048608 | tf_op jit(solution)/shard_map/ppermute | solution.py:402
  275.4 10.9 %mixer_bwd.5 = (bf16[256,1024]{1,0:T(8,128)(2,1)S(1)}, bf16[256,1024]{1,0:T(8,128)(2,1)S(1)}, bf16[256,1024]{1,0:T(8,128)(2,1)S(1)}, bf16[256,1024]{1,0:T(8,128)...) custom-call(s32[1]{0:T(128)} %bitcast.96.refs_0_, ...), custom_call_target="tpu_custom_call", output_to_operand_aliasing={{0}: (14, {}), {1}: (15, {}), {2}: (16, {}), {3}: (17, {}),... | custom-call | flops 10000000000 | bytes 10000000 | tf_op jit(solution)/shard_map/mixer_bwd/pallas_call | solution.py:256
  295.4 11.2 %mixer_bwd.6 = (bf16[256,1024]{1,0:T(8,128)(2,1)S(1)}, bf16[256,1024]{1,0:T(8,128)(2,1)S(1)}, bf16[256,1024]{1,0:T(8,128)(2,1)S(1)}, bf16[256,1024]{1,0:T(8,128)...) custom-call(s32[1]{0:T(128)} %bitcast.96.refs_0_, ...), custom_call_target="tpu_custom_call", output_to_operand_aliasing={{0}: (14, {}), {1}: (15, {}), {2}: (16, {}), {3}: (17, {}),... | custom-call | flops 10000000000 | bytes 10000000 | tf_op jit(solution)/shard_map/mixer_bwd/pallas_call | solution.py:256
  322.5 11.1 %mixer_bwd.7 = (bf16[256,1024]{1,0:T(8,128)(2,1)S(1)}, bf16[256,1024]{1,0:T(8,128)(2,1)S(1)}, bf16[256,1024]{1,0:T(8,128)(2,1)S(1)}, bf16[256,1024]{1,0:T(8,128)...) custom-call(s32[1]{0:T(128)} %bitcast.96.refs_0_, ...), custom_call_target="tpu_custom_call", output_to_operand_aliasing={{0}: (14, {}), {1}: (15, {}), {2}: (16, {}), {3}: (17, {}),... | custom-call | flops 10000000000 | bytes 10000000 | tf_op jit(solution)/shard_map/mixer_bwd/pallas_call | solution.py:256
  373.0 4.8 %collective-permute-done.40 = bf16[64,1024]{1,0:T(8,128)(2,1)S(1)} collective-permute-done((bf16[64,1024]{1,0:T(8,128)(2,1)}, bf16[64,1024]{1,0:T(8,128)(2,1)S(1)}, u32[]{:S(2)}, u32[]{:S(2)}) %collective-permute-start.40) | collective-permute-done | bytes 131104 | tf_op jit(solution)/shard_map/ppermute | solution.py:402
  396.8 4.3 collective-permute-start.47
  455.5 4.2 collective-permute-done.56
  (685 shorter events, 246.5 us)
Async XLA Ops:
  33.6 19.2 %collective-permute-start.7 = (bf16[2,2,64,1024]{3,2,1,0:T(8,128)(2,1)S(1)}, bf16[2,2,64,1024]{3,2,1,0:T(8,128)(2,1)S(1)}, u32[]{:S(2)}, u32[]{:S(2)}) collective-permute-start(bf16[2,2,64,1024]{3,2,1,0:T(8,128)(2,1)S(1)} %maximum_select_fusion.20), channel_id=1, source_target_pairs={{0,2},{1,3},{2,0},{3,1},{4,6},{5,7},{6,4},{7,5},{8,10},{9,11},{10,... | collective-permute-start | bytes 1572872 | tf_op jit(solution)/shard_map/ppermute | solution.py:402
  54.3 22.2 %collective-permute-start.11 = (bf16[2,2,2,64,896]{4,3,1,0,2:T(8,128)(2,1)S(1)}, bf16[2,2,2,64,896]{4,3,1,0,2:T(8,128)(2,1)S(1)}, u32[]{:S(2)}, u32[]{:S(2)}) collective-permute-start(bf16[2,2,2,64,896]{4,3,1,0,2:T(8,128)(2,1)S(1)} %maximum_select_fusion.17), channel_id=1, source_target_pairs={{0,2},{1,3},{2,0},{3,1},{4,6},{5,7},{6,4},{7,5},{8,10},{9,11},{10,... | collective-permute-start | bytes 2752520 | tf_op jit(solution)/shard_map/ppermute | solution.py:402
  55.0 23.9 %collective-permute-start.10 = (bf16[2,2,2,64,1024]{4,3,2,1,0:T(8,128)(2,1)S(1)}, bf16[2,2,2,64,1024]{4,3,2,1,0:T(8,128)(2,1)}, u32[]{:S(2)}, u32[]{:S(2)}) collective-permute-start(bf16[2,2,2,64,1024]{4,3,2,1,0:T(8,128)(2,1)S(1)} %maximum_select_fusion.11), channel_id=1, source_target_pairs={{0,4},{1,5},{2,6},{3,7},{4,0},{5,1},{6,2},{7,3},{8,12},{9,13},{10,... | collective-permute-start | bytes 3145736 | tf_op jit(solution)/shard_map/ppermute | solution.py:402
  55.7 20.8 %collective-permute-start.12 = (bf16[2,64,2560]{2,1,0:T(8,128)(2,1)S(1)}, bf16[2,64,2560]{2,1,0:T(8,128)(2,1)S(1)}, u32[]{:S(2)}, u32[]{:S(2)}) collective-permute-start(bf16[2,64,2560]{2,1,0:T(8,128)(2,1)S(1)} %maximum_select_fusion.18), channel_id=1, source_target_pairs={{0,8},{1,9},{2,10},{3,11},{4,12},{5,13},{6,14},{7,15},{8,0},{9,1},... | collective-permute-start | bytes 1966088 | tf_op jit(solution)/shard_map/ppermute | solution.py:402
  56.5 19.2 %collective-permute-start.13 = (bf16[128,1024]{1,0:T(8,128)(2,1)S(1)}, bf16[128,1024]{1,0:T(8,128)(2,1)S(1)}, u32[]{:S(2)}, u32[]{:S(2)}) collective-permute-start(bf16[128,1024]{1,0:T(8,128)(2,1)S(1)} %copy-done.105), channel_id=1, source_target_pairs={{0,16},{1,17},{2,18},{3,19},{4,20},{5,21},{6,22},{7,23},{8,24},{9,... | collective-permute-start | bytes 786440 | tf_op jit(solution)/shard_map/ppermute | solution.py:402
  93.1 32.2 %collective-permute-start.17 = (bf16[2,2,64,2560]{3,2,1,0:T(8,128)(2,1)S(1)}, bf16[2,2,64,2560]{3,2,1,0:T(8,128)(2,1)S(1)}, u32[]{:S(2)}, u32[]{:S(2)}) collective-permute-start(bf16[2,2,64,2560]{3,2,1,0:T(8,128)(2,1)S(1)} %copy-done.40), channel_id=1, source_target_pairs={{0,2},{1,3},{2,0},{3,1},{4,6},{5,7},{6,4},{7,5},{8,10},{9,11},{10,... | collective-permute-start | bytes 3932168 | tf_op jit(solution)/shard_map/ppermute | solution.py:402
  103.6 24.9 %collective-permute-start.18 = (bf16[2,2,128,1024]{3,2,0,1:T(8,128)(2,1)S(1)}, bf16[2,2,128,1024]{3,2,0,1:T(8,128)(2,1)S(1)}, u32[]{:S(2)}, u32[]{:S(2)}) collective-permute-start(bf16[2,2,128,1024]{3,2,0,1:T(8,128)(2,1)S(1)} %maximum_select_fusion.12), channel_id=1, source_target_pairs={{0,4},{1,5},{2,6},{3,7},{4,0},{5,1},{6,2},{7,3},{8,12},{9,13},{10,... | collective-permute-start | bytes 3145736 | tf_op jit(solution)/shard_map/ppermute | solution.py:402
  128.8 46.5 %collective-permute-start.20 = (bf16[2,2,2,128,1024]{4,3,0,1,2:T(8,128)(2,1)S(1)}, bf16[2,2,2,128,1024]{4,3,0,1,2:T(8,128)(2,1)S(1)}, u32[]{:S(2)}, u32[]{:S(2)}) collective-permute-start(bf16[2,2,2,128,1024]{4,3,0,1,2:T(8,128)(2,1)S(1)} %maximum_select_fusion.4), channel_id=1, source_target_pairs={{0,2},{1,3},{2,0},{3,1},{4,6},{5,7},{6,4},{7,5},{8,10},{9,11},{10,... | collective-permute-start | bytes 6291464 | tf_op jit(solution)/shard_map/ppermute | solution.py:402
  131.0 57.4 %collective-permute-start.19 = (bf16[2,2,2,64,2560]{4,3,2,1,0:T(8,128)(2,1)S(1)}, bf16[2,2,2,64,2560]{4,3,2,1,0:T(8,128)(2,1)S(1)}, u32[]{:S(2)}, u32[]{:S(2)}) collective-permute-start(bf16[2,2,2,64,2560]{4,3,2,1,0:T(8,128)(2,1)S(1)} %maximum_select_fusion.2), channel_id=1, source_target_pairs={{0,4},{1,5},{2,6},{3,7},{4,0},{5,1},{6,2},{7,3},{8,12},{9,13},{10,... | collective-permute-start | bytes 7864328 | tf_op jit(solution)/shard_map/ppermute | solution.py:402
  248.2 26.1 %collective-permute-start.27 = (bf16[2,2,2,64,1024]{4,3,0,1,2:T(8,128)(2,1)S(1)}, bf16[2,2,2,64,1024]{4,3,0,1,2:T(8,128)(2,1)S(1)}, u32[]{:S(2)}, u32[]{:S(2)}) collective-permute-start(bf16[2,2,2,64,1024]{4,3,0,1,2:T(8,128)(2,1)S(1)} %dynamic-slice_bitcast_fusion.3), channel_id=1, source_target_pairs={{0,4},{1,5},{2,6},{3,7},{4,0},{5,1},{6,2},{7,3},{8,12},{9,13},{10,... | collective-permute-start | bytes 3145736 | tf_op jit(solution)/shard_map/ppermute | solution.py:402
  249.2 26.2 %collective-permute-start.28 = (bf16[2,2,2,64,1024]{4,3,0,1,2:T(8,128)(2,1)S(1)}, bf16[2,2,2,64,1024]{4,3,0,1,2:T(8,128)(2,1)}, u32[]{:S(2)}, u32[]{:S(2)}) collective-permute-start(bf16[2,2,2,64,1024]{4,3,0,1,2:T(8,128)(2,1)S(1)} %dynamic-slice_bitcast_fusion.2), channel_id=1, source_target_pairs={{0,2},{1,3},{2,0},{3,1},{4,6},{5,7},{6,4},{7,5},{8,10},{9,11},{10,... | collective-permute-start | bytes 3145736 | tf_op jit(solution)/shard_map/ppermute | solution.py:402
  253.0 56.9 %collective-permute-start.31 = (bf16[2,2,2,32,2560]{4,3,0,1,2:T(8,128)(2,1)}, bf16[2,2,2,32,2560]{4,3,0,1,2:T(8,128)(2,1)}, u32[]{:S(2)}, u32[]{:S(2)}) collective-permute-start(bf16[2,2,2,32,2560]{4,3,0,1,2:T(8,128)(2,1)} %dynamic-slice_bitcast_fusion.1), channel_id=1, source_target_pairs={{0,4},{1,5},{2,6},{3,7},{4,0},{5,1},{6,2},{7,3},{8,12},{9,13},{10,... | collective-permute-start | bytes 3932168 | tf_op jit(solution)/shard_map/ppermute | solution.py:402
  254.2 55.7 %collective-permute-start.32 = (bf16[2,2,2,32,2560]{4,3,2,1,0:T(8,128)(2,1)}, bf16[2,2,2,32,2560]{4,3,2,1,0:T(8,128)(2,1)}, u32[]{:S(2)}, u32[]{:S(2)}) collective-permute-start(bf16[2,2,2,32,2560]{4,3,2,1,0:T(8,128)(2,1)} %dynamic-slice_bitcast_fusion), channel_id=1, source_target_pairs={{0,2},{1,3},{2,0},{3,1},{4,6},{5,7},{6,4},{7,5},{8,10},{9,11},{10,... | collective-permute-start | bytes 3932168 | tf_op jit(solution)/shard_map/ppermute | solution.py:402
  291.7 21.3 %collective-permute-start.30 = (bf16[2,2,64,1024]{3,2,0,1:T(8,128)(2,1)S(1)}, bf16[2,2,64,1024]{3,2,0,1:T(8,128)(2,1)S(1)}, u32[]{:S(2)}, u32[]{:S(2)}) collective-permute-start(bf16[2,2,64,1024]{3,2,0,1:T(8,128)(2,1)S(1)} %dynamic-slice_bitcast_fusion.6), channel_id=1, source_target_pairs={{0,4},{1,5},{2,6},{3,7},{4,0},{5,1},{6,2},{7,3},{8,12},{9,13},{10,... | collective-permute-start | bytes 1572872 | tf_op jit(solution)/shard_map/ppermute | solution.py:402
  294.2 19.5 %collective-permute-start.29 = (bf16[2,2,64,1024]{3,2,0,1:T(8,128)(2,1)}, bf16[2,2,64,1024]{3,2,0,1:T(8,128)(2,1)S(1)}, u32[]{:S(2)}, u32[]{:S(2)}) collective-permute-start(bf16[2,2,64,1024]{3,2,0,1:T(8,128)(2,1)} %dynamic-slice_bitcast_fusion.7), channel_id=1, source_target_pairs={{0,2},{1,3},{2,0},{3,1},{4,6},{5,7},{6,4},{7,5},{8,10},{9,11},{10,... | collective-permute-start | bytes 1572872 | tf_op jit(solution)/shard_map/ppermute | solution.py:402
  321.6 57.9 %collective-permute-start.38 = (bf16[512,1536]{0,1:T(8,128)(2,1)}, bf16[512,1536]{0,1:T(8,128)(2,1)}, u32[]{:S(2)}, u32[]{:S(2)}) collective-permute-start(bf16[512,1536]{0,1:T(8,128)(2,1)} %fusion), channel_id=1, source_target_pairs={{0,4},{1,5},{2,6},{3,7},{4,0},{5,1},{6,2},{7,3},{8,12},{9,13},{10,... | collective-permute-start | bytes 4718600 | tf_op jit(solution)/shard_map/ppermute | solution.py:402
  338.6 20.2 %collective-permute-start.44 = (bf16[1024,288]{0,1:T(8,128)(2,1)S(1)}, bf16[1024,288]{0,1:T(8,128)(2,1)S(1)}, u32[]{:S(2)}, u32[]{:S(2)}) collective-permute-start(bf16[1024,288]{0,1:T(8,128)(2,1)S(1)} %select_convert_fusion), channel_id=1, source_target_pairs={{0,1},{1,0},{2,3},{3,2},{4,5},{5,4},{6,7},{7,6},{8,9},{9,8},{10,11... | collective-permute-start | bytes 1769480 | tf_op jit(solution)/shard_map/ppermute | solution.py:402
  340.3 37.5 %collective-permute-start.43 = (bf16[2,32,2560]{2,1,0:T(8,128)(2,1)}, bf16[2,32,2560]{2,1,0:T(8,128)(2,1)S(1)}, u32[]{:S(2)}, u32[]{:S(2)}) collective-permute-start(bf16[2,32,2560]{2,1,0:T(8,128)(2,1)} %dynamic-slice_bitcast_fusion.10), channel_id=1, source_target_pairs={{0,8},{1,9},{2,10},{3,11},{4,12},{5,13},{6,14},{7,15},{8,0},{9,1},... | collective-permute-start | bytes 983048 | tf_op jit(solution)/shard_map/ppermute | solution.py:402
  343.0 34.9 %collective-permute-start.42 = (bf16[2,32,2560]{2,1,0:T(8,128)(2,1)}, bf16[2,32,2560]{2,1,0:T(8,128)(2,1)}, u32[]{:S(2)}, u32[]{:S(2)}) collective-permute-start(bf16[2,32,2560]{2,1,0:T(8,128)(2,1)} %dynamic-slice_bitcast_fusion.11), channel_id=1, source_target_pairs={{0,8},{1,9},{2,10},{3,11},{4,12},{5,13},{6,14},{7,15},{8,0},{9,1},... | collective-permute-start | bytes 983048 | tf_op jit(solution)/shard_map/ppermute | solution.py:402
  345.8 23.4 %collective-permute-start.39 = (bf16[512,1536]{0,1:T(8,128)(2,1)}, bf16[512,1536]{0,1:T(8,128)(2,1)}, u32[]{:S(2)}, u32[]{:S(2)}) collective-permute-start(bf16[512,1536]{0,1:T(8,128)(2,1)} %pad_maximum_fusion.3), channel_id=1, source_target_pairs={{0,1},{1,0},{2,3},{3,2},{4,5},{5,4},{6,7},{7,6},{8,9},{9,8},{10,11... | collective-permute-start | bytes 4718600 | tf_op jit(solution)/shard_map/ppermute | solution.py:402
  381.3 30.8 %collective-permute-start.62 = (bf16[32,2560]{1,0:T(8,128)(2,1)}, bf16[32,2560]{1,0:T(8,128)(2,1)}, u32[]{:S(2)}, u32[]{:S(2)}) collective-permute-start(bf16[32,2560]{1,0:T(8,128)(2,1)} %dynamic-slice_bitcast_fusion.18), channel_id=1, source_target_pairs={{0,16},{1,17},{2,18},{3,19},{4,20},{5,21},{6,22},{7,23},{8,24},{9,... | collective-permute-start | bytes 491528 | tf_op jit(solution)/shard_map/ppermute | solution.py:402
  385.8 27.3 %collective-permute-start.63 = (bf16[32,2560]{1,0:T(8,128)(2,1)}, bf16[32,2560]{1,0:T(8,128)(2,1)}, u32[]{:S(2)}, u32[]{:S(2)}) collective-permute-start(bf16[32,2560]{1,0:T(8,128)(2,1)} %dynamic-slice_bitcast_fusion.17), channel_id=1, source_target_pairs={{0,16},{1,17},{2,18},{3,19},{4,20},{5,21},{6,22},{7,23},{8,24},{9,... | collective-permute-start | bytes 491528 | tf_op jit(solution)/shard_map/ppermute | solution.py:402
  387.6 34.1 %collective-permute-start.48 = (bf16[2,2,64,288]{3,2,1,0:T(8,128)(2,1)}, bf16[2,2,64,288]{3,2,1,0:T(8,128)(2,1)}, u32[]{:S(2)}, u32[]{:S(2)}) collective-permute-start(bf16[2,2,64,288]{3,2,1,0:T(8,128)(2,1)} %dynamic-slice_bitcast_fusion.16), channel_id=1, source_target_pairs={{0,2},{1,3},{2,0},{3,1},{4,6},{5,7},{6,4},{7,5},{8,10},{9,11},{10,... | collective-permute-start | bytes 442376 | tf_op jit(solution)/shard_map/ppermute | solution.py:402
  396.8 24.8 %collective-permute-start.47 = (bf16[2,2,32,1536]{3,2,1,0:T(8,128)(2,1)}, bf16[2,2,32,1536]{3,2,1,0:T(8,128)(2,1)}, u32[]{:S(2)}, u32[]{:S(2)}) collective-permute-start(bf16[2,2,32,1536]{3,2,1,0:T(8,128)(2,1)} %dynamic-slice_bitcast_fusion.8), channel_id=1, source_target_pairs={{0,8},{1,9},{2,10},{3,11},{4,12},{5,13},{6,14},{7,15},{8,0},{9,1},... | collective-permute-start | bytes 1179656 | tf_op jit(solution)/shard_map/ppermute | solution.py:402
  (182 other events, 1378.0 us)

commit v3 on v2

--- a/solution.py
+++ b/solution.py
@@ -1,3 +1,4 @@
+import functools
 import math
 
 import jax
@@ -292,10 +293,10 @@
 FFN_BLOCK = 512
 
 
-def ffn_params(name):
+def ffn_params(name, flops=5 * 10**9, moved=10**7):
     return dict(
         compiler_params=pltpu.CompilerParams(vmem_limit_bytes=32 * 1024 * 1024),
-        cost_estimate=pl.CostEstimate(flops=5 * 10**9, bytes_accessed=10**7, transcendentals=0),
+        cost_estimate=pl.CostEstimate(flops=flops, bytes_accessed=moved, transcendentals=0),
         name=name)
 
 
@@ -362,6 +363,40 @@
         input_output_aliases={3: 0},
         **ffn_params("conc_grad"),
     )(att, gated, got, d_key)
+
+
+def proj_kernel(*refs, gots, split):
+    cols = refs[0].shape[1]
+    outs = refs[6 + gots:]
+    for i in range(3):
+        at = slice(i * cols, (i + 1) * cols)
+        val = tmm(refs[i][...], refs[3 + i][...])
+        for ref in refs[6:6 + gots]:
+            val = val + ref[:, at].astype(f32)
+        if not split:
+            outs[0][:, at] = val.astype(bf16)
+            continue
+        for c in range(cols // 64):
+            for h in range(2):
+                outs[h][c * 32:(c + 1) * 32, at] = val[c * 64 + h * 32:c * 64 + h * 32 + 32].astype(bf16)
+
+
+def proj_grad(gs, xs, keep, near, gots, split):
+    rows, width = xs[0].shape
+    half = width // 2
+    full = pl.BlockSpec((half, 3 * half), lambda j: (0, 0))
+    part = half // 2 if split else half
+    n_out = 2 if split else 1
+    res = pl.pallas_call(
+        functools.partial(proj_kernel, gots=len(gots), split=split),
+        grid=(1,),
+        in_specs=[pl.BlockSpec((rows, half), lambda j: (0, keep))] * 3
+        + [pl.BlockSpec((rows, half), lambda j: (0, 0 if near else 1))] * 3 + [full] * len(gots),
+        out_specs=[pl.BlockSpec((part, 3 * half), lambda j: (0, 0))] * n_out,
+        out_shape=[jax.ShapeDtypeStruct((part, 3 * half), bf16)] * n_out,
+        **ffn_params("proj_grad", 3 * 10**8, 10**6),
+    )(*gs, *xs, *gots)
+    return res if split else res[0]
 
 
 def layer_norm(x, gain, bias):
@@ -621,6 +656,8 @@
     val_got, key_got = swap(val_far, 1), swap(key_far, 1)
     g_mixed, g_mix_c, g_gain_c, g_bias_c = pull_chan((g_xc + g_xc_far,))
     g_mixed = g_out + g_mixed
+    early = jnp.concatenate(
+        [g_mix_c, g_gain_c[None], g_bias_c[None], jnp.zeros((5, width), f32)], 0)
     g_att = g_mixed.astype(bf16)
     conc_got = swap(tmm(g_att, gated_far).astype(bf16), 1)
     gg = in_core_order(mm(g_att, wo), mm(g_att, wo_far), 1)
@@ -636,13 +673,13 @@
     v_got = send(d_value, 1)
     grads = mixer_bwd(args, par, saved, gg, side_y, 1, grads)
 
-    def proj_part(near, keep):
+    x_proj = [xs[0], xs[2], xs[3]]
+
+    def proj_part(near):
         cols = slice(0, half) if near else slice(half, width)
-        outs = slice(half, width) if keep else slice(0, half)
-        return jnp.concatenate(
-            [tmm(grads[9 + i][:, outs], xs[j][:, cols]) for i, j in enumerate((0, 2, 3))], 1)
-
-    away = on_core(proj_part(True, False), proj_part(False, False).astype(bf16))
+        return jnp.concatenate([tmm(grads[9 + i][:, :half], x_proj[i][:, cols]) for i in range(3)], 1)
+
+    away = on_core(proj_part(True), proj_part(False).astype(bf16))
     grads = mixer_bwd(args, par, saved, gg, side_y, 2, grads)
     grads, v_got, k_got, away = tie(grads, v_got, k_got, away)
     d_value, d_key = take(d_value, v_got, 1), take(d_key, k_got, 0)
@@ -653,7 +690,7 @@
     grads, v_got, k_got = tie(grads, v_got, k_got)
     d_value, d_key = take(d_value, v_got, 2), take(d_key, k_got, 1)
     v_got, k_got = send(d_value, 3), send(d_key, 2)
-    home = proj_part(True, True) + swap(proj_part(False, True).astype(bf16), 1).astype(f32)
+    home = swap(proj_grad(grads[9:12], x_proj, 1, False, [], False), 1)
     gp = jnp.sum(grads[8].reshape(-1, 8, width), 0)
     g_proj, g_os, g_first = grads[:3], grads[3:7], grads[7]
     g_ls = tuple(mm(g_os[i], w_out[:, CUTS[i]:CUTS[i + 1]]) for i in range(4))
@@ -673,18 +710,19 @@
         d_low = [d_low.reshape(2, 2, 2, 2, 64, -1)]
         l_got = sum_send(d_low, ONE[0])
     if small_slice:
-        g_xs, away, home, v_got, k_got, l_got = tie(g_xs, away, home, v_got, k_got, l_got)
-        d_proj = (home + away.astype(f32)).astype(bf16)
-        d_proj = d_proj.reshape(2, 2, 2, 64, d_proj.shape[1])
-        d_proj = [d_proj[..., :32, :], d_proj[..., 32:, :]]
+        g_xs, away, home = tie(g_xs, away, home)
+        d_proj = proj_grad(grads[9:12], x_proj, 1, True, [home, away], True)
+        d_proj = [p.reshape(2, 2, 2, 32, -1) for p in d_proj]
+        p_send = [pick(p, 1 - side_of(bit), axis) for p, (axis, bit) in zip(d_proj, TAIL[0])]
+        p_send, v_got, k_got, l_got = tie(p_send, v_got, k_got, l_got)
+        p_got = [swap(p, bit) for p, (axis, bit) in zip(p_send, TAIL[0])]
         d_key, d_low = take(d_key, k_got, 2), sum_take(d_low, l_got, ONE[0])
-        p_got, l_got, k_got = sum_send(d_proj, TAIL[0]), sum_send(d_low, ONE[1]), send(d_key, 3)
+        l_got, k_got = sum_send(d_low, ONE[1]), send(d_key, 3)
     g_x, g_mix_t, g_gain_t, g_bias_t = pull_front(g_xs)
     g_x = g_mixed + by_core(g_x)
     g_mix_t, g_gain_t, g_bias_t = by_core(g_mix_t), by_core(g_gain_t), by_core(g_bias_t)
     d_small = jnp.concatenate(
-        [g_mix_t, g_mix_c, g_gain_t[None], gp[6:7], g_gain_c[None], g_bias_t[None], gp[7:8],
-         g_bias_c[None], gp[0:6], jnp.zeros((5, width), f32)], 0)
+        [gp, jnp.concatenate([g_mix_t, g_gain_t[None], g_bias_t[None]], 0), early], 0)
     if small_slice:
         d_small, p_got, l_got, hidden, hidden_far = tie(d_small, p_got, l_got, hidden, hidden_far)
         d_proj, d_low = sum_take(d_proj, p_got, TAIL[0]), sum_take(d_low, l_got, ONE[1])
@@ -692,14 +730,17 @@
         for bit in (1, 2, 4, 8, 16):
             d_small = d_small + swap(d_small, bit)
         out = mixed + mm(hidden, wv)
-        out, p_got, l_got = tie(out, p_got, l_got)
+        out, p_got, l_got, k_got, v_got = tie(out, p_got, l_got, k_got, v_got)
         d_proj, d_low = sum_take(d_proj, p_got, TAIL[1]), sum_take(d_low, l_got, ONE[2])
-        p_got, l_got = sum_send(d_proj, TAIL[2]), sum_send(d_low, ONE[3])
+        p_send = [pick(p, 1 - side_of(bit), axis) for p, (axis, bit) in zip(d_proj, TAIL[2])]
+        p_send, v_got, k_got = tie(p_send, v_got, k_got)
+        p_got = [swap(p, bit) for p, (axis, bit) in zip(p_send, TAIL[2])]
+        l_got = sum_send(d_low, ONE[3])
         out = valid * (out + mm(hidden_far, wv_far))
         d_proj = finish(sum_take(d_proj, p_got, TAIL[2]))
         d_low = finish(sum_take(d_low, l_got, ONE[3]))
     else:
-        home = home.astype(bf16).reshape(width // 256, 1, 128, -1)
+        home = proj_grad(grads[9:12], x_proj, 1, True, [home], False).reshape(width // 256, 1, 128, -1)
         d_proj = whole_sum(jnp.concatenate([home, away.reshape(home.shape)], 1).reshape(width, -1))
         d_low = whole_sum(d_low)
         d_small = lax.psum(d_small, "dp")
@@ -720,8 +761,11 @@
     d_key = d_key.reshape(shard, -1)
     return (
         out.astype(bf16).reshape(x_in.shape), g_x.astype(bf16).reshape(x_in.shape),
-        g_first.reshape(x_in.shape), d_small[0:7], d_small[7:10], d_small[10:13],
-        d_small[13:15], d_small[15], d_small[16], d_small[17:19],
+        g_first.reshape(x_in.shape),
+        jnp.concatenate([d_small[8:14], d_small[16:17]], 0),
+        jnp.concatenate([d_small[14:15], d_small[6:7], d_small[17:18]], 0),
+        jnp.concatenate([d_small[15:16], d_small[7:8], d_small[18:19]], 0),
+        d_small[0:2], d_small[2], d_small[3], d_small[4:6],
         low_a, low_b.T, d_in, d_conc, d_key, d_value * scale)
 
 

time: 469 us -> 460 us (0.981)
  local copies, waits for them, and re-layouts: 55.1 us -> 48.1 us
    dot_general x55 -> x49, matrix products: 36.3 us -> 33.3 us  [dn(): lax.dot_general(x, y, (((cx,), (cy,)), ((), ())), preferred_element_type=...]
    unnamed x293 -> x273, local copies, waits for them, and re-layouts: 15.4 us -> 13.1 us
    convert_element_type x24 -> x25, other arithmetic: 15.5 us -> 16.1 us  [add(): return (a.astype(f32) + b.astype(f32)).astype(bf16)]
  transfers between devices with their start and end apart: 65 -> 65, of which waited for: 27 -> 27; matrix products, arithmetic and copies ran while one was open for 26% -> 24% of each run, Pallas kernels for 22% -> 24%
where the time goes in v3:
time: 460 us; the launch traced here: 454 us
  Pallas kernels  126 us (27%)
  waiting for transfers between devices  112 us (24%)
  starting transfers between devices  66.5 us (14%)
  other arithmetic  64.4 us (14%)
  local copies, waits for them, and re-layouts  48.1 us (10%)
  matrix products  33.3 us (7%)
    ppermute x65, waiting for transfers between devices, swap(): return lax.ppermute(x, 'dp', [(i, i ^ bit) for i in range(n)])  112 us
    ppermute x65, starting transfers between devices, swap(): return lax.ppermute(x, 'dp', [(i, i ^ bit) for i in range(n)])  66.5 us
    pallas_call x4, Pallas kernels, mixer_fwd(): pl.pallas_call(body, grid=(seqs // 2, pairs // 4), in_specs=[tile] * 8 +...  51.9 us
    pallas_call x4, Pallas kernels, mixer_bwd(): pl.pallas_call(body, grid_spec=pltpu.PrefetchScalarGridSpec(num_scalar_pr...  44.7 us
    dot_general x49, matrix products, dn(): lax.dot_general(x, y, (((cx,), (cy,)), ((), ())), preferred_element_type=...  33.3 us
    pallas_call x2, Pallas kernels, ffn_half(): pl.pallas_call(ffn_kernel, grid=(units // FFN_BLOCK,), in_specs=[tall, pl...  17.3 us
    select_n x26, other arithmetic, join(): jnp.where(mine == 0, jnp.stack([a, b], axis), jnp.stack([b, a], axis))  16.1 us
    convert_element_type x25, other arithmetic, add(): return (a.astype(f32) + b.astype(f32)).astype(bf16)  16.1 us
  transfers between devices with their start and end apart: 65, of which 27 were waited for; matrix products, arithmetic and copies ran while one was open for 24% of the time, Pallas kernels for 24%

profile of v3, /device:TPU:0, one launch (start us, length us, event | category | flops | bytes accessed | tf_op | source)
XLA Modules:
  0.0 454.1 jit_solution(1887423517779963912)
XLA Ops:
  11.9 8.7 %collective-permute-done.4 = bf16[64,896]{1,0:T(8,128)(2,1)S(1)} collective-permute-done((bf16[64,896]{1,0:T(8,128)(2,1)S(1)}, bf16[64,896]{1,0:T(8,128)(2,1)S(1)}, u32[]{:S(2)}, u32[]{:S(2)}) %collective-permute-start.4) | collective-permute-done | bytes 114720 | tf_op jit(solution)/shard_map/ppermute | solution.py:437
  23.9 5.3 %collective-permute-done.5 = bf16[2,64,896]{2,1,0:T(8,128)(2,1)S(1)} collective-permute-done((bf16[2,64,896]{2,1,0:T(8,128)(2,1)S(1)}, bf16[2,64,896]{2,1,0:T(8,128)(2,1)S(1)}, u32[]{:S(2)}, u32[]{:S(2)}) %collective-permute-start.5) | collective-permute-done | bytes 229408 | tf_op jit(solution)/shard_map/ppermute | solution.py:437
  29.3 4.3 collective-permute-done.2
  39.3 13.5 %collective-permute-done.9 = bf16[64,2560]{1,0:T(8,128)(2,1)S(1)} collective-permute-done((bf16[64,2560]{1,0:T(8,128)(2,1)S(1)}, bf16[64,2560]{1,0:T(8,128)(2,1)S(1)}, u32[]{:S(2)}, u32[]{:S(2)}) %collective-permute-start.9) | collective-permute-done | bytes 327712 | tf_op jit(solution)/shard_map/ppermute | solution.py:437
  61.3 14.4 %collective-permute-done.13 = bf16[128,1024]{1,0:T(8,128)(2,1)S(1)} collective-permute-done((bf16[128,1024]{1,0:T(8,128)(2,1)S(1)}, bf16[128,1024]{1,0:T(8,128)(2,1)S(1)}, u32[]{:S(2)}, u32[]{:S(2)}) %collective-permute-start.13) | collective-permute-done | bytes 262176 | tf_op jit(solution)/shard_map/ppermute | solution.py:437
  98.3 4.4 collective-permute-done.15
  112.0 13.0 %mixer_fwd.4 = (bf16[256,1024]{1,0:T(8,128)(2,1)S(1)}, f32[2048,256]{1,0:T(8,128)S(1)}, f32[256,1024]{1,0:T(8,128)S(1)}, f32[256,1024]{1,0:T(8,128)S(1)}) custom-call(f32[256,1024]{1,0:T(8,128)S(1)} %convolution_add_fusion.5.refs_0_.refs_1_, f32[256,1024]{1,0:T(8,128)S(1)} %convolution_add_fusion.4.refs_1_.refs_2_, ...), custom_call_target="tpu_custom_call" | custom-call | flops 10000000000 | bytes 10000000 | tf_op jit(solution)/shard_map/mixer_fwd/pallas_call | solution.py:226
  131.6 13.0 %mixer_fwd.5 = (bf16[256,1024]{1,0:T(8,128)(2,1)S(1)}, f32[2048,256]{1,0:T(8,128)S(1)}, f32[256,1024]{1,0:T(8,128)S(1)}, f32[256,1024]{1,0:T(8,128)S(1)}) custom-call(f32[256,1024]{1,0:T(8,128)S(1)} %convolution_add_fusion.5.refs_0_.refs_1_, ...), custom_call_target="tpu_custom_call", output_to_operand_aliasing={{0}: (9, {}), {1}: (10, {}), {2}: (11, {}), {3}: (12, {})} | custom-call | flops 10000000000 | bytes 10000000 | tf_op jit(solution)/shard_map/mixer_fwd/pallas_call | solution.py:226
  144.8 13.0 %mixer_fwd.6 = (bf16[256,1024]{1,0:T(8,128)(2,1)S(1)}, f32[2048,256]{1,0:T(8,128)S(1)}, f32[256,1024]{1,0:T(8,128)S(1)}, f32[256,1024]{1,0:T(8,128)S(1)}) custom-call(f32[256,1024]{1,0:T(8,128)S(1)} %convolution_add_fusion.5.refs_0_.refs_1_, ...), custom_call_target="tpu_custom_call", output_to_operand_aliasing={{0}: (9, {}), {1}: (10, {}), {2}: (11, {}), {3}: (12, {})} | custom-call | flops 10000000000 | bytes 10000000 | tf_op jit(solution)/shard_map/mixer_fwd/pallas_call | solution.py:226
  157.9 13.0 %mixer_fwd.7 = (bf16[256,1024]{1,0:T(8,128)(2,1)S(1)}, f32[2048,256]{1,0:T(8,128)S(1)}, f32[256,1024]{1,0:T(8,128)S(1)}, f32[256,1024]{1,0:T(8,128)S(1)}) custom-call(f32[256,1024]{1,0:T(8,128)S(1)} %convolution_add_fusion.5.refs_0_.refs_1_, ...), custom_call_target="tpu_custom_call", output_to_operand_aliasing={{0}: (9, {}), {1}: (10, {}), {2}: (11, {}), {3}: (12, {})} | custom-call | flops 10000000000 | bytes 10000000 | tf_op jit(solution)/shard_map/mixer_fwd/pallas_call | solution.py:226
  174.7 13.0 %collective-permute-done.19 = bf16[2,2,2,64,2560]{4,3,2,1,0:T(8,128)(2,1)S(1)} collective-permute-done((bf16[2,2,2,64,2560]{4,3,2,1,0:T(8,128)(2,1)S(1)}, bf16[2,2,2,64,2560]{4,3,2,1,0:T(8,128)(2,1)S(1)}, u32[]{:S(2)}, u32[]{:S(2)}) %collective-permute-start.19) | collective-permute-done | bytes 2621472 | tf_op jit(solution)/shard_map/ppermute | solution.py:437
  205.9 6.7 %ffn_half.2 = (bf16[256,2048]{1,0:T(8,128)(2,1)S(1)}, bf16[256,2048]{1,0:T(8,128)(2,1)S(1)}, f32[256,1024]{1,0:T(8,128)S(1)}) custom-call(bf16[256,1024]{1,0:T(8,128)(2,1)S(1)} %add_convert_fusion.1.xc, bf16[1024,256]{1,0:T(8,128)(2,1)S(1)} %copy-done.16, bf16[256,1024]{1,0:T(8,128)(2,1)S(1)} %fusion.22.gf, bf16[1024,2560]{1,0:T(8,128)(2,1)} %bitcast.91.wk, ...), custom_call_target="tpu_custom_call" | custom-call | flops 5000000000 | bytes 10000000 | tf_op jit(solution)/shard_map/ffn_half/pallas_call | solution.py:312
  213.3 10.5 %ffn_half.3 = (bf16[256,2048]{1,0:T(8,128)(2,1)S(1)}, bf16[256,2048]{1,0:T(8,128)(2,1)}, f32[256,1024]{1,0:T(8,128)S(1)}, bf16[2048,1024]{1,0:T(8,128)(2,1)}, bf16[1024,2048]{1,0:T(8,128)(2,1)}) custom-call(bf16[256,1024]{1,0:T(8,128)(2,1)S(1)} %add_convert_fusion.1.xc, bf16[1024,256]{1,0:T(8,128)(2,1)S(1)} %copy-done.16, bf16[256,1024]{1,0:T(8,128)(2,1)S(1)} %fusion.22.gf, ...), custom_call_target="tpu_custom_call" | custom-call | flops 5000000000 | bytes 10000000 | tf_op jit(solution)/shard_map/ffn_half/pallas_call | solution.py:312
  234.7 4.3 collective-permute-done.26.got
  239.1 5.8 %ffn_grads.1 = (bf16[2048,1024]{1,0:T(8,128)(2,1)S(1)}, bf16[1024,2560]{1,0:T(8,128)(2,1)S(1)}) custom-call(bf16[1024,256]{1,0:T(8,128)(2,1)S(1)} %copy-done.17, bf16[256,1024]{1,0:T(8,128)(2,1)S(1)} %fusion.22.gf, bf16[256,2048]{1,0:T(8,128)(2,1)S(1)} %copy-done.21, bf16[256,2048]{1,0:T(8,128)(2,1)S(1)} %copy-done.26, ...), custom_call_target="tpu_custom_call" | custom-call | flops 5000000000 | bytes 10000000 | tf_op jit(solution)/shard_map/ffn_grads/pallas_call | solution.py:334
  256.2 11.4 %mixer_bwd.4 = (bf16[256,1024]{1,0:T(8,128)(2,1)S(1)}, bf16[256,1024]{1,0:T(8,128)(2,1)S(1)}, bf16[256,1024]{1,0:T(8,128)(2,1)S(1)}, bf16[256,1024]{1,0:T(8,128)...) custom-call(s32[1]{0:T(128)} %bitcast.96.refs_0_, ...), custom_call_target="tpu_custom_call" | custom-call | flops 10000000000 | bytes 10000000 | tf_op jit(solution)/shard_map/mixer_bwd/pallas_call | solution.py:257
  267.6 6.1 %collective-permute-done.27 = bf16[2,2,2,64,1024]{4,3,0,1,2:T(8,128)(2,1)S(1)} collective-permute-done((bf16[2,2,2,64,1024]{4,3,0,1,2:T(8,128)(2,1)S(1)}, bf16[2,2,2,64,1024]{4,3,0,1,2:T(8,128)(2,1)S(1)}, u32[]{:S(2)}, u32[]{:S(2)}) %collective-permute-start.27) | collective-permute-done | bytes 1048608 | tf_op jit(solution)/shard_map/ppermute | solution.py:437
  274.9 10.9 %mixer_bwd.5 = (bf16[256,1024]{1,0:T(8,128)(2,1)S(1)}, bf16[256,1024]{1,0:T(8,128)(2,1)S(1)}, bf16[256,1024]{1,0:T(8,128)(2,1)S(1)}, bf16[256,1024]{1,0:T(8,128)...) custom-call(s32[1]{0:T(128)} %bitcast.96.refs_0_, ...), custom_call_target="tpu_custom_call", output_to_operand_aliasing={{0}: (14, {}), {1}: (15, {}), {2}: (16, {}), {3}: (17, {}),... | custom-call | flops 10000000000 | bytes 10000000 | tf_op jit(solution)/shard_map/mixer_bwd/pallas_call | solution.py:257
  293.8 11.2 %mixer_bwd.6 = (bf16[256,1024]{1,0:T(8,128)(2,1)S(1)}, bf16[256,1024]{1,0:T(8,128)(2,1)S(1)}, bf16[256,1024]{1,0:T(8,128)(2,1)S(1)}, bf16[256,1024]{1,0:T(8,128)...) custom-call(s32[1]{0:T(128)} %bitcast.96.refs_0_, ...), custom_call_target="tpu_custom_call", output_to_operand_aliasing={{0}: (14, {}), {1}: (15, {}), {2}: (16, {}), {3}: (17, {}),... | custom-call | flops 10000000000 | bytes 10000000 | tf_op jit(solution)/shard_map/mixer_bwd/pallas_call | solution.py:257
  308.1 4.5 collective-permute-done.30
  323.8 11.1 %mixer_bwd.7 = (bf16[256,1024]{1,0:T(8,128)(2,1)S(1)}, bf16[256,1024]{1,0:T(8,128)(2,1)S(1)}, bf16[256,1024]{1,0:T(8,128)(2,1)S(1)}, bf16[256,1024]{1,0:T(8,128)...) custom-call(s32[1]{0:T(128)} %bitcast.96.refs_0_, ...), custom_call_target="tpu_custom_call", output_to_operand_aliasing={{0}: (14, {}), {1}: (15, {}), {2}: (16, {}), {3}: (17, {}),... | custom-call | flops 10000000000 | bytes 10000000 | tf_op jit(solution)/shard_map/mixer_bwd/pallas_call | solution.py:257
  396.2 4.1 concatenate.378
  403.5 4.5 collective-permute-start.50
  445.5 5.3 %collective-permute-done.58 = f32[24,1024]{1,0:T(8,128)S(1)} collective-permute-done((f32[24,1024]{1,0:T(8,128)S(1)}, f32[24,1024]{1,0:T(8,128)S(1)}, u32[]{:S(2)}, u32[]{:S(2)}) %collective-permute-start.58) | collective-permute-done | bytes 98336 | tf_op jit(solution)/shard_map/ppermute | solution.py:437
  (659 shorter events, 238.0 us)
Async XLA Ops:
  33.6 19.2 %collective-permute-start.7 = (bf16[2,2,64,1024]{3,2,1,0:T(8,128)(2,1)S(1)}, bf16[2,2,64,1024]{3,2,1,0:T(8,128)(2,1)S(1)}, u32[]{:S(2)}, u32[]{:S(2)}) collective-permute-start(bf16[2,2,64,1024]{3,2,1,0:T(8,128)(2,1)S(1)} %maximum_select_fusion.20), channel_id=1, source_target_pairs={{0,2},{1,3},{2,0},{3,1},{4,6},{5,7},{6,4},{7,5},{8,10},{9,11},{10,... | collective-permute-start | bytes 1572872 | tf_op jit(solution)/shard_map/ppermute | solution.py:437
  54.3 22.2 %collective-permute-start.11 = (bf16[2,2,2,64,896]{4,3,1,0,2:T(8,128)(2,1)S(1)}, bf16[2,2,2,64,896]{4,3,1,0,2:T(8,128)(2,1)S(1)}, u32[]{:S(2)}, u32[]{:S(2)}) collective-permute-start(bf16[2,2,2,64,896]{4,3,1,0,2:T(8,128)(2,1)S(1)} %maximum_select_fusion.17), channel_id=1, source_target_pairs={{0,2},{1,3},{2,0},{3,1},{4,6},{5,7},{6,4},{7,5},{8,10},{9,11},{10,... | collective-permute-start | bytes 2752520 | tf_op jit(solution)/shard_map/ppermute | solution.py:437
  55.0 23.9 %collective-permute-start.10 = (bf16[2,2,2,64,1024]{4,3,2,1,0:T(8,128)(2,1)S(1)}, bf16[2,2,2,64,1024]{4,3,2,1,0:T(8,128)(2,1)}, u32[]{:S(2)}, u32[]{:S(2)}) collective-permute-start(bf16[2,2,2,64,1024]{4,3,2,1,0:T(8,128)(2,1)S(1)} %maximum_select_fusion.11), channel_id=1, source_target_pairs={{0,4},{1,5},{2,6},{3,7},{4,0},{5,1},{6,2},{7,3},{8,12},{9,13},{10,... | collective-permute-start | bytes 3145736 | tf_op jit(solution)/shard_map/ppermute | solution.py:437
  55.7 20.8 %collective-permute-start.12 = (bf16[2,64,2560]{2,1,0:T(8,128)(2,1)S(1)}, bf16[2,64,2560]{2,1,0:T(8,128)(2,1)S(1)}, u32[]{:S(2)}, u32[]{:S(2)}) collective-permute-start(bf16[2,64,2560]{2,1,0:T(8,128)(2,1)S(1)} %maximum_select_fusion.18), channel_id=1, source_target_pairs={{0,8},{1,9},{2,10},{3,11},{4,12},{5,13},{6,14},{7,15},{8,0},{9,1},... | collective-permute-start | bytes 1966088 | tf_op jit(solution)/shard_map/ppermute | solution.py:437
  56.5 19.2 %collective-permute-start.13 = (bf16[128,1024]{1,0:T(8,128)(2,1)S(1)}, bf16[128,1024]{1,0:T(8,128)(2,1)S(1)}, u32[]{:S(2)}, u32[]{:S(2)}) collective-permute-start(bf16[128,1024]{1,0:T(8,128)(2,1)S(1)} %copy-done.95), channel_id=1, source_target_pairs={{0,16},{1,17},{2,18},{3,19},{4,20},{5,21},{6,22},{7,23},{8,24},{9,... | collective-permute-start | bytes 786440 | tf_op jit(solution)/shard_map/ppermute | solution.py:437
  92.4 32.6 %collective-permute-start.17 = (bf16[2,2,64,2560]{3,2,1,0:T(8,128)(2,1)S(1)}, bf16[2,2,64,2560]{3,2,1,0:T(8,128)(2,1)S(1)}, u32[]{:S(2)}, u32[]{:S(2)}) collective-permute-start(bf16[2,2,64,2560]{3,2,1,0:T(8,128)(2,1)S(1)} %copy-done.43), channel_id=1, source_target_pairs={{0,2},{1,3},{2,0},{3,1},{4,6},{5,7},{6,4},{7,5},{8,10},{9,11},{10,... | collective-permute-start | bytes 3932168 | tf_op jit(solution)/shard_map/ppermute | solution.py:437
  102.9 24.9 %collective-permute-start.18 = (bf16[2,2,128,1024]{3,2,0,1:T(8,128)(2,1)S(1)}, bf16[2,2,128,1024]{3,2,0,1:T(8,128)(2,1)S(1)}, u32[]{:S(2)}, u32[]{:S(2)}) collective-permute-start(bf16[2,2,128,1024]{3,2,0,1:T(8,128)(2,1)S(1)} %maximum_select_fusion.12), channel_id=1, source_target_pairs={{0,4},{1,5},{2,6},{3,7},{4,0},{5,1},{6,2},{7,3},{8,12},{9,13},{10,... | collective-permute-start | bytes 3145736 | tf_op jit(solution)/shard_map/ppermute | solution.py:437
  128.1 46.6 %collective-permute-start.20 = (bf16[2,2,2,128,1024]{4,3,0,1,2:T(8,128)(2,1)S(1)}, bf16[2,2,2,128,1024]{4,3,0,1,2:T(8,128)(2,1)}, u32[]{:S(2)}, u32[]{:S(2)}) collective-permute-start(bf16[2,2,2,128,1024]{4,3,0,1,2:T(8,128)(2,1)S(1)} %maximum_select_fusion.4), channel_id=1, source_target_pairs={{0,2},{1,3},{2,0},{3,1},{4,6},{5,7},{6,4},{7,5},{8,10},{9,11},{10,... | collective-permute-start | bytes 6291464 | tf_op jit(solution)/shard_map/ppermute | solution.py:437
  130.3 57.4 %collective-permute-start.19 = (bf16[2,2,2,64,2560]{4,3,2,1,0:T(8,128)(2,1)S(1)}, bf16[2,2,2,64,2560]{4,3,2,1,0:T(8,128)(2,1)S(1)}, u32[]{:S(2)}, u32[]{:S(2)}) collective-permute-start(bf16[2,2,2,64,2560]{4,3,2,1,0:T(8,128)(2,1)S(1)} %maximum_select_fusion.2), channel_id=1, source_target_pairs={{0,4},{1,5},{2,6},{3,7},{4,0},{5,1},{6,2},{7,3},{8,12},{9,13},{10,... | collective-permute-start | bytes 7864328 | tf_op jit(solution)/shard_map/ppermute | solution.py:437
  247.7 26.1 %collective-permute-start.27 = (bf16[2,2,2,64,1024]{4,3,0,1,2:T(8,128)(2,1)S(1)}, bf16[2,2,2,64,1024]{4,3,0,1,2:T(8,128)(2,1)S(1)}, u32[]{:S(2)}, u32[]{:S(2)}) collective-permute-start(bf16[2,2,2,64,1024]{4,3,0,1,2:T(8,128)(2,1)S(1)} %dynamic-slice_bitcast_fusion.3), channel_id=1, source_target_pairs={{0,4},{1,5},{2,6},{3,7},{4,0},{5,1},{6,2},{7,3},{8,12},{9,13},{10,... | collective-permute-start | bytes 3145736 | tf_op jit(solution)/shard_map/ppermute | solution.py:437
  248.7 26.2 %collective-permute-start.28 = (bf16[2,2,2,64,1024]{4,3,0,1,2:T(8,128)(2,1)S(1)}, bf16[2,2,2,64,1024]{4,3,0,1,2:T(8,128)(2,1)}, u32[]{:S(2)}, u32[]{:S(2)}) collective-permute-start(bf16[2,2,2,64,1024]{4,3,0,1,2:T(8,128)(2,1)S(1)} %dynamic-slice_bitcast_fusion.2), channel_id=1, source_target_pairs={{0,2},{1,3},{2,0},{3,1},{4,6},{5,7},{6,4},{7,5},{8,10},{9,11},{10,... | collective-permute-start | bytes 3145736 | tf_op jit(solution)/shard_map/ppermute | solution.py:437
  252.3 55.8 %collective-permute-start.31 = (bf16[2,2,2,32,2560]{4,3,0,1,2:T(8,128)(2,1)}, bf16[2,2,2,32,2560]{4,3,0,1,2:T(8,128)(2,1)}, u32[]{:S(2)}, u32[]{:S(2)}) collective-permute-start(bf16[2,2,2,32,2560]{4,3,0,1,2:T(8,128)(2,1)} %dynamic-slice_bitcast_fusion.1), channel_id=1, source_target_pairs={{0,4},{1,5},{2,6},{3,7},{4,0},{5,1},{6,2},{7,3},{8,12},{9,13},{10,... | collective-permute-start | bytes 3932168 | tf_op jit(solution)/shard_map/ppermute | solution.py:437
  253.6 54.5 %collective-permute-start.32 = (bf16[2,2,2,32,2560]{4,3,2,1,0:T(8,128)(2,1)}, bf16[2,2,2,32,2560]{4,3,2,1,0:T(8,128)(2,1)}, u32[]{:S(2)}, u32[]{:S(2)}) collective-permute-start(bf16[2,2,2,32,2560]{4,3,2,1,0:T(8,128)(2,1)} %dynamic-slice_bitcast_fusion), channel_id=1, source_target_pairs={{0,2},{1,3},{2,0},{3,1},{4,6},{5,7},{6,4},{7,5},{8,10},{9,11},{10,... | collective-permute-start | bytes 3932168 | tf_op jit(solution)/shard_map/ppermute | solution.py:437
  290.8 21.8 %collective-permute-start.30 = (bf16[2,2,64,1024]{3,2,0,1:T(8,128)(2,1)}, bf16[2,2,64,1024]{3,2,0,1:T(8,128)(2,1)}, u32[]{:S(2)}, u32[]{:S(2)}) collective-permute-start(bf16[2,2,64,1024]{3,2,0,1:T(8,128)(2,1)} %dynamic-slice_bitcast_fusion.6), channel_id=1, source_target_pairs={{0,4},{1,5},{2,6},{3,7},{4,0},{5,1},{6,2},{7,3},{8,12},{9,13},{10,... | collective-permute-start | bytes 1572872 | tf_op jit(solution)/shard_map/ppermute | solution.py:437
  292.5 20.7 %collective-permute-start.29 = (bf16[2,2,64,1024]{3,2,0,1:T(8,128)(2,1)S(1)}, bf16[2,2,64,1024]{3,2,0,1:T(8,128)(2,1)S(1)}, u32[]{:S(2)}, u32[]{:S(2)}) collective-permute-start(bf16[2,2,64,1024]{3,2,0,1:T(8,128)(2,1)S(1)} %dynamic-slice_bitcast_fusion.7), channel_id=1, source_target_pairs={{0,2},{1,3},{2,0},{3,1},{4,6},{5,7},{6,4},{7,5},{8,10},{9,11},{10,... | collective-permute-start | bytes 1572872 | tf_op jit(solution)/shard_map/ppermute | solution.py:437
  315.7 19.3 %collective-permute-start.37 = (bf16[2,2,32,2560]{3,2,1,0:T(8,128)(2,1)S(1)}, bf16[2,2,32,2560]{3,2,1,0:T(8,128)(2,1)S(1)}, u32[]{:S(2)}, u32[]{:S(2)}) collective-permute-start(bf16[2,2,32,2560]{3,2,1,0:T(8,128)(2,1)S(1)} %dynamic-slice_bitcast_fusion.4), channel_id=1, source_target_pairs={{0,4},{1,5},{2,6},{3,7},{4,0},{5,1},{6,2},{7,3},{8,12},{9,13},{10,... | collective-permute-start | bytes 1966088 | tf_op jit(solution)/shard_map/ppermute | solution.py:437
  323.0 43.2 %collective-permute-start.38 = (bf16[512,1536]{1,0:T(8,128)(2,1)}, bf16[512,1536]{1,0:T(8,128)(2,1)}, u32[]{:S(2)}, u32[]{:S(2)}) collective-permute-start(bf16[512,1536]{1,0:T(8,128)(2,1)} %fusion), channel_id=1, source_target_pairs={{0,4},{1,5},{2,6},{3,7},{4,0},{5,1},{6,2},{7,3},{8,12},{9,13},{10,... | collective-permute-start | bytes 4718600 | tf_op jit(solution)/shard_map/ppermute | solution.py:437
  338.7 19.5 %collective-permute-start.44 = (bf16[1024,288]{0,1:T(8,128)(2,1)S(1)}, bf16[1024,288]{0,1:T(8,128)(2,1)S(1)}, u32[]{:S(2)}, u32[]{:S(2)}) collective-permute-start(bf16[1024,288]{0,1:T(8,128)(2,1)S(1)} %select_convert_fusion), channel_id=1, source_target_pairs={{0,1},{1,0},{2,3},{3,2},{4,5},{5,4},{6,7},{7,6},{8,9},{9,8},{10,11... | collective-permute-start | bytes 1769480 | tf_op jit(solution)/shard_map/ppermute | solution.py:437
  339.8 35.5 %collective-permute-start.43 = (bf16[2,32,2560]{2,1,0:T(8,128)(2,1)}, bf16[2,32,2560]{2,1,0:T(8,128)(2,1)}, u32[]{:S(2)}, u32[]{:S(2)}) collective-permute-start(bf16[2,32,2560]{2,1,0:T(8,128)(2,1)} %dynamic-slice_bitcast_fusion.10), channel_id=1, source_target_pairs={{0,8},{1,9},{2,10},{3,11},{4,12},{5,13},{6,14},{7,15},{8,0},{9,1},... | collective-permute-start | bytes 983048 | tf_op jit(solution)/shard_map/ppermute | solution.py:437
  342.3 33.0 %collective-permute-start.42 = (bf16[2,32,2560]{2,1,0:T(8,128)(2,1)}, bf16[2,32,2560]{2,1,0:T(8,128)(2,1)}, u32[]{:S(2)}, u32[]{:S(2)}) collective-permute-start(bf16[2,32,2560]{2,1,0:T(8,128)(2,1)} %dynamic-slice_bitcast_fusion.11), channel_id=1, source_target_pairs={{0,8},{1,9},{2,10},{3,11},{4,12},{5,13},{6,14},{7,15},{8,0},{9,1},... | collective-permute-start | bytes 983048 | tf_op jit(solution)/shard_map/ppermute | solution.py:437
  344.8 24.2 %collective-permute-start.39 = (bf16[512,1536]{1,0:T(8,128)(2,1)}, bf16[512,1536]{1,0:T(8,128)(2,1)}, u32[]{:S(2)}, u32[]{:S(2)}) collective-permute-start(bf16[512,1536]{1,0:T(8,128)(2,1)} %proj_grad.2), channel_id=1, source_target_pairs={{0,1},{1,0},{2,3},{3,2},{4,5},{5,4},{6,7},{7,6},{8,9},{9,8},{10,11... | collective-permute-start | bytes 4718600 | tf_op jit(solution)/shard_map/ppermute | solution.py:437
  380.1 36.3 %collective-permute-start.53 = (bf16[32,2560]{1,0:T(8,128)(2,1)}, bf16[32,2560]{1,0:T(8,128)(2,1)}, u32[]{:S(2)}, u32[]{:S(2)}) collective-permute-start(bf16[32,2560]{1,0:T(8,128)(2,1)} %dynamic-slice_bitcast_fusion.17), channel_id=1, source_target_pairs={{0,16},{1,17},{2,18},{3,19},{4,20},{5,21},{6,22},{7,23},{8,24},{9,... | collective-permute-start | bytes 491528 | tf_op jit(solution)/shard_map/ppermute | solution.py:437
  383.3 34.7 %collective-permute-start.52 = (bf16[32,2560]{1,0:T(8,128)(2,1)}, bf16[32,2560]{1,0:T(8,128)(2,1)}, u32[]{:S(2)}, u32[]{:S(2)}) collective-permute-start(bf16[32,2560]{1,0:T(8,128)(2,1)} %dynamic-slice_bitcast_fusion.18), channel_id=1, source_target_pairs={{0,16},{1,17},{2,18},{3,19},{4,20},{5,21},{6,22},{7,23},{8,24},{9,... | collective-permute-start | bytes 491528 | tf_op jit(solution)/shard_map/ppermute | solution.py:437
  416.4 18.1 %collective-permute-start.55 = (f32[24,1024]{1,0:T(8,128)S(1)}, f32[24,1024]{1,0:T(8,128)S(1)}, u32[]{:S(2)}, u32[]{:S(2)}) collective-permute-start(f32[24,1024]{1,0:T(8,128)S(1)} %add.509), channel_id=1, source_target_pairs={{0,2},{1,3},{2,0},{3,1},{4,6},{5,7},{6,4},{7,5},{8,10},{9,11},{10,... | collective-permute-start | bytes 294920 | tf_op jit(solution)/shard_map/ppermute | solution.py:437
  (172 other events, 1539.1 us)

commit v4 on v3

--- a/solution.py
+++ b/solution.py
@@ -86,10 +86,14 @@
     TT = jnp.concatenate([T0, T1], 1)
     while s < T:
         m = ((r // (2*s)) == (c // (2*s))) & ((r // s) != (c // s))
+        yield
         o = dot(TT, bd(jnp.where(m, N0, 0.0), jnp.where(m, N1, 0.0)), passes=passes)
+        yield
         TT = TT + dot(o, bd(TT[:, :T], TT[:, T:]), passes=passes)
         s *= 2
+    yield
     res = jnp.concatenate([eye, eye], 1) - TT + dot(jnp.concatenate([N0, N1], 1), bd(TT[:, :T], TT[:, T:]))
+    yield
     return TT + dot(TT, bd(res[:, :T], res[:, T:]), passes=1)
 
 def fwd_core(r_, kx, vx, ow, oa, ov, og, first, par, pA=3, pI=1, pO=3):
@@ -98,21 +102,29 @@
     at = -kk * B; rt = r_ * G; bt = kk * ag * S; kt = km * S
     Q = jnp.concatenate([at, rt], 0); Kf = jnp.concatenate([bt, kt], 0)
     Q0, Q1 = halves(Q, h0)
+    yield
     A0 = dot(Q0, Kf, 1, 1, pA); A1 = dot(Q1, Kf, 1, 1, pA)
+    yield
     st = r > c; inc = r >= c
     def msk(A):
         return (jnp.where(st, A[:T, :T], 0.0), jnp.where(st, A[:T, T:], 0.0),
                 jnp.where(inc, A[T:, :T], 0.0), jnp.where(inc, A[T:, T:], 0.0))
     ab0, ak0, rb0, rk0 = msk(A0); ab1, ak1, rb1, rk1 = msk(A1)
-    TT = inverse(ab0, ab1, K, pI)
+    TT = yield from inverse(ab0, ab1, K, pI)
+    yield
     v0, v1 = halves(v2, h0)
     Pm = dot(jnp.concatenate([ak0, ak1], 1), jnp.concatenate([v0, v1], 0), passes=pO)
+    yield
     U = dot(TT, jnp.concatenate(halves(Pm, h0), 0), passes=pO)
+    yield
     u0, u1 = halves(U, h0)
     Y = dot(jnp.concatenate([rb0, rk0, rb1, rk1], 1), jnp.concatenate([u0, v0, u1, v1], 0), passes=pO)
+    yield
     mean = head_sum(Y, J) * (1/64)
+    yield
     cy = Y - mean
     rstd = lax.rsqrt(head_sum(cy * cy, J) * (1/64) + 4.0)
+    yield
     bonus, gain, bias = par[2:3], par[6:7], par[7:8]
     bs = head_sum(r_ * km * bonus, J)
     out = (cy * rstd * gain + bias + bs * v2) * og
@@ -123,51 +135,72 @@
     dk0, dk1, bonus, db, sq0, sq1, gain, bias = (par[i:i+1] for i in range(8))
     sg, ld, G, S, B, ag, vg, v2, kfac, km, n, kk = prep(r_, kx, vx, ow, oa, ov, first, par, K)
     at = -kk * B; rt = r_ * G; bt = kk * ag * S; kt = km * S
+    yield
     mean = head_sum(Y, J) * (1/64)
+    yield
     cy = Y - mean
     rstd = lax.rsqrt(head_sum(cy * cy, J) * (1/64) + 4.0)
+    yield
     gn = cy * rstd
     bs = head_sum(r_ * km * bonus, J)
     g_og = gg * (gn * gain + bias + bs * v2)
     gi = gg * og
     g_gn = gi * gain
     gY = rstd * (g_gn - head_sum(g_gn, J) * (1/64) - gn * (head_sum(g_gn * gn, J) * (1/64)))
+    yield
     g_bs = head_sum(gi * v2, J)
+    yield
     Q = jnp.concatenate([at, rt], 0); Kf = jnp.concatenate([bt, kt], 0)
     Q0, Q1 = halves(Q, h0)
-    At0 = dot(Kf, Q0, 1, 1, pA); At1 = dot(Kf, Q1, 1, 1, pA)
+    At0 = dot(Kf, Q0, 1, 1, pA)
+    yield
+    At1 = dot(Kf, Q1, 1, 1, pA)
+    yield
     st = r < c; inc = r <= c
     akT = jnp.concatenate([jnp.where(st, At0[T:, :T], 0.0), jnp.where(st, At1[T:, :T], 0.0)], 1)
     inc2 = jnp.concatenate([inc, inc], 0)
     rT = jnp.concatenate([jnp.where(inc2, At0[:, T:], 0.0), jnp.where(inc2, At1[:, T:], 0.0)], 1)
+    yield
     gy0, gy1 = halves(gY, h0)
     dUV = dot(rT, jnp.concatenate([gy0, gy1], 0), passes=pW)
+    yield
     dU, dV = dUV[:T], dUV[T:]
     R = dot(TT, dU, 0, 0, pW)
+    yield
     W = jnp.where(h0, R[:T], R[T:])
     w0, w1 = halves(W, h0)
     dV = dV + dot(akT, jnp.concatenate([w0, w1], 0), passes=pW)
+    yield
     X = jnp.concatenate([U, v2], 0)
     Yg0 = jnp.concatenate([w0, gy0], 0); Yg1 = jnp.concatenate([w1, gy1], 0)
     r2, c2 = iota((2*T, 2*T), 0), iota((2*T, 2*T), 1)
     keep = ((r2 & 127) > (c2 & 127)) | ((r2 >= T) & ((r2 & 127) == (c2 & 127)))
     keepT = ((r2 & 127) < (c2 & 127)) | ((c2 >= T) & ((r2 & 127) == (c2 & 127)))
+    yield
     dA0 = jnp.where(keep, dot(Yg0, X, 1, 1, pD), 0.0)
+    yield
     dA1 = jnp.where(keep, dot(Yg1, X, 1, 1, pD), 0.0)
+    yield
     dT0 = jnp.where(keepT, dot(X, Yg0, 1, 1, pD), 0.0)
+    yield
     dT1 = jnp.where(keepT, dot(X, Yg1, 1, 1, pD), 0.0)
+    yield
     K0, K1 = halves(Kf, h0)
     dQ = dot(jnp.concatenate([dA0, dA1], 1), jnp.concatenate([K0, K1], 0), passes=pD)
+    yield
     dK = dot(jnp.concatenate([dT0, dT1], 1), jnp.concatenate([Q0, Q1], 0), passes=pD)
+    yield
     da_, dr_ = dQ[:T], dQ[T:]; db_, dk_ = dK[:T], dK[T:]
     e = dr_ * rt - db_ * bt - dk_ * kt
     f = da_ * at
+    yield
     g_ld = ones_dot(up, e + f) - f
     g_kk = db_ * S * ag - da_ * B
     g_b = db_ * S
     g_km = g_bs * r_ * bonus + dk_ * S
     g_r = g_bs * km * bonus + dr_ * G
     g_ag = g_b * kk + g_km * kx * dk1
+    yield
     g_c = n * (g_kk - kk * head_sum(g_kk * kk, J))
     g_kx = g_km * kfac + g_c * dk0
     g_v2 = gi * bs + dV
@@ -176,29 +209,47 @@
     g_ov = g_first * (1.0 - vg) * (first - vx)
     g_oa = g_ag * ag * (1.0 - ag)
     g_ow = g_ld * ld * (1.0 - sg)
+    yield
     def cs(x): return jnp.sum(x, 0, keepdims=True)
     pg = jnp.concatenate([cs(g_c * kx), cs(g_km * kx * (ag - 1.0)), cs(g_bs * r_ * km),
                           cs(g_ow), cs(g_oa), cs(g_ov), cs(gi * gn), cs(gi)], 0)
     return g_r, g_kx, g_vx, g_ow, g_oa, g_ov, g_og, g_first, pg
 
 
-def fwd_kernel(*refs):
-    ins, par, outs = refs[:8], refs[8], refs[9:]
+def in_step(parts):
+    results, live = [None] * len(parts), list(range(len(parts)))
+    while live:
+        for i in list(live):
+            try:
+                next(parts[i])
+            except StopIteration as end:
+                results[i] = end.value
+                live.remove(i)
+    return results
+
+
+def two_seqs(ins, par, saved, core):
+    work = []
     for q in range(2):
         rows = pl.ds(q * T, T)
         vals = [ref[rows, :] for ref in ins]
-        res = fwd_core(*vals[:7], vals[7].astype(f32), par[...])
+        work.append(core(*vals[:7], vals[7].astype(f32), par[...], *[ref[rows, :] for ref in saved]))
+    return in_step(work)
+
+
+def fwd_kernel(*refs):
+    outs = refs[9:]
+    for q, res in enumerate(two_seqs(refs[:8], refs[8], [], fwd_core)):
+        rows = pl.ds(q * T, T)
         outs[0][rows, :] = res[0].astype(bf16)
         for ref, val in zip(outs[1:], res[1:]):
             ref[rows, :] = val
 
 
 def bwd_kernel(*refs):
-    ins, par, saved, outs = refs[:8], refs[8], refs[9:13], refs[13:]
-    for q in range(2):
+    outs = refs[13:]
+    for q, res in enumerate(two_seqs(refs[:8], refs[8], refs[9:13], bwd_core)):
         rows = pl.ds(q * T, T)
-        vals = [ref[rows, :] for ref in ins]
-        res = bwd_core(*vals[:7], vals[7].astype(f32), par[...], *[ref[rows, :] for ref in saved])
         for ref, val in zip(outs[:8], res[:8]):
             ref[rows, :] = val.astype(bf16)
         outs[8][pl.ds(q * 8, 8), :] = res[8]

time: 460 us -> 459 us (level)
  waiting for transfers between devices: 112 us -> 142 us
  Pallas kernels: 126 us -> 98.4 us
    ppermute x65, waiting for transfers between devices: 112 us -> 142 us  [swap(): return lax.ppermute(x, 'dp', [(i, i ^ bit) for i in range(n)])]
    pallas_call x4, Pallas kernels: 51.9 us -> 30.8 us  [mixer_fwd(): pl.pallas_call(body, grid=(seqs // 2, pairs // 4), in_specs=[tile] * 8 +...]
    pallas_call x4, Pallas kernels: 44.7 us -> 38.3 us  [mixer_bwd(): pl.pallas_call(body, grid_spec=pltpu.PrefetchScalarGridSpec(num_scalar_pr...]
  transfers between devices with their start and end apart: 65 -> 65, of which waited for: 27 -> 30; matrix products, arithmetic and copies ran while one was open for 24% -> 24% of each run, Pallas kernels for 24% -> 18%
where the time goes in v4:
time: 459 us; the launch traced here: 452 us
  waiting for transfers between devices  142 us (31%)
  Pallas kernels  98.4 us (21%)
  other arithmetic  64.1 us (14%)
  starting transfers between devices  63.2 us (14%)
  local copies, waits for them, and re-layouts  47.9 us (10%)
  matrix products  33.4 us (7%)
    ppermute x65, waiting for transfers between devices, swap(): return lax.ppermute(x, 'dp', [(i, i ^ bit) for i in range(n)])  142 us
    ppermute x65, starting transfers between devices, swap(): return lax.ppermute(x, 'dp', [(i, i ^ bit) for i in range(n)])  63.2 us
    pallas_call x4, Pallas kernels, mixer_bwd(): pl.pallas_call(body, grid_spec=pltpu.PrefetchScalarGridSpec(num_scalar_pr...  38.3 us
    dot_general x49, matrix products, dn(): lax.dot_general(x, y, (((cx,), (cy,)), ((), ())), preferred_element_type=...  33.4 us
    pallas_call x4, Pallas kernels, mixer_fwd(): pl.pallas_call(body, grid=(seqs // 2, pairs // 4), in_specs=[tile] * 8 +...  30.8 us
    pallas_call x2, Pallas kernels, ffn_half(): pl.pallas_call(ffn_kernel, grid=(units // FFN_BLOCK,), in_specs=[tall, pl...  17.3 us
    convert_element_type x25, other arithmetic, add(): return (a.astype(f32) + b.astype(f32)).astype(bf16)  16.1 us
    select_n x26, other arithmetic, join(): jnp.where(mine == 0, jnp.stack([a, b], axis), jnp.stack([b, a], axis))  15.9 us
  transfers between devices with their start and end apart: 65, of which 30 were waited for; matrix products, arithmetic and copies ran while one was open for 24% of the time, Pallas kernels for 18%

profile of v4, /device:TPU:0, one launch (start us, length us, event | category | flops | bytes accessed | tf_op | source)
XLA Modules:
  0.0 452.5 jit_solution(10297479193050585479)
XLA Ops:
  11.9 8.7 %collective-permute-done.4 = bf16[64,896]{1,0:T(8,128)(2,1)S(1)} collective-permute-done((bf16[64,896]{1,0:T(8,128)(2,1)S(1)}, bf16[64,896]{1,0:T(8,128)(2,1)S(1)}, u32[]{:S(2)}, u32[]{:S(2)}) %collective-permute-start.4) | collective-permute-done | bytes 114720 | tf_op jit(solution)/shard_map/ppermute | solution.py:488
  23.9 5.3 %collective-permute-done.5 = bf16[2,64,896]{2,1,0:T(8,128)(2,1)S(1)} collective-permute-done((bf16[2,64,896]{2,1,0:T(8,128)(2,1)S(1)}, bf16[2,64,896]{2,1,0:T(8,128)(2,1)S(1)}, u32[]{:S(2)}, u32[]{:S(2)}) %collective-permute-start.5) | collective-permute-done | bytes 229408 | tf_op jit(solution)/shard_map/ppermute | solution.py:488
  29.3 4.3 collective-permute-done.2
  39.3 13.5 %collective-permute-done.9 = bf16[64,2560]{1,0:T(8,128)(2,1)S(1)} collective-permute-done((bf16[64,2560]{1,0:T(8,128)(2,1)S(1)}, bf16[64,2560]{1,0:T(8,128)(2,1)S(1)}, u32[]{:S(2)}, u32[]{:S(2)}) %collective-permute-start.9) | collective-permute-done | bytes 327712 | tf_op jit(solution)/shard_map/ppermute | solution.py:488
  61.3 14.4 %collective-permute-done.13 = bf16[128,1024]{1,0:T(8,128)(2,1)S(1)} collective-permute-done((bf16[128,1024]{1,0:T(8,128)(2,1)S(1)}, bf16[128,1024]{1,0:T(8,128)(2,1)S(1)}, u32[]{:S(2)}, u32[]{:S(2)}) %collective-permute-start.13) | collective-permute-done | bytes 262176 | tf_op jit(solution)/shard_map/ppermute | solution.py:488
  98.1 4.4 collective-permute-done.15
  111.9 7.5 %mixer_fwd.4 = (bf16[256,1024]{1,0:T(8,128)(2,1)S(1)}, f32[2048,256]{1,0:T(8,128)S(1)}, f32[256,1024]{1,0:T(8,128)S(1)}, f32[256,1024]{1,0:T(8,128)S(1)}) custom-call(f32[256,1024]{1,0:T(8,128)S(1)} %convolution_add_fusion.5.refs_0_.refs_1_, f32[256,1024]{1,0:T(8,128)S(1)} %convolution_add_fusion.4.refs_1_.refs_2_, ...), custom_call_target="tpu_custom_call" | custom-call | flops 10000000000 | bytes 10000000 | tf_op jit(solution)/shard_map/mixer_fwd/pallas_call | solution.py:277
  123.1 4.4 collective-permute-done.18
  131.2 8.1 %mixer_fwd.5 = (bf16[256,1024]{1,0:T(8,128)(2,1)S(1)}, f32[2048,256]{1,0:T(8,128)S(1)}, f32[256,1024]{1,0:T(8,128)S(1)}, f32[256,1024]{1,0:T(8,128)S(1)}) custom-call(f32[256,1024]{1,0:T(8,128)S(1)} %convolution_add_fusion.5.refs_0_.refs_1_, ...), custom_call_target="tpu_custom_call", output_to_operand_aliasing={{0}: (9, {}), {1}: (10, {}), {2}: (11, {}), {3}: (12, {})} | custom-call | flops 10000000000 | bytes 10000000 | tf_op jit(solution)/shard_map/mixer_fwd/pallas_call | solution.py:277
  139.6 7.6 %mixer_fwd.6 = (bf16[256,1024]{1,0:T(8,128)(2,1)S(1)}, f32[2048,256]{1,0:T(8,128)S(1)}, f32[256,1024]{1,0:T(8,128)S(1)}, f32[256,1024]{1,0:T(8,128)S(1)}) custom-call(f32[256,1024]{1,0:T(8,128)S(1)} %convolution_add_fusion.5.refs_0_.refs_1_, ...), custom_call_target="tpu_custom_call", output_to_operand_aliasing={{0}: (9, {}), {1}: (10, {}), {2}: (11, {}), {3}: (12, {})} | custom-call | flops 10000000000 | bytes 10000000 | tf_op jit(solution)/shard_map/mixer_fwd/pallas_call | solution.py:277
  147.2 7.6 %mixer_fwd.7 = (bf16[256,1024]{1,0:T(8,128)(2,1)S(1)}, f32[2048,256]{1,0:T(8,128)S(1)}, f32[256,1024]{1,0:T(8,128)S(1)}, f32[256,1024]{1,0:T(8,128)S(1)}) custom-call(f32[256,1024]{1,0:T(8,128)S(1)} %convolution_add_fusion.5.refs_0_.refs_1_, ...), custom_call_target="tpu_custom_call", output_to_operand_aliasing={{0}: (9, {}), {1}: (10, {}), {2}: (11, {}), {3}: (12, {})} | custom-call | flops 10000000000 | bytes 10000000 | tf_op jit(solution)/shard_map/mixer_fwd/pallas_call | solution.py:277
  154.9 19.6 %collective-permute-done.20 = bf16[2,2,2,128,1024]{4,3,0,1,2:T(8,128)(2,1)} collective-permute-done((bf16[2,2,2,128,1024]{4,3,0,1,2:T(8,128)(2,1)S(1)}, bf16[2,2,2,128,1024]{4,3,0,1,2:T(8,128)(2,1)}, u32[]{:S(2)}, u32[]{:S(2)}) %collective-permute-start.20) | collective-permute-done | bytes 2097184 | tf_op jit(solution)/shard_map/ppermute | solution.py:488
  174.5 12.8 %collective-permute-done.19 = bf16[2,2,2,64,2560]{4,3,2,1,0:T(8,128)(2,1)S(1)} collective-permute-done((bf16[2,2,2,64,2560]{4,3,2,1,0:T(8,128)(2,1)S(1)}, bf16[2,2,2,64,2560]{4,3,2,1,0:T(8,128)(2,1)S(1)}, u32[]{:S(2)}, u32[]{:S(2)}) %collective-permute-start.19) | collective-permute-done | bytes 2621472 | tf_op jit(solution)/shard_map/ppermute | solution.py:488
  205.5 6.7 %ffn_half.2 = (bf16[256,2048]{1,0:T(8,128)(2,1)S(1)}, bf16[256,2048]{1,0:T(8,128)(2,1)S(1)}, f32[256,1024]{1,0:T(8,128)S(1)}) custom-call(bf16[256,1024]{1,0:T(8,128)(2,1)S(1)} %add_convert_fusion.1.xc, bf16[1024,256]{1,0:T(8,128)(2,1)S(1)} %copy-done.16, bf16[256,1024]{1,0:T(8,128)(2,1)S(1)} %fusion.22.gf, bf16[1024,2560]{1,0:T(8,128)(2,1)} %bitcast.91.wk, ...), custom_call_target="tpu_custom_call" | custom-call | flops 5000000000 | bytes 10000000 | tf_op jit(solution)/shard_map/ffn_half/pallas_call | solution.py:363
  212.9 10.5 %ffn_half.3 = (bf16[256,2048]{1,0:T(8,128)(2,1)S(1)}, bf16[256,2048]{1,0:T(8,128)(2,1)}, f32[256,1024]{1,0:T(8,128)S(1)}, bf16[2048,1024]{1,0:T(8,128)(2,1)}, bf16[1024,2048]{1,0:T(8,128)(2,1)}) custom-call(bf16[256,1024]{1,0:T(8,128)(2,1)S(1)} %add_convert_fusion.1.xc, bf16[1024,256]{1,0:T(8,128)(2,1)S(1)} %copy-done.16, bf16[256,1024]{1,0:T(8,128)(2,1)S(1)} %fusion.22.gf, ...), custom_call_target="tpu_custom_call" | custom-call | flops 5000000000 | bytes 10000000 | tf_op jit(solution)/shard_map/ffn_half/pallas_call | solution.py:363
  234.3 4.3 collective-permute-done.26.got
  238.7 5.8 %ffn_grads.1 = (bf16[2048,1024]{1,0:T(8,128)(2,1)S(1)}, bf16[1024,2560]{1,0:T(8,128)(2,1)S(1)}) custom-call(bf16[1024,256]{1,0:T(8,128)(2,1)S(1)} %copy-done.17, bf16[256,1024]{1,0:T(8,128)(2,1)S(1)} %fusion.22.gf, bf16[256,2048]{1,0:T(8,128)(2,1)S(1)} %copy-done.21, bf16[256,2048]{1,0:T(8,128)(2,1)S(1)} %copy-done.26, ...), custom_call_target="tpu_custom_call" | custom-call | flops 5000000000 | bytes 10000000 | tf_op jit(solution)/shard_map/ffn_grads/pallas_call | solution.py:385
  255.8 9.6 %mixer_bwd.4 = (bf16[256,1024]{1,0:T(8,128)(2,1)S(1)}, bf16[256,1024]{1,0:T(8,128)(2,1)S(1)}, bf16[256,1024]{1,0:T(8,128)(2,1)S(1)}, bf16[256,1024]{1,0:T(8,128)...) custom-call(s32[1]{0:T(128)} %bitcast.96.refs_0_, ...), custom_call_target="tpu_custom_call" | custom-call | flops 10000000000 | bytes 10000000 | tf_op jit(solution)/shard_map/mixer_bwd/pallas_call | solution.py:308
  265.4 7.9 %collective-permute-done.27 = bf16[2,2,2,64,1024]{4,3,0,1,2:T(8,128)(2,1)S(1)} collective-permute-done((bf16[2,2,2,64,1024]{4,3,0,1,2:T(8,128)(2,1)S(1)}, bf16[2,2,2,64,1024]{4,3,0,1,2:T(8,128)(2,1)S(1)}, u32[]{:S(2)}, u32[]{:S(2)}) %collective-permute-start.27) | collective-permute-done | bytes 1048608 | tf_op jit(solution)/shard_map/ppermute | solution.py:488
  274.5 9.3 %mixer_bwd.5 = (bf16[256,1024]{1,0:T(8,128)(2,1)S(1)}, bf16[256,1024]{1,0:T(8,128)(2,1)S(1)}, bf16[256,1024]{1,0:T(8,128)(2,1)S(1)}, bf16[256,1024]{1,0:T(8,128)...) custom-call(s32[1]{0:T(128)} %bitcast.96.refs_0_, ...), custom_call_target="tpu_custom_call", output_to_operand_aliasing={{0}: (14, {}), {1}: (15, {}), {2}: (16, {}), {3}: (17, {}),... | custom-call | flops 10000000000 | bytes 10000000 | tf_op jit(solution)/shard_map/mixer_bwd/pallas_call | solution.py:308
  291.8 9.9 %mixer_bwd.6 = (bf16[256,1024]{1,0:T(8,128)(2,1)S(1)}, bf16[256,1024]{1,0:T(8,128)(2,1)S(1)}, bf16[256,1024]{1,0:T(8,128)(2,1)S(1)}, bf16[256,1024]{1,0:T(8,128)...) custom-call(s32[1]{0:T(128)} %bitcast.96.refs_0_, ...), custom_call_target="tpu_custom_call", output_to_operand_aliasing={{0}: (14, {}), {1}: (15, {}), {2}: (16, {}), {3}: (17, {}),... | custom-call | flops 10000000000 | bytes 10000000 | tf_op jit(solution)/shard_map/mixer_bwd/pallas_call | solution.py:308
  304.8 7.4 %collective-permute-done.30 = bf16[2,2,64,1024]{3,2,0,1:T(8,128)(2,1)} collective-permute-done((bf16[2,2,64,1024]{3,2,0,1:T(8,128)(2,1)}, bf16[2,2,64,1024]{3,2,0,1:T(8,128)(2,1)}, u32[]{:S(2)}, u32[]{:S(2)}) %collective-permute-start.30) | collective-permute-done | bytes 524320 | tf_op jit(solution)/shard_map/ppermute | solution.py:488
  323.5 9.5 %mixer_bwd.7 = (bf16[256,1024]{1,0:T(8,128)(2,1)S(1)}, bf16[256,1024]{1,0:T(8,128)(2,1)S(1)}, bf16[256,1024]{1,0:T(8,128)(2,1)S(1)}, bf16[256,1024]{1,0:T(8,128)...) custom-call(s32[1]{0:T(128)} %bitcast.96.refs_0_, ...), custom_call_target="tpu_custom_call", output_to_operand_aliasing={{0}: (14, {}), {1}: (15, {}), {2}: (16, {}), {3}: (17, {}),... | custom-call | flops 10000000000 | bytes 10000000 | tf_op jit(solution)/shard_map/mixer_bwd/pallas_call | solution.py:308
  444.0 5.3 %collective-permute-done.58 = f32[24,1024]{1,0:T(8,128)S(1)} collective-permute-done((f32[24,1024]{1,0:T(8,128)S(1)}, f32[24,1024]{1,0:T(8,128)S(1)}, u32[]{:S(2)}, u32[]{:S(2)}) %collective-permute-start.58) | collective-permute-done | bytes 98336 | tf_op jit(solution)/shard_map/ppermute | solution.py:488
  (659 shorter events, 244.0 us)
Async XLA Ops:
  33.6 19.2 %collective-permute-start.7 = (bf16[2,2,64,1024]{3,2,1,0:T(8,128)(2,1)S(1)}, bf16[2,2,64,1024]{3,2,1,0:T(8,128)(2,1)S(1)}, u32[]{:S(2)}, u32[]{:S(2)}) collective-permute-start(bf16[2,2,64,1024]{3,2,1,0:T(8,128)(2,1)S(1)} %maximum_select_fusion.20), channel_id=1, source_target_pairs={{0,2},{1,3},{2,0},{3,1},{4,6},{5,7},{6,4},{7,5},{8,10},{9,11},{10,... | collective-permute-start | bytes 1572872 | tf_op jit(solution)/shard_map/ppermute | solution.py:488
  54.3 22.2 %collective-permute-start.11 = (bf16[2,2,2,64,896]{4,3,1,0,2:T(8,128)(2,1)S(1)}, bf16[2,2,2,64,896]{4,3,1,0,2:T(8,128)(2,1)S(1)}, u32[]{:S(2)}, u32[]{:S(2)}) collective-permute-start(bf16[2,2,2,64,896]{4,3,1,0,2:T(8,128)(2,1)S(1)} %maximum_select_fusion.17), channel_id=1, source_target_pairs={{0,2},{1,3},{2,0},{3,1},{4,6},{5,7},{6,4},{7,5},{8,10},{9,11},{10,... | collective-permute-start | bytes 2752520 | tf_op jit(solution)/shard_map/ppermute | solution.py:488
  55.0 23.9 %collective-permute-start.10 = (bf16[2,2,2,64,1024]{4,3,2,1,0:T(8,128)(2,1)S(1)}, bf16[2,2,2,64,1024]{4,3,2,1,0:T(8,128)(2,1)}, u32[]{:S(2)}, u32[]{:S(2)}) collective-permute-start(bf16[2,2,2,64,1024]{4,3,2,1,0:T(8,128)(2,1)S(1)} %maximum_select_fusion.11), channel_id=1, source_target_pairs={{0,4},{1,5},{2,6},{3,7},{4,0},{5,1},{6,2},{7,3},{8,12},{9,13},{10,... | collective-permute-start | bytes 3145736 | tf_op jit(solution)/shard_map/ppermute | solution.py:488
  55.7 20.8 %collective-permute-start.12 = (bf16[2,64,2560]{2,1,0:T(8,128)(2,1)S(1)}, bf16[2,64,2560]{2,1,0:T(8,128)(2,1)S(1)}, u32[]{:S(2)}, u32[]{:S(2)}) collective-permute-start(bf16[2,64,2560]{2,1,0:T(8,128)(2,1)S(1)} %maximum_select_fusion.18), channel_id=1, source_target_pairs={{0,8},{1,9},{2,10},{3,11},{4,12},{5,13},{6,14},{7,15},{8,0},{9,1},... | collective-permute-start | bytes 1966088 | tf_op jit(solution)/shard_map/ppermute | solution.py:488
  56.5 19.2 %collective-permute-start.13 = (bf16[128,1024]{1,0:T(8,128)(2,1)S(1)}, bf16[128,1024]{1,0:T(8,128)(2,1)S(1)}, u32[]{:S(2)}, u32[]{:S(2)}) collective-permute-start(bf16[128,1024]{1,0:T(8,128)(2,1)S(1)} %copy-done.95), channel_id=1, source_target_pairs={{0,16},{1,17},{2,18},{3,19},{4,20},{5,21},{6,22},{7,23},{8,24},{9,... | collective-permute-start | bytes 786440 | tf_op jit(solution)/shard_map/ppermute | solution.py:488
  92.2 31.0 %collective-permute-start.17 = (bf16[2,2,64,2560]{3,2,1,0:T(8,128)(2,1)S(1)}, bf16[2,2,64,2560]{3,2,1,0:T(8,128)(2,1)S(1)}, u32[]{:S(2)}, u32[]{:S(2)}) collective-permute-start(bf16[2,2,64,2560]{3,2,1,0:T(8,128)(2,1)S(1)} %copy-done.43), channel_id=1, source_target_pairs={{0,2},{1,3},{2,0},{3,1},{4,6},{5,7},{6,4},{7,5},{8,10},{9,11},{10,... | collective-permute-start | bytes 3932168 | tf_op jit(solution)/shard_map/ppermute | solution.py:488
  102.7 24.9 %collective-permute-start.18 = (bf16[2,2,128,1024]{3,2,0,1:T(8,128)(2,1)S(1)}, bf16[2,2,128,1024]{3,2,0,1:T(8,128)(2,1)S(1)}, u32[]{:S(2)}, u32[]{:S(2)}) collective-permute-start(bf16[2,2,128,1024]{3,2,0,1:T(8,128)(2,1)S(1)} %maximum_select_fusion.12), channel_id=1, source_target_pairs={{0,4},{1,5},{2,6},{3,7},{4,0},{5,1},{6,2},{7,3},{8,12},{9,13},{10,... | collective-permute-start | bytes 3145736 | tf_op jit(solution)/shard_map/ppermute | solution.py:488
  127.9 46.6 %collective-permute-start.20 = (bf16[2,2,2,128,1024]{4,3,0,1,2:T(8,128)(2,1)S(1)}, bf16[2,2,2,128,1024]{4,3,0,1,2:T(8,128)(2,1)}, u32[]{:S(2)}, u32[]{:S(2)}) collective-permute-start(bf16[2,2,2,128,1024]{4,3,0,1,2:T(8,128)(2,1)S(1)} %maximum_select_fusion.4), channel_id=1, source_target_pairs={{0,2},{1,3},{2,0},{3,1},{4,6},{5,7},{6,4},{7,5},{8,10},{9,11},{10,... | collective-permute-start | bytes 6291464 | tf_op jit(solution)/shard_map/ppermute | solution.py:488
  129.9 57.4 %collective-permute-start.19 = (bf16[2,2,2,64,2560]{4,3,2,1,0:T(8,128)(2,1)S(1)}, bf16[2,2,2,64,2560]{4,3,2,1,0:T(8,128)(2,1)S(1)}, u32[]{:S(2)}, u32[]{:S(2)}) collective-permute-start(bf16[2,2,2,64,2560]{4,3,2,1,0:T(8,128)(2,1)S(1)} %maximum_select_fusion.2), channel_id=1, source_target_pairs={{0,4},{1,5},{2,6},{3,7},{4,0},{5,1},{6,2},{7,3},{8,12},{9,13},{10,... | collective-permute-start | bytes 7864328 | tf_op jit(solution)/shard_map/ppermute | solution.py:488
  247.3 26.1 %collective-permute-start.27 = (bf16[2,2,2,64,1024]{4,3,0,1,2:T(8,128)(2,1)S(1)}, bf16[2,2,2,64,1024]{4,3,0,1,2:T(8,128)(2,1)S(1)}, u32[]{:S(2)}, u32[]{:S(2)}) collective-permute-start(bf16[2,2,2,64,1024]{4,3,0,1,2:T(8,128)(2,1)S(1)} %dynamic-slice_bitcast_fusion.3), channel_id=1, source_target_pairs={{0,4},{1,5},{2,6},{3,7},{4,0},{5,1},{6,2},{7,3},{8,12},{9,13},{10,... | collective-permute-start | bytes 3145736 | tf_op jit(solution)/shard_map/ppermute | solution.py:488
  248.3 26.2 %collective-permute-start.28 = (bf16[2,2,2,64,1024]{4,3,0,1,2:T(8,128)(2,1)S(1)}, bf16[2,2,2,64,1024]{4,3,0,1,2:T(8,128)(2,1)}, u32[]{:S(2)}, u32[]{:S(2)}) collective-permute-start(bf16[2,2,2,64,1024]{4,3,0,1,2:T(8,128)(2,1)S(1)} %dynamic-slice_bitcast_fusion.2), channel_id=1, source_target_pairs={{0,2},{1,3},{2,0},{3,1},{4,6},{5,7},{6,4},{7,5},{8,10},{9,11},{10,... | collective-permute-start | bytes 3145736 | tf_op jit(solution)/shard_map/ppermute | solution.py:488
  252.0 52.8 %collective-permute-start.31 = (bf16[2,2,2,32,2560]{4,3,0,1,2:T(8,128)(2,1)}, bf16[2,2,2,32,2560]{4,3,0,1,2:T(8,128)(2,1)}, u32[]{:S(2)}, u32[]{:S(2)}) collective-permute-start(bf16[2,2,2,32,2560]{4,3,0,1,2:T(8,128)(2,1)} %dynamic-slice_bitcast_fusion.1), channel_id=1, source_target_pairs={{0,4},{1,5},{2,6},{3,7},{4,0},{5,1},{6,2},{7,3},{8,12},{9,13},{10,... | collective-permute-start | bytes 3932168 | tf_op jit(solution)/shard_map/ppermute | solution.py:488
  253.2 51.6 %collective-permute-start.32 = (bf16[2,2,2,32,2560]{4,3,2,1,0:T(8,128)(2,1)}, bf16[2,2,2,32,2560]{4,3,2,1,0:T(8,128)(2,1)}, u32[]{:S(2)}, u32[]{:S(2)}) collective-permute-start(bf16[2,2,2,32,2560]{4,3,2,1,0:T(8,128)(2,1)} %dynamic-slice_bitcast_fusion), channel_id=1, source_target_pairs={{0,2},{1,3},{2,0},{3,1},{4,6},{5,7},{6,4},{7,5},{8,10},{9,11},{10,... | collective-permute-start | bytes 3932168 | tf_op jit(solution)/shard_map/ppermute | solution.py:488
  288.9 23.4 %collective-permute-start.30 = (bf16[2,2,64,1024]{3,2,0,1:T(8,128)(2,1)}, bf16[2,2,64,1024]{3,2,0,1:T(8,128)(2,1)}, u32[]{:S(2)}, u32[]{:S(2)}) collective-permute-start(bf16[2,2,64,1024]{3,2,0,1:T(8,128)(2,1)} %dynamic-slice_bitcast_fusion.6), channel_id=1, source_target_pairs={{0,4},{1,5},{2,6},{3,7},{4,0},{5,1},{6,2},{7,3},{8,12},{9,13},{10,... | collective-permute-start | bytes 1572872 | tf_op jit(solution)/shard_map/ppermute | solution.py:488
  290.5 22.3 %collective-permute-start.29 = (bf16[2,2,64,1024]{3,2,0,1:T(8,128)(2,1)S(1)}, bf16[2,2,64,1024]{3,2,0,1:T(8,128)(2,1)S(1)}, u32[]{:S(2)}, u32[]{:S(2)}) collective-permute-start(bf16[2,2,64,1024]{3,2,0,1:T(8,128)(2,1)S(1)} %dynamic-slice_bitcast_fusion.7), channel_id=1, source_target_pairs={{0,2},{1,3},{2,0},{3,1},{4,6},{5,7},{6,4},{7,5},{8,10},{9,11},{10,... | collective-permute-start | bytes 1572872 | tf_op jit(solution)/shard_map/ppermute | solution.py:488
  315.3 17.7 %collective-permute-start.37 = (bf16[2,2,32,2560]{3,2,1,0:T(8,128)(2,1)S(1)}, bf16[2,2,32,2560]{3,2,1,0:T(8,128)(2,1)S(1)}, u32[]{:S(2)}, u32[]{:S(2)}) collective-permute-start(bf16[2,2,32,2560]{3,2,1,0:T(8,128)(2,1)S(1)} %dynamic-slice_bitcast_fusion.4), channel_id=1, source_target_pairs={{0,4},{1,5},{2,6},{3,7},{4,0},{5,1},{6,2},{7,3},{8,12},{9,13},{10,... | collective-permute-start | bytes 1966088 | tf_op jit(solution)/shard_map/ppermute | solution.py:488
  322.6 42.9 %collective-permute-start.38 = (bf16[512,1536]{1,0:T(8,128)(2,1)}, bf16[512,1536]{1,0:T(8,128)(2,1)}, u32[]{:S(2)}, u32[]{:S(2)}) collective-permute-start(bf16[512,1536]{1,0:T(8,128)(2,1)} %fusion), channel_id=1, source_target_pairs={{0,4},{1,5},{2,6},{3,7},{4,0},{5,1},{6,2},{7,3},{8,12},{9,13},{10,... | collective-permute-start | bytes 4718600 | tf_op jit(solution)/shard_map/ppermute | solution.py:488
  337.6 19.5 %collective-permute-start.44 = (bf16[1024,288]{0,1:T(8,128)(2,1)S(1)}, bf16[1024,288]{0,1:T(8,128)(2,1)S(1)}, u32[]{:S(2)}, u32[]{:S(2)}) collective-permute-start(bf16[1024,288]{0,1:T(8,128)(2,1)S(1)} %select_convert_fusion), channel_id=1, source_target_pairs={{0,1},{1,0},{2,3},{3,2},{4,5},{5,4},{6,7},{7,6},{8,9},{9,8},{10,11... | collective-permute-start | bytes 1769480 | tf_op jit(solution)/shard_map/ppermute | solution.py:488
  338.7 35.8 %collective-permute-start.43 = (bf16[2,32,2560]{2,1,0:T(8,128)(2,1)}, bf16[2,32,2560]{2,1,0:T(8,128)(2,1)}, u32[]{:S(2)}, u32[]{:S(2)}) collective-permute-start(bf16[2,32,2560]{2,1,0:T(8,128)(2,1)} %dynamic-slice_bitcast_fusion.10), channel_id=1, source_target_pairs={{0,8},{1,9},{2,10},{3,11},{4,12},{5,13},{6,14},{7,15},{8,0},{9,1},... | collective-permute-start | bytes 983048 | tf_op jit(solution)/shard_map/ppermute | solution.py:488
  341.4 33.2 %collective-permute-start.42 = (bf16[2,32,2560]{2,1,0:T(8,128)(2,1)}, bf16[2,32,2560]{2,1,0:T(8,128)(2,1)}, u32[]{:S(2)}, u32[]{:S(2)}) collective-permute-start(bf16[2,32,2560]{2,1,0:T(8,128)(2,1)} %dynamic-slice_bitcast_fusion.11), channel_id=1, source_target_pairs={{0,8},{1,9},{2,10},{3,11},{4,12},{5,13},{6,14},{7,15},{8,0},{9,1},... | collective-permute-start | bytes 983048 | tf_op jit(solution)/shard_map/ppermute | solution.py:488
  343.7 25.0 %collective-permute-start.39 = (bf16[512,1536]{1,0:T(8,128)(2,1)}, bf16[512,1536]{1,0:T(8,128)(2,1)}, u32[]{:S(2)}, u32[]{:S(2)}) collective-permute-start(bf16[512,1536]{1,0:T(8,128)(2,1)} %proj_grad.2), channel_id=1, source_target_pairs={{0,1},{1,0},{2,3},{3,2},{4,5},{5,4},{6,7},{7,6},{8,9},{9,8},{10,11... | collective-permute-start | bytes 4718600 | tf_op jit(solution)/shard_map/ppermute | solution.py:488
  379.7 35.2 %collective-permute-start.53 = (bf16[32,2560]{1,0:T(8,128)(2,1)}, bf16[32,2560]{1,0:T(8,128)(2,1)}, u32[]{:S(2)}, u32[]{:S(2)}) collective-permute-start(bf16[32,2560]{1,0:T(8,128)(2,1)} %dynamic-slice_bitcast_fusion.17), channel_id=1, source_target_pairs={{0,16},{1,17},{2,18},{3,19},{4,20},{5,21},{6,22},{7,23},{8,24},{9,... | collective-permute-start | bytes 491528 | tf_op jit(solution)/shard_map/ppermute | solution.py:488
  382.5 33.2 %collective-permute-start.52 = (bf16[32,2560]{1,0:T(8,128)(2,1)}, bf16[32,2560]{1,0:T(8,128)(2,1)}, u32[]{:S(2)}, u32[]{:S(2)}) collective-permute-start(bf16[32,2560]{1,0:T(8,128)(2,1)} %dynamic-slice_bitcast_fusion.18), channel_id=1, source_target_pairs={{0,16},{1,17},{2,18},{3,19},{4,20},{5,21},{6,22},{7,23},{8,24},{9,... | collective-permute-start | bytes 491528 | tf_op jit(solution)/shard_map/ppermute | solution.py:488
  414.9 18.1 %collective-permute-start.55 = (f32[24,1024]{1,0:T(8,128)S(1)}, f32[24,1024]{1,0:T(8,128)S(1)}, u32[]{:S(2)}, u32[]{:S(2)}) collective-permute-start(f32[24,1024]{1,0:T(8,128)S(1)} %add.509), channel_id=1, source_target_pairs={{0,2},{1,3},{2,0},{3,1},{4,6},{5,7},{6,4},{7,5},{8,10},{9,11},{10,... | collective-permute-start | bytes 294920 | tf_op jit(solution)/shard_map/ppermute | solution.py:488
  (172 other events, 1496.4 us)

commit v5 on v4

--- a/solution.py
+++ b/solution.py
@@ -341,7 +341,7 @@
         gx[...] += g
 
 
-FFN_BLOCK = 512
+FFN_BLOCK = 1024
 
 
 def ffn_params(name, flops=5 * 10**9, moved=10**7):
@@ -448,6 +448,29 @@
         **ffn_params("proj_grad", 3 * 10**8, 10**6),
     )(*gs, *xs, *gots)
     return res if split else res[0]
+
+
+def small_kernel(core, gp, mix, gain, bias, early, out):
+    half = out.shape[1] // 2
+    out[:8, :] = gp[...]
+    out[16:, :] = early[...]
+    for ref, at in ((mix, 8), (gain, 14), (bias, 15)):
+        n = ref.shape[0]
+        a, b = ref[:, :half], ref[:, half:]
+        turn = jnp.full((n, half), core[0], jnp.int32) == 1
+        out[at:at + n, :half] = jnp.where(turn, b, a)
+        out[at:at + n, half:] = jnp.where(turn, a, b)
+
+
+def small_rows(core, gp, mix, gain, bias, early):
+    vmem = pl.BlockSpec(memory_space=pltpu.VMEM)
+    return pl.pallas_call(
+        small_kernel,
+        in_specs=[pl.BlockSpec(memory_space=pltpu.SMEM)] + [vmem] * 5,
+        out_specs=vmem,
+        out_shape=jax.ShapeDtypeStruct((24, gp.shape[1]), f32),
+        name="small_rows",
+    )(core.reshape(1), gp, mix, gain, bias, early)
 
 
 def layer_norm(x, gain, bias):
@@ -771,9 +794,7 @@
         l_got, k_got = sum_send(d_low, ONE[1]), send(d_key, 3)
     g_x, g_mix_t, g_gain_t, g_bias_t = pull_front(g_xs)
     g_x = g_mixed + by_core(g_x)
-    g_mix_t, g_gain_t, g_bias_t = by_core(g_mix_t), by_core(g_gain_t), by_core(g_bias_t)
-    d_small = jnp.concatenate(
-        [gp, jnp.concatenate([g_mix_t, g_gain_t[None], g_bias_t[None]], 0), early], 0)
+    d_small = small_rows(core, gp, g_mix_t, g_gain_t[None], g_bias_t[None], early)
     if small_slice:
         d_small, p_got, l_got, hidden, hidden_far = tie(d_small, p_got, l_got, hidden, hidden_far)
         d_proj, d_low = sum_take(d_proj, p_got, TAIL[0]), sum_take(d_low, l_got, ONE[1])

time: 459 us -> 458 us (level)
  local copies, waits for them, and re-layouts: 47.9 us -> 43.2 us
    unnamed x273 -> x269, local copies, waits for them, and re-layouts: 13.1 us -> 13 us
  transfers between devices with their start and end apart: 65 -> 65, of which waited for: 30 -> 32; matrix products, arithmetic and copies ran while one was open for 24% -> 23% of each run, Pallas kernels for 18% -> 18%
where the time goes in v5:
time: 458 us; the launch traced here: 452 us
  waiting for transfers between devices  146 us (32%)
  Pallas kernels  98.8 us (22%)
  starting transfers between devices  63.9 us (14%)
  other arithmetic  62.7 us (14%)
  local copies, waits for them, and re-layouts  43.2 us (9%)
  matrix products  33.4 us (7%)
    ppermute x65, waiting for transfers between devices, swap(): return lax.ppermute(x, 'dp', [(i, i ^ bit) for i in range(n)])  146 us
    ppermute x65, starting transfers between devices, swap(): return lax.ppermute(x, 'dp', [(i, i ^ bit) for i in range(n)])  63.9 us
    pallas_call x4, Pallas kernels, mixer_bwd(): pl.pallas_call(body, grid_spec=pltpu.PrefetchScalarGridSpec(num_scalar_pr...  38 us
    dot_general x49, matrix products, dn(): lax.dot_general(x, y, (((cx,), (cy,)), ((), ())), preferred_element_type=...  33.4 us
    pallas_call x4, Pallas kernels, mixer_fwd(): pl.pallas_call(body, grid=(seqs // 2, pairs // 4), in_specs=[tile] * 8 +...  30.8 us
    pallas_call x2, Pallas kernels, ffn_half(): pl.pallas_call(ffn_kernel, grid=(units // FFN_BLOCK,), in_specs=[tall, pl...  16.7 us
    select_n x26, other arithmetic, join(): jnp.where(mine == 0, jnp.stack([a, b], axis), jnp.stack([b, a], axis))  16 us
    convert_element_type x25, other arithmetic, add(): return (a.astype(f32) + b.astype(f32)).astype(bf16)  15.9 us
  transfers between devices with their start and end apart: 65, of which 32 were waited for; matrix products, arithmetic and copies ran while one was open for 23% of the time, Pallas kernels for 18%

profile of v5, /device:TPU:0, one launch (start us, length us, event | category | flops | bytes accessed | tf_op | source)
XLA Modules:
  0.0 451.8 jit_solution(9856585843735017856)
XLA Ops:
  11.9 8.7 %collective-permute-done.4 = bf16[64,896]{1,0:T(8,128)(2,1)S(1)} collective-permute-done((bf16[64,896]{1,0:T(8,128)(2,1)S(1)}, bf16[64,896]{1,0:T(8,128)(2,1)S(1)}, u32[]{:S(2)}, u32[]{:S(2)}) %collective-permute-start.4) | collective-permute-done | bytes 114720 | tf_op jit(solution)/shard_map/ppermute | solution.py:511
  23.9 5.3 %collective-permute-done.5 = bf16[2,64,896]{2,1,0:T(8,128)(2,1)S(1)} collective-permute-done((bf16[2,64,896]{2,1,0:T(8,128)(2,1)S(1)}, bf16[2,64,896]{2,1,0:T(8,128)(2,1)S(1)}, u32[]{:S(2)}, u32[]{:S(2)}) %collective-permute-start.5) | collective-permute-done | bytes 229408 | tf_op jit(solution)/shard_map/ppermute | solution.py:511
  39.3 13.5 %collective-permute-done.9 = bf16[64,2560]{1,0:T(8,128)(2,1)S(1)} collective-permute-done((bf16[64,2560]{1,0:T(8,128)(2,1)S(1)}, bf16[64,2560]{1,0:T(8,128)(2,1)S(1)}, u32[]{:S(2)}, u32[]{:S(2)}) %collective-permute-start.9) | collective-permute-done | bytes 327712 | tf_op jit(solution)/shard_map/ppermute | solution.py:511
  61.3 14.4 %collective-permute-done.13 = bf16[128,1024]{1,0:T(8,128)(2,1)S(1)} collective-permute-done((bf16[128,1024]{1,0:T(8,128)(2,1)S(1)}, bf16[128,1024]{1,0:T(8,128)(2,1)S(1)}, u32[]{:S(2)}, u32[]{:S(2)}) %collective-permute-start.13) | collective-permute-done | bytes 262176 | tf_op jit(solution)/shard_map/ppermute | solution.py:511
  97.5 4.5 collective-permute-done.15
  111.3 7.5 %mixer_fwd.4 = (bf16[256,1024]{1,0:T(8,128)(2,1)S(1)}, f32[2048,256]{1,0:T(8,128)S(1)}, f32[256,1024]{1,0:T(8,128)S(1)}, f32[256,1024]{1,0:T(8,128)S(1)}) custom-call(f32[256,1024]{1,0:T(8,128)S(1)} %convolution_add_fusion.5.refs_0_.refs_1_, f32[256,1024]{1,0:T(8,128)S(1)} %convolution_add_fusion.4.refs_1_.refs_2_, ...), custom_call_target="tpu_custom_call" | custom-call | flops 10000000000 | bytes 10000000 | tf_op jit(solution)/shard_map/mixer_fwd/pallas_call | solution.py:277
  122.6 4.4 collective-permute-done.18
  130.6 8.1 %mixer_fwd.5 = (bf16[256,1024]{1,0:T(8,128)(2,1)S(1)}, f32[2048,256]{1,0:T(8,128)S(1)}, f32[256,1024]{1,0:T(8,128)S(1)}, f32[256,1024]{1,0:T(8,128)S(1)}) custom-call(f32[256,1024]{1,0:T(8,128)S(1)} %convolution_add_fusion.5.refs_0_.refs_1_, ...), custom_call_target="tpu_custom_call", output_to_operand_aliasing={{0}: (9, {}), {1}: (10, {}), {2}: (11, {}), {3}: (12, {})} | custom-call | flops 10000000000 | bytes 10000000 | tf_op jit(solution)/shard_map/mixer_fwd/pallas_call | solution.py:277
  139.0 7.6 %mixer_fwd.6 = (bf16[256,1024]{1,0:T(8,128)(2,1)S(1)}, f32[2048,256]{1,0:T(8,128)S(1)}, f32[256,1024]{1,0:T(8,128)S(1)}, f32[256,1024]{1,0:T(8,128)S(1)}) custom-call(f32[256,1024]{1,0:T(8,128)S(1)} %convolution_add_fusion.5.refs_0_.refs_1_, ...), custom_call_target="tpu_custom_call", output_to_operand_aliasing={{0}: (9, {}), {1}: (10, {}), {2}: (11, {}), {3}: (12, {})} | custom-call | flops 10000000000 | bytes 10000000 | tf_op jit(solution)/shard_map/mixer_fwd/pallas_call | solution.py:277
  146.7 7.6 %mixer_fwd.7 = (bf16[256,1024]{1,0:T(8,128)(2,1)S(1)}, f32[2048,256]{1,0:T(8,128)S(1)}, f32[256,1024]{1,0:T(8,128)S(1)}, f32[256,1024]{1,0:T(8,128)S(1)}) custom-call(f32[256,1024]{1,0:T(8,128)S(1)} %convolution_add_fusion.5.refs_0_.refs_1_, ...), custom_call_target="tpu_custom_call", output_to_operand_aliasing={{0}: (9, {}), {1}: (10, {}), {2}: (11, {}), {3}: (12, {})} | custom-call | flops 10000000000 | bytes 10000000 | tf_op jit(solution)/shard_map/mixer_fwd/pallas_call | solution.py:277
  154.3 19.6 %collective-permute-done.20 = bf16[2,2,2,128,1024]{4,3,0,1,2:T(8,128)(2,1)} collective-permute-done((bf16[2,2,2,128,1024]{4,3,0,1,2:T(8,128)(2,1)S(1)}, bf16[2,2,2,128,1024]{4,3,0,1,2:T(8,128)(2,1)}, u32[]{:S(2)}, u32[]{:S(2)}) %collective-permute-start.20) | collective-permute-done | bytes 2097184 | tf_op jit(solution)/shard_map/ppermute | solution.py:511
  173.9 12.8 %collective-permute-done.19 = bf16[2,2,2,64,2560]{4,3,2,1,0:T(8,128)(2,1)S(1)} collective-permute-done((bf16[2,2,2,64,2560]{4,3,2,1,0:T(8,128)(2,1)S(1)}, bf16[2,2,2,64,2560]{4,3,2,1,0:T(8,128)(2,1)S(1)}, u32[]{:S(2)}, u32[]{:S(2)}) %collective-permute-start.19) | collective-permute-done | bytes 2621472 | tf_op jit(solution)/shard_map/ppermute | solution.py:511
  204.9 6.2 %ffn_half.2 = (bf16[256,2048]{1,0:T(8,128)(2,1)S(1)}, bf16[256,2048]{1,0:T(8,128)(2,1)S(1)}, f32[256,1024]{1,0:T(8,128)S(1)}) custom-call(bf16[256,1024]{1,0:T(8,128)(2,1)S(1)} %add_convert_fusion.1.xc, bf16[1024,256]{1,0:T(8,128)(2,1)S(1)} %copy-done.16, bf16[256,1024]{1,0:T(8,128)(2,1)S(1)} %fusion.22.gf, bf16[1024,2560]{1,0:T(8,128)(2,1)} %bitcast.91.wk, ...), custom_call_target="tpu_custom_call" | custom-call | flops 5000000000 | bytes 10000000 | tf_op jit(solution)/shard_map/ffn_half/pallas_call | solution.py:363
  212.4 10.5 %ffn_half.3 = (bf16[256,2048]{1,0:T(8,128)(2,1)S(1)}, bf16[256,2048]{1,0:T(8,128)(2,1)}, f32[256,1024]{1,0:T(8,128)S(1)}, bf16[2048,1024]{1,0:T(8,128)(2,1)}, bf16[1024,2048]{1,0:T(8,128)(2,1)}) custom-call(bf16[256,1024]{1,0:T(8,128)(2,1)S(1)} %add_convert_fusion.1.xc, bf16[1024,256]{1,0:T(8,128)(2,1)S(1)} %copy-done.16, bf16[256,1024]{1,0:T(8,128)(2,1)S(1)} %fusion.22.gf, ...), custom_call_target="tpu_custom_call" | custom-call | flops 5000000000 | bytes 10000000 | tf_op jit(solution)/shard_map/ffn_half/pallas_call | solution.py:363
  238.0 5.7 %ffn_grads.1 = (bf16[2048,1024]{1,0:T(8,128)(2,1)S(1)}, bf16[1024,2560]{1,0:T(8,128)(2,1)S(1)}) custom-call(bf16[1024,256]{1,0:T(8,128)(2,1)S(1)} %copy-done.17, bf16[256,1024]{1,0:T(8,128)(2,1)S(1)} %fusion.22.gf, bf16[256,2048]{1,0:T(8,128)(2,1)S(1)} %copy-done.21, bf16[256,2048]{1,0:T(8,128)(2,1)S(1)} %copy-done.26, ...), custom_call_target="tpu_custom_call" | custom-call | flops 5000000000 | bytes 10000000 | tf_op jit(solution)/shard_map/ffn_grads/pallas_call | solution.py:385
  255.0 9.3 %mixer_bwd.4 = (bf16[256,1024]{1,0:T(8,128)(2,1)S(1)}, bf16[256,1024]{1,0:T(8,128)(2,1)S(1)}, bf16[256,1024]{1,0:T(8,128)(2,1)S(1)}, bf16[256,1024]{1,0:T(8,128)...) custom-call(s32[1]{0:T(128)} %bitcast.97.refs_0_, ...), custom_call_target="tpu_custom_call" | custom-call | flops 10000000000 | bytes 10000000 | tf_op jit(solution)/shard_map/mixer_bwd/pallas_call | solution.py:308
  264.3 8.2 %collective-permute-done.27 = bf16[2,2,2,64,1024]{4,3,0,1,2:T(8,128)(2,1)S(1)} collective-permute-done((bf16[2,2,2,64,1024]{4,3,0,1,2:T(8,128)(2,1)S(1)}, bf16[2,2,2,64,1024]{4,3,0,1,2:T(8,128)(2,1)S(1)}, u32[]{:S(2)}, u32[]{:S(2)}) %collective-permute-start.27) | collective-permute-done | bytes 1048608 | tf_op jit(solution)/shard_map/ppermute | solution.py:511
  273.7 9.7 %mixer_bwd.5 = (bf16[256,1024]{1,0:T(8,128)(2,1)S(1)}, bf16[256,1024]{1,0:T(8,128)(2,1)S(1)}, bf16[256,1024]{1,0:T(8,128)(2,1)S(1)}, bf16[256,1024]{1,0:T(8,128)...) custom-call(s32[1]{0:T(128)} %bitcast.97.refs_0_, ...), custom_call_target="tpu_custom_call", output_to_operand_aliasing={{0}: (14, {}), {1}: (15, {}), {2}: (16, {}), {3}: (17, {}),... | custom-call | flops 10000000000 | bytes 10000000 | tf_op jit(solution)/shard_map/mixer_bwd/pallas_call | solution.py:308
  291.4 9.5 %mixer_bwd.6 = (bf16[256,1024]{1,0:T(8,128)(2,1)S(1)}, bf16[256,1024]{1,0:T(8,128)(2,1)S(1)}, bf16[256,1024]{1,0:T(8,128)(2,1)S(1)}, bf16[256,1024]{1,0:T(8,128)...) custom-call(s32[1]{0:T(128)} %bitcast.97.refs_0_, ...), custom_call_target="tpu_custom_call", output_to_operand_aliasing={{0}: (14, {}), {1}: (15, {}), {2}: (16, {}), {3}: (17, {}),... | custom-call | flops 10000000000 | bytes 10000000 | tf_op jit(solution)/shard_map/mixer_bwd/pallas_call | solution.py:308
  304.0 7.5 %collective-permute-done.30 = bf16[2,2,64,1024]{3,2,0,1:T(8,128)(2,1)} collective-permute-done((bf16[2,2,64,1024]{3,2,0,1:T(8,128)(2,1)}, bf16[2,2,64,1024]{3,2,0,1:T(8,128)(2,1)}, u32[]{:S(2)}, u32[]{:S(2)}) %collective-permute-start.30) | collective-permute-done | bytes 524320 | tf_op jit(solution)/shard_map/ppermute | solution.py:511
  322.7 9.5 %mixer_bwd.7 = (bf16[256,1024]{1,0:T(8,128)(2,1)S(1)}, bf16[256,1024]{1,0:T(8,128)(2,1)S(1)}, bf16[256,1024]{1,0:T(8,128)(2,1)S(1)}, bf16[256,1024]{1,0:T(8,128)...) custom-call(s32[1]{0:T(128)} %bitcast.97.refs_0_, ...), custom_call_target="tpu_custom_call", output_to_operand_aliasing={{0}: (14, {}), {1}: (15, {}), {2}: (16, {}), {3}: (17, {}),... | custom-call | flops 10000000000 | bytes 10000000 | tf_op jit(solution)/shard_map/mixer_bwd/pallas_call | solution.py:308
  400.5 5.4 %collective-permute-start.50 = (bf16[2,32,1536]{2,1,0:T(8,128)(2,1)S(1)}, bf16[2,32,1536]{2,1,0:T(8,128)(2,1)S(1)}, u32[]{:S(2)}, u32[]{:S(2)}) collective-permute-start(bf16[2,32,1536]{2,1,0:T(8,128)(2,1)S(1)} %dynamic-slice_bitcast_fusion.14), channel_id=1, source_target_pairs={{0,16},{1,17},{2,18},{3,19},{4,20},{5,21},{6,22},{7,23},{8,24},{9,... | collective-permute-start | bytes 589832 | tf_op jit(solution)/shard_map/ppermute | solution.py:511
  426.4 5.0 %collective-permute-done.59 = bf16[64,288]{1,0:T(8,128)(2,1)S(1)} collective-permute-done((bf16[64,288]{1,0:T(8,128)(2,1)S(1)}, bf16[64,288]{1,0:T(8,128)(2,1)S(1)}, u32[]{:S(2)}, u32[]{:S(2)}) %collective-permute-start.59) | collective-permute-done | bytes 36896 | tf_op jit(solution)/shard_map/ppermute | solution.py:511
  443.4 5.3 %collective-permute-done.58 = f32[24,1024]{1,0:T(8,128)S(1)} collective-permute-done((f32[24,1024]{1,0:T(8,128)S(1)}, f32[24,1024]{1,0:T(8,128)S(1)}, u32[]{:S(2)}, u32[]{:S(2)}) %collective-permute-start.58) | collective-permute-done | bytes 98336 | tf_op jit(solution)/shard_map/ppermute | solution.py:511
  (648 shorter events, 242.3 us)
Async XLA Ops:
  33.6 19.2 %collective-permute-start.7 = (bf16[2,2,64,1024]{3,2,1,0:T(8,128)(2,1)S(1)}, bf16[2,2,64,1024]{3,2,1,0:T(8,128)(2,1)S(1)}, u32[]{:S(2)}, u32[]{:S(2)}) collective-permute-start(bf16[2,2,64,1024]{3,2,1,0:T(8,128)(2,1)S(1)} %maximum_select_fusion.20), channel_id=1, source_target_pairs={{0,2},{1,3},{2,0},{3,1},{4,6},{5,7},{6,4},{7,5},{8,10},{9,11},{10,... | collective-permute-start | bytes 1572872 | tf_op jit(solution)/shard_map/ppermute | solution.py:511
  54.3 22.2 %collective-permute-start.11 = (bf16[2,2,2,64,896]{4,3,1,0,2:T(8,128)(2,1)S(1)}, bf16[2,2,2,64,896]{4,3,1,0,2:T(8,128)(2,1)S(1)}, u32[]{:S(2)}, u32[]{:S(2)}) collective-permute-start(bf16[2,2,2,64,896]{4,3,1,0,2:T(8,128)(2,1)S(1)} %maximum_select_fusion.17), channel_id=1, source_target_pairs={{0,2},{1,3},{2,0},{3,1},{4,6},{5,7},{6,4},{7,5},{8,10},{9,11},{10,... | collective-permute-start | bytes 2752520 | tf_op jit(solution)/shard_map/ppermute | solution.py:511
  55.0 23.9 %collective-permute-start.10 = (bf16[2,2,2,64,1024]{4,3,2,1,0:T(8,128)(2,1)S(1)}, bf16[2,2,2,64,1024]{4,3,2,1,0:T(8,128)(2,1)}, u32[]{:S(2)}, u32[]{:S(2)}) collective-permute-start(bf16[2,2,2,64,1024]{4,3,2,1,0:T(8,128)(2,1)S(1)} %maximum_select_fusion.11), channel_id=1, source_target_pairs={{0,4},{1,5},{2,6},{3,7},{4,0},{5,1},{6,2},{7,3},{8,12},{9,13},{10,... | collective-permute-start | bytes 3145736 | tf_op jit(solution)/shard_map/ppermute | solution.py:511
  55.7 20.8 %collective-permute-start.12 = (bf16[2,64,2560]{2,1,0:T(8,128)(2,1)S(1)}, bf16[2,64,2560]{2,1,0:T(8,128)(2,1)S(1)}, u32[]{:S(2)}, u32[]{:S(2)}) collective-permute-start(bf16[2,64,2560]{2,1,0:T(8,128)(2,1)S(1)} %maximum_select_fusion.18), channel_id=1, source_target_pairs={{0,8},{1,9},{2,10},{3,11},{4,12},{5,13},{6,14},{7,15},{8,0},{9,1},... | collective-permute-start | bytes 1966088 | tf_op jit(solution)/shard_map/ppermute | solution.py:511
  56.5 19.2 %collective-permute-start.13 = (bf16[128,1024]{1,0:T(8,128)(2,1)S(1)}, bf16[128,1024]{1,0:T(8,128)(2,1)S(1)}, u32[]{:S(2)}, u32[]{:S(2)}) collective-permute-start(bf16[128,1024]{1,0:T(8,128)(2,1)S(1)} %copy-done.95), channel_id=1, source_target_pairs={{0,16},{1,17},{2,18},{3,19},{4,20},{5,21},{6,22},{7,23},{8,24},{9,... | collective-permute-start | bytes 786440 | tf_op jit(solution)/shard_map/ppermute | solution.py:511
  91.6 31.0 %collective-permute-start.17 = (bf16[2,2,64,2560]{3,2,1,0:T(8,128)(2,1)S(1)}, bf16[2,2,64,2560]{3,2,1,0:T(8,128)(2,1)S(1)}, u32[]{:S(2)}, u32[]{:S(2)}) collective-permute-start(bf16[2,2,64,2560]{3,2,1,0:T(8,128)(2,1)S(1)} %copy-done.43), channel_id=1, source_target_pairs={{0,2},{1,3},{2,0},{3,1},{4,6},{5,7},{6,4},{7,5},{8,10},{9,11},{10,... | collective-permute-start | bytes 3932168 | tf_op jit(solution)/shard_map/ppermute | solution.py:511
  102.1 24.9 %collective-permute-start.18 = (bf16[2,2,128,1024]{3,2,0,1:T(8,128)(2,1)S(1)}, bf16[2,2,128,1024]{3,2,0,1:T(8,128)(2,1)S(1)}, u32[]{:S(2)}, u32[]{:S(2)}) collective-permute-start(bf16[2,2,128,1024]{3,2,0,1:T(8,128)(2,1)S(1)} %maximum_select_fusion.12), channel_id=1, source_target_pairs={{0,4},{1,5},{2,6},{3,7},{4,0},{5,1},{6,2},{7,3},{8,12},{9,13},{10,... | collective-permute-start | bytes 3145736 | tf_op jit(solution)/shard_map/ppermute | solution.py:511
  127.3 46.6 %collective-permute-start.20 = (bf16[2,2,2,128,1024]{4,3,0,1,2:T(8,128)(2,1)S(1)}, bf16[2,2,2,128,1024]{4,3,0,1,2:T(8,128)(2,1)}, u32[]{:S(2)}, u32[]{:S(2)}) collective-permute-start(bf16[2,2,2,128,1024]{4,3,0,1,2:T(8,128)(2,1)S(1)} %maximum_select_fusion.4), channel_id=1, source_target_pairs={{0,2},{1,3},{2,0},{3,1},{4,6},{5,7},{6,4},{7,5},{8,10},{9,11},{10,... | collective-permute-start | bytes 6291464 | tf_op jit(solution)/shard_map/ppermute | solution.py:511
  129.3 57.4 %collective-permute-start.19 = (bf16[2,2,2,64,2560]{4,3,2,1,0:T(8,128)(2,1)S(1)}, bf16[2,2,2,64,2560]{4,3,2,1,0:T(8,128)(2,1)S(1)}, u32[]{:S(2)}, u32[]{:S(2)}) collective-permute-start(bf16[2,2,2,64,2560]{4,3,2,1,0:T(8,128)(2,1)S(1)} %maximum_select_fusion.2), channel_id=1, source_target_pairs={{0,4},{1,5},{2,6},{3,7},{4,0},{5,1},{6,2},{7,3},{8,12},{9,13},{10,... | collective-permute-start | bytes 7864328 | tf_op jit(solution)/shard_map/ppermute | solution.py:511
  246.5 26.1 %collective-permute-start.27 = (bf16[2,2,2,64,1024]{4,3,0,1,2:T(8,128)(2,1)S(1)}, bf16[2,2,2,64,1024]{4,3,0,1,2:T(8,128)(2,1)S(1)}, u32[]{:S(2)}, u32[]{:S(2)}) collective-permute-start(bf16[2,2,2,64,1024]{4,3,0,1,2:T(8,128)(2,1)S(1)} %dynamic-slice_bitcast_fusion.3), channel_id=1, source_target_pairs={{0,4},{1,5},{2,6},{3,7},{4,0},{5,1},{6,2},{7,3},{8,12},{9,13},{10,... | collective-permute-start | bytes 3145736 | tf_op jit(solution)/shard_map/ppermute | solution.py:511
  247.5 26.2 %collective-permute-start.28 = (bf16[2,2,2,64,1024]{4,3,0,1,2:T(8,128)(2,1)S(1)}, bf16[2,2,2,64,1024]{4,3,0,1,2:T(8,128)(2,1)}, u32[]{:S(2)}, u32[]{:S(2)}) collective-permute-start(bf16[2,2,2,64,1024]{4,3,0,1,2:T(8,128)(2,1)S(1)} %dynamic-slice_bitcast_fusion.2), channel_id=1, source_target_pairs={{0,2},{1,3},{2,0},{3,1},{4,6},{5,7},{6,4},{7,5},{8,10},{9,11},{10,... | collective-permute-start | bytes 3145736 | tf_op jit(solution)/shard_map/ppermute | solution.py:511
  251.1 52.8 %collective-permute-start.31 = (bf16[2,2,2,32,2560]{4,3,0,1,2:T(8,128)(2,1)}, bf16[2,2,2,32,2560]{4,3,0,1,2:T(8,128)(2,1)}, u32[]{:S(2)}, u32[]{:S(2)}) collective-permute-start(bf16[2,2,2,32,2560]{4,3,0,1,2:T(8,128)(2,1)} %dynamic-slice_bitcast_fusion.1), channel_id=1, source_target_pairs={{0,4},{1,5},{2,6},{3,7},{4,0},{5,1},{6,2},{7,3},{8,12},{9,13},{10,... | collective-permute-start | bytes 3932168 | tf_op jit(solution)/shard_map/ppermute | solution.py:511
  252.4 51.6 %collective-permute-start.32 = (bf16[2,2,2,32,2560]{4,3,2,1,0:T(8,128)(2,1)}, bf16[2,2,2,32,2560]{4,3,2,1,0:T(8,128)(2,1)}, u32[]{:S(2)}, u32[]{:S(2)}) collective-permute-start(bf16[2,2,2,32,2560]{4,3,2,1,0:T(8,128)(2,1)} %dynamic-slice_bitcast_fusion), channel_id=1, source_target_pairs={{0,2},{1,3},{2,0},{3,1},{4,6},{5,7},{6,4},{7,5},{8,10},{9,11},{10,... | collective-permute-start | bytes 3932168 | tf_op jit(solution)/shard_map/ppermute | solution.py:511
  288.4 23.0 %collective-permute-start.30 = (bf16[2,2,64,1024]{3,2,0,1:T(8,128)(2,1)}, bf16[2,2,64,1024]{3,2,0,1:T(8,128)(2,1)}, u32[]{:S(2)}, u32[]{:S(2)}) collective-permute-start(bf16[2,2,64,1024]{3,2,0,1:T(8,128)(2,1)} %dynamic-slice_bitcast_fusion.6), channel_id=1, source_target_pairs={{0,4},{1,5},{2,6},{3,7},{4,0},{5,1},{6,2},{7,3},{8,12},{9,13},{10,... | collective-permute-start | bytes 1572872 | tf_op jit(solution)/shard_map/ppermute | solution.py:511
  290.1 21.9 %collective-permute-start.29 = (bf16[2,2,64,1024]{3,2,0,1:T(8,128)(2,1)S(1)}, bf16[2,2,64,1024]{3,2,0,1:T(8,128)(2,1)S(1)}, u32[]{:S(2)}, u32[]{:S(2)}) collective-permute-start(bf16[2,2,64,1024]{3,2,0,1:T(8,128)(2,1)S(1)} %dynamic-slice_bitcast_fusion.7), channel_id=1, source_target_pairs={{0,2},{1,3},{2,0},{3,1},{4,6},{5,7},{6,4},{7,5},{8,10},{9,11},{10,... | collective-permute-start | bytes 1572872 | tf_op jit(solution)/shard_map/ppermute | solution.py:511
  314.5 17.7 %collective-permute-start.37 = (bf16[2,2,32,2560]{3,2,1,0:T(8,128)(2,1)S(1)}, bf16[2,2,32,2560]{3,2,1,0:T(8,128)(2,1)S(1)}, u32[]{:S(2)}, u32[]{:S(2)}) collective-permute-start(bf16[2,2,32,2560]{3,2,1,0:T(8,128)(2,1)S(1)} %dynamic-slice_bitcast_fusion.4), channel_id=1, source_target_pairs={{0,4},{1,5},{2,6},{3,7},{4,0},{5,1},{6,2},{7,3},{8,12},{9,13},{10,... | collective-permute-start | bytes 1966088 | tf_op jit(solution)/shard_map/ppermute | solution.py:511
  321.8 42.8 %collective-permute-start.38 = (bf16[512,1536]{1,0:T(8,128)(2,1)}, bf16[512,1536]{1,0:T(8,128)(2,1)}, u32[]{:S(2)}, u32[]{:S(2)}) collective-permute-start(bf16[512,1536]{1,0:T(8,128)(2,1)} %fusion), channel_id=1, source_target_pairs={{0,4},{1,5},{2,6},{3,7},{4,0},{5,1},{6,2},{7,3},{8,12},{9,13},{10,... | collective-permute-start | bytes 4718600 | tf_op jit(solution)/shard_map/ppermute | solution.py:511
  336.8 19.5 %collective-permute-start.44 = (bf16[1024,288]{0,1:T(8,128)(2,1)S(1)}, bf16[1024,288]{0,1:T(8,128)(2,1)S(1)}, u32[]{:S(2)}, u32[]{:S(2)}) collective-permute-start(bf16[1024,288]{0,1:T(8,128)(2,1)S(1)} %select_convert_fusion), channel_id=1, source_target_pairs={{0,1},{1,0},{2,3},{3,2},{4,5},{5,4},{6,7},{7,6},{8,9},{9,8},{10,11... | collective-permute-start | bytes 1769480 | tf_op jit(solution)/shard_map/ppermute | solution.py:511
  337.9 35.8 %collective-permute-start.43 = (bf16[2,32,2560]{2,1,0:T(8,128)(2,1)}, bf16[2,32,2560]{2,1,0:T(8,128)(2,1)}, u32[]{:S(2)}, u32[]{:S(2)}) collective-permute-start(bf16[2,32,2560]{2,1,0:T(8,128)(2,1)} %dynamic-slice_bitcast_fusion.10), channel_id=1, source_target_pairs={{0,8},{1,9},{2,10},{3,11},{4,12},{5,13},{6,14},{7,15},{8,0},{9,1},... | collective-permute-start | bytes 983048 | tf_op jit(solution)/shard_map/ppermute | solution.py:511
  340.6 33.2 %collective-permute-start.42 = (bf16[2,32,2560]{2,1,0:T(8,128)(2,1)}, bf16[2,32,2560]{2,1,0:T(8,128)(2,1)}, u32[]{:S(2)}, u32[]{:S(2)}) collective-permute-start(bf16[2,32,2560]{2,1,0:T(8,128)(2,1)} %dynamic-slice_bitcast_fusion.11), channel_id=1, source_target_pairs={{0,8},{1,9},{2,10},{3,11},{4,12},{5,13},{6,14},{7,15},{8,0},{9,1},... | collective-permute-start | bytes 983048 | tf_op jit(solution)/shard_map/ppermute | solution.py:511
  342.9 24.9 %collective-permute-start.39 = (bf16[512,1536]{1,0:T(8,128)(2,1)}, bf16[512,1536]{1,0:T(8,128)(2,1)}, u32[]{:S(2)}, u32[]{:S(2)}) collective-permute-start(bf16[512,1536]{1,0:T(8,128)(2,1)} %proj_grad.2), channel_id=1, source_target_pairs={{0,1},{1,0},{2,3},{3,2},{4,5},{5,4},{6,7},{7,6},{8,9},{9,8},{10,11... | collective-permute-start | bytes 4718600 | tf_op jit(solution)/shard_map/ppermute | solution.py:511
  378.9 35.4 %collective-permute-start.53 = (bf16[32,2560]{1,0:T(8,128)(2,1)}, bf16[32,2560]{1,0:T(8,128)(2,1)}, u32[]{:S(2)}, u32[]{:S(2)}) collective-permute-start(bf16[32,2560]{1,0:T(8,128)(2,1)} %dynamic-slice_bitcast_fusion.17), channel_id=1, source_target_pairs={{0,16},{1,17},{2,18},{3,19},{4,20},{5,21},{6,22},{7,23},{8,24},{9,... | collective-permute-start | bytes 491528 | tf_op jit(solution)/shard_map/ppermute | solution.py:511
  381.7 33.2 %collective-permute-start.52 = (bf16[32,2560]{1,0:T(8,128)(2,1)}, bf16[32,2560]{1,0:T(8,128)(2,1)}, u32[]{:S(2)}, u32[]{:S(2)}) collective-permute-start(bf16[32,2560]{1,0:T(8,128)(2,1)} %dynamic-slice_bitcast_fusion.18), channel_id=1, source_target_pairs={{0,16},{1,17},{2,18},{3,19},{4,20},{5,21},{6,22},{7,23},{8,24},{9,... | collective-permute-start | bytes 491528 | tf_op jit(solution)/shard_map/ppermute | solution.py:511
  414.3 18.1 %collective-permute-start.55 = (f32[24,1024]{1,0:T(8,128)S(1)}, f32[24,1024]{1,0:T(8,128)S(1)}, u32[]{:S(2)}, u32[]{:S(2)}) collective-permute-start(f32[24,1024]{1,0:T(8,128)S(1)} %add.509), channel_id=1, source_target_pairs={{0,2},{1,3},{2,0},{3,1},{4,6},{5,7},{6,4},{7,5},{8,10},{9,11},{10,... | collective-permute-start | bytes 294920 | tf_op jit(solution)/shard_map/ppermute | solution.py:511
  (170 other events, 1481.3 us)
